TPU v7x, 256 devices: a whole 4x4x8 slice. The times are simulated.
256 devices in a mesh: pairs: 32 (over x, y, core), coef: 8 (over z).
Axes of the slice: x: 4, y: 4, z: 8, core: 2. Of those that a mesh axis runs over, the one named last changes fastest.
Arguments:
- integrals: bfloat16 [4096, 64, 64, 64], P('pairs', 'coef'), may hold values from -6 to 6
- block_shells: int32 [32, 64, 2], P('pairs', 'coef'), may hold values from 0 to 143
- live_counts: int32 [32, 8], P('pairs', 'coef'), may hold values from 1 to 8, as said below
- significance: int32 [144, 144], replicated, may hold values 0 or 1
- occ_coef: bfloat16 [9216, 64], P('coef'), may hold values from -0.375 to 0.375
- lam_coef: bfloat16 [64, 128], P('coef'), may hold values from -0.75 to 0.75
- sig_coef: bfloat16 [64, 128], P('coef'), may hold values from -0.75 to 0.75
Outputs:
- mo_integrals: float32 [4096, 128, 128], P(('pairs', 'coef'))
Inputs may be any that keep to these rules, and one draw needn't show every extreme that they name: `live_counts`: each device's live slots are its first ones; some device has all 8 live.
All inputs are finite; a program needn't handle non-finite values.
Results may differ from a plain program's by a relative error of at most 0.0029.
Values may be sent and summed in bfloat16 or wider, within the bound.
No kernel may reach another device: no remote copies, remote signals or barrier semaphores. Data moves between devices by JAX's collectives and lax.ppermute only.
A program may use at most 64 MiB of HBM per device.

v0:
```python
import jax
import jax.numpy as jnp
from jax import lax
from jax.sharding import PartitionSpec as P


def on_device(integrals, block_shells, live_counts, significance, occ_coef, lam_coef, sig_coef):
    occupied, lam_panel, sig_panel = (
        lax.all_gather(occ_coef, "coef", axis=0, tiled=True),
        lax.all_gather(lam_coef, "coef", axis=0, tiled=True),
        lax.all_gather(sig_coef, "coef", axis=0, tiled=True),
    )
    shell_size = integrals.shape[2]
    slot_count = integrals.shape[1]
    local_pairs = integrals.shape[0]
    occ_count = occupied.shape[1]
    shell_table = occupied.reshape(-1, shell_size, occ_count)
    pair_shells = block_shells[0]
    row_shells = shell_table[pair_shells[:, 0]]
    col_shells = shell_table[pair_shells[:, 1]]
    screened = significance[pair_shells[:, 0], pair_shells[:, 1]]
    live_total = live_counts[0, 0]
    is_live = (jnp.arange(slot_count) < live_total) & (screened == 1)
    col_weighted = col_shells * is_live.astype(jnp.bfloat16)[:, None, None]
    quarter = jnp.einsum(
        "smi,lsmn->lsin", row_shells, integrals, preferred_element_type=jnp.float32
    ).astype(jnp.bfloat16)
    partial_sums = jnp.einsum(
        "lsin,snj->ijl", quarter, col_weighted, preferred_element_type=jnp.float32
    )
    flat_sums = partial_sums.reshape(occ_count * occ_count, local_pairs)
    moved = lax.all_to_all(flat_sums, "pairs", split_axis=0, concat_axis=1, tiled=True)
    owned = lax.psum_scatter(moved, "coef", scatter_dimension=0, tiled=True)
    lam_width = lam_panel.shape[0]
    sig_width = sig_panel.shape[0]
    owned_grid = owned.reshape(owned.shape[0], lam_width, sig_width)
    partly = jnp.einsum(
        "xa,qxy->qay", lam_panel.astype(jnp.float32), owned_grid, precision=lax.Precision.HIGHEST
    )
    return jnp.einsum(
        "qay,yb->qab", partly, sig_panel.astype(jnp.float32), precision=lax.Precision.HIGHEST
    )


def solution(mesh):
    placed = (
        P("pairs", "coef", None, None),
        P("pairs", "coef", None),
        P("pairs", "coef"),
        P(),
        P("coef", None),
        P("coef", None),
        P("coef", None),
    )
    return jax.shard_map(
        on_device,
        mesh=mesh,
        in_specs=placed,
        out_specs=P(("pairs", "coef"), None, None),
        check_vma=False,
    )
```

profile of v0, /device:TPU:32, one launch (start us, length us, event | category | flops | bytes accessed | tf_op | source)
XLA Modules:
  0.0 163.2 jit_solution(3676585388277604607)
XLA Ops:
  6.5 0.0 copy-start
  6.5 0.0 all-gather.2.cloned.1.call-start
  6.5 0.7 all-gather.2.cloned.1.call-update
  7.3 0.0 reduce-scatter.4.cloned.1.call-start
  8.0 0.8 or_bitcast_fusion
  8.7 0.0 copy-done
  8.7 0.6 gather_fusion.1
  9.4 40.9 %all-gather.2.cloned.1.call-done = bf16[9216,64]{0,1:T(8,128)(2,1)} async-done(((bf16[1152,64]{0,1:T(8,128)(2,1)}), bf16[9216,64]{0,1:T(8,128)(2,1)}) %all-gather.2.cloned.1.call-update) | async-done | bytes 1179664 | tf_op jit(solution)/shard_map/all_gather | solution.py:9
  50.3 2.8 %copy.28 = bf16[9216,64]{1,0:T(8,128)(2,1)S(1)} copy(bf16[9216,64]{0,1:T(8,128)(2,1)} %all-gather.2.cloned.1.call-done) | data formatting | bytes 2359296 | tf_op jit(solution)/shard_map/reshape | solution.py:17
  53.1 0.6 gather_fusion.2
  53.7 0.6 gather_fusion
  54.2 10.4 %convert_bitcast_fusion = bf16[128,8,64,64]{0,2,3,1:T(8,128)(2,1)S(1)} fusion(bf16[128,8,64,64]{0,3,2,1:T(8,128)(2,1)} %param.7, bf16[8,64,64]{2,1,0:T(8,128)(2,1)S(1)} %gather_fusion.2), kind=kOutput, calls=%fused_computation.7 | convolution fusion | flops 541065216 | bytes 16842752 | tf_op jit(solution)/shard_map/smi,lsmn->lsin/dot_general | solution.py:25
  64.6 4.9 %fusion = f32[64,128,64,1]{1,0,3,2:T(8,128)S(1)} fusion(bf16[128,8,64,64]{0,2,3,1:T(8,128)(2,1)S(1)} %convert_bitcast_fusion, bf16[8,64,64]{2,1,0:T(8,128)(2,1)S(1)} %gather_fusion, bf16[8]{0:T(256)(128)(2,1)S(1)} %and_convert_fusion), kind=kOutput, calls=%fused_computation.3 | convolution fusion | flops 537001984 | bytes 10551312 | tf_op jit(solution)/shard_map/lsin,snj->ijl/dot_general | solution.py:28
  69.6 0.0 copy-start.1
  69.6 0.0 copy-start.2
  69.6 1.9 %copy.18 = f32[32,128,128]{1,2,0:T(8,128)} copy(f32[32,128,128]{2,1,0:T(8,128)S(1)} %bitcast.41) | data formatting | bytes 4194304 | tf_op jit(solution)/shard_map/all_to_all | solution.py:32
  71.5 35.1 %all_to_all.19 = f32[32,128,128]{1,2,0:T(8,128)S(1)} all-to-all(f32[32,128,128]{1,2,0:T(8,128)} %copy.18), channel_id=1, replica_groups=mesh['pairs'=32,'coef'=8] {'pairs'}, dimensions={0} | all-to-all | bytes 4194304 | tf_op jit(solution)/shard_map/all_to_all | solution.py:32
  106.6 1.9 %copy.26 = f32[128,4096]{1,0:T(8,128)} copy(f32[128,4096]{0,1:T(8,128)S(1)} %bitcast.43) | data formatting | bytes 4194304
  108.5 0.0 reduce-scatter.4.cloned.1.call-update
  108.5 0.0 copy-done.1
  108.5 21.7 %all_gather.10 = bf16[64,128]{1,0:T(8,128)(2,1)S(1)} all-gather(bf16[8,128]{1,0:T(8,128)(2,1)S(1)} %copy-done.1), channel_id=1, replica_groups=mesh['pairs'=32,'coef'=8] {'coef'}, dimensions={0}, use_global_device_ids=true | all-gather | bytes 18432 | tf_op jit(solution)/shard_map/all_gather | solution.py:10
  130.2 0.0 copy-done.2
  130.2 20.9 %all_gather.11 = bf16[64,128]{1,0:T(8,128)(2,1)S(1)} all-gather(bf16[8,128]{1,0:T(8,128)(2,1)S(1)} %copy-done.2), channel_id=1, replica_groups=mesh['pairs'=32,'coef'=8] {'coef'}, dimensions={0}, use_global_device_ids=true | all-gather | bytes 18432 | tf_op jit(solution)/shard_map/all_gather | solution.py:11
  151.1 0.0 reduce-scatter.4.cloned.1.call-done
  151.1 1.5 copy.27
  152.7 1.3 copy.19
  154.0 0.4 convolution_bitcast_fusion
  154.4 2.0 %fusion.10 = f32[16,128,128]{2,1,0:T(8,128)} fusion(f32[16,128,64]{1,2,0:T(8,128)S(1)} %convolution_bitcast_fusion, bf16[64,128]{1,0:T(8,128)(2,1)S(1)} %all_gather.11), kind=kOutput, calls=%fused_computation.13 | convolution fusion | flops 201326592 | bytes 1589248 | tf_op jit(solution)/shard_map/qay,yb->qab/dot_general | solution.py:40
  (2 shorter events, 0.0 us)
Async XLA Ops:
  6.5 2.2 %copy-start = (s32[144,144]{1,0:T(8,128)S(1)}, s32[144,144]{1,0:T(8,128)}, u32[]{:S(2)}) copy-start(s32[144,144]{1,0:T(8,128)} %param.10) | copy-start | bytes 248836
  6.5 43.8 %all-gather.2.cloned.1.call-start = ((), (), s32[]{:S(2)}) async-start(), calls=%async_computation.2 | async-start | bytes 1327104 | tf_op jit(solution)/shard_map/all_gather | solution.py:9
  7.3 143.9 %reduce-scatter.4.cloned.1.call-start = ((), (), s32[]{:S(2)}) async-start(), calls=%async_computation.3 | async-start | bytes 2359296
  69.6 38.9 %copy-start.1 = (bf16[8,128]{1,0:T(8,128)(2,1)S(1)}, bf16[8,128]{1,0:T(8,128)(2,1)}, u32[]{:S(2)}) copy-start(bf16[8,128]{1,0:T(8,128)(2,1)} %param.12) | copy-start | bytes 6148
  69.6 60.6 %copy-start.2 = (bf16[8,128]{1,0:T(8,128)(2,1)S(1)}, bf16[8,128]{1,0:T(8,128)(2,1)}, u32[]{:S(2)}) copy-start(bf16[8,128]{1,0:T(8,128)(2,1)} %param.13) | copy-start | bytes 6148
Sparse Core Ops, SparseCore 0:
  9.2 41.1 all-gather.1
  108.6 37.0 reduce-scatter.3
where the time goes:
time: 164 us; the launch traced here: 163 us
  blocking collectives  77.8 us (47%)
  waiting for transfers between devices  41.7 us (25%)
  matrix products  17.7 us (11%)
  between operations  14.1 us (9%)
  local copies, waits for them, and re-layouts  11.1 us (7%)
    all_gather x1, waiting for transfers between devices, on_device(): lax.all_gather(occ_coef, 'coef', axis=0, tiled=True)  40.9 us
    all_to_all x1, blocking collectives, on_device(): lax.all_to_all(flat_sums, 'pairs', split_axis=0, concat_axis=1, tiled=True)  35.1 us
    all_gather x1, blocking collectives, on_device(): lax.all_gather(lam_coef, 'coef', axis=0, tiled=True)  21.7 us
    all_gather x1, blocking collectives, on_device(): lax.all_gather(sig_coef, 'coef', axis=0, tiled=True)  20.9 us
    dot_general x1, matrix products, on_device(): jnp.einsum('smi,lsmn->lsin', row_shells, integrals, preferred_element_typ...  10.4 us
    dot_general x1, matrix products, on_device(): jnp.einsum('lsin,snj->ijl', quarter, col_weighted, preferred_element_type...  4.93 us
    unnamed x8, local copies, waits for them, and re-layouts  3.43 us
  transfers between devices with their start and end apart: 2, of which 1 were waited for; matrix products, arithmetic and copies ran while one was open for 1% of the time, Pallas kernels for 0%

commit v1 on v0

v1 whole, which is shorter than its diff:
```python
import jax
import jax.numpy as jnp
from jax import lax
from jax.sharding import PartitionSpec as P


def on_device(integrals, block_shells, live_counts, significance, occ_coef, lam_coef, sig_coef):
    core = lax.axis_index("pairs") % 2
    n_coef = lax.axis_size("coef")
    n_pairs = lax.axis_size("pairs")
    mine = lax.dynamic_slice_in_dim(occ_coef.T, core * 32, 32, axis=0)
    mine = mine.reshape(32, 9, 128).transpose(1, 0, 2).reshape(288, 128)
    panel = jnp.where(core == 0, lam_coef, sig_coef)
    mine = jnp.concatenate([mine, panel], axis=0)
    copies = jnp.broadcast_to(mine[None], (n_coef,) + mine.shape)
    got = lax.all_to_all(copies, "coef", 0, 0, tiled=True)
    other = lax.ppermute(got, "pairs", [(i, i ^ 1) for i in range(n_pairs)])
    low = jnp.where(core == 0, got, other)
    high = jnp.where(core == 0, other, got)
    lam_panel = low[:, 288:].reshape(64, 128)
    sig_panel = high[:, 288:].reshape(64, 128)
    table = jnp.stack([low[:, :288].reshape(72, 32, 128), high[:, :288].reshape(72, 32, 128)], axis=1)
    table = table.reshape(72, 64, 2, 64).transpose(0, 2, 1, 3).reshape(144, 64, 64)

    pair_shells = block_shells[0]
    row_shells = table[pair_shells[:, 0]]
    col_shells = table[pair_shells[:, 1]]
    screened = significance[pair_shells[:, 0], pair_shells[:, 1]]
    is_live = (jnp.arange(8) < live_counts[0, 0]) & (screened == 1)
    col_weighted = col_shells * is_live.astype(jnp.bfloat16)[:, None, None]
    quarter = jnp.einsum(
        "sim,lsmn->lsin", row_shells, integrals, preferred_element_type=jnp.float32
    ).astype(jnp.bfloat16)
    half = jnp.einsum(
        "lsin,sjn->ijl", quarter, col_weighted, preferred_element_type=jnp.float32
    )
    chunks = half.reshape(32, 2, 4, 16, 128).transpose(1, 2, 0, 3, 4).reshape(8, 512, 128)
    chunks = chunks.astype(jnp.bfloat16)
    parts = lax.all_to_all(chunks, "coef", 0, 0, tiled=True)
    reduced = jnp.sum(parts.astype(jnp.float32), axis=0).reshape(32, 16, 128)
    moved = lax.all_to_all(reduced, "pairs", 0, 0, tiled=True)
    owned = moved.reshape(32, 16, 2, 64)
    partly = jnp.einsum(
        "hqxy,yb->qhxb", owned, sig_panel.astype(jnp.float32), precision=lax.Precision.HIGHEST
    )
    lam = lam_panel.astype(jnp.float32).reshape(32, 2, 128)
    return jnp.einsum("hxa,qhxb->qab", lam, partly, precision=lax.Precision.HIGHEST)


def solution(mesh):
    placed = (
        P("pairs", "coef", None, None),
        P("pairs", "coef", None),
        P("pairs", "coef"),
        P(),
        P("coef", None),
        P("coef", None),
        P("coef", None),
    )
    return jax.shard_map(
        on_device,
        mesh=mesh,
        in_specs=placed,
        out_specs=P(("pairs", "coef"), None, None),
        check_vma=False,
    )
```

time: 164 us -> 115 us (0.70)
  the two profiles are of different devices: /device:TPU:32 before, /device:TPU:1 now
where the time goes in v1:
time: 115 us
  blocking collectives  58.7 us (51%)
  matrix products  17.1 us (15%)
  local copies, waits for them, and re-layouts  17 us (15%)
  starting transfers between devices  9.51 us (8%)
  waiting for transfers between devices  8.27 us (7%)
  other arithmetic  3.54 us (3%)
    all_to_all x1, blocking collectives, on_device(): parts = lax.all_to_all(chunks, 'coef', 0, 0, tiled=True)  31.7 us
    all_to_all x1, blocking collectives, on_device(): got = lax.all_to_all(copies, 'coef', 0, 0, tiled=True)  27 us
    dot_general x1, matrix products, on_device(): jnp.einsum('sim,lsmn->lsin', row_shells, integrals, preferred_element_typ...  10.4 us
    all_to_all x1, waiting for transfers between devices, on_device(): moved = lax.all_to_all(reduced, 'pairs', 0, 0, tiled=True)  8.26 us
    all_to_all x1, starting transfers between devices, on_device(): moved = lax.all_to_all(reduced, 'pairs', 0, 0, tiled=True)  7.52 us
    dot_general x1, matrix products, on_device(): jnp.einsum('lsin,sjn->ijl', quarter, col_weighted, preferred_element_type...  5.04 us
    reshape x1, local copies, waits for them, and re-layouts, on_device(): table.reshape(72, 64, 2, 64).transpose(0, 2, 1, 3).reshape(144, 64, 64)  4.4 us
  transfers between devices with their start and end apart: 2, of which 1 were waited for; matrix products, arithmetic and copies ran while one was open for 3% of the time, Pallas kernels for 0%

profile of v1, /device:TPU:1, one launch (start us, length us, event | category | flops | bytes accessed | tf_op | source)
XLA Modules:
  0.0 114.9 jit_solution(345747261507212439)
XLA Ops:
  0.0 0.0 copy-start
  0.0 0.9 copy-done
  1.0 0.7 broadcast_select_fusion.2
  1.7 0.1 broadcast_in_dim.2
  1.8 27.0 %all_to_all.15 = bf16[8,296,128]{2,1,0:T(8,128)(2,1)S(1)} all-to-all(bf16[8,296,128]{2,1,0:T(8,128)(2,1)S(1)} %broadcast_in_dim.2), channel_id=1, replica_groups=mesh['pairs'=32,'coef'=8] {'coef'}, dimensions={0} | all-to-all | bytes 1212416 | tf_op jit(solution)/shard_map/all_to_all | solution.py:16
  28.8 2.0 %collective-permute-start = (bf16[8,296,128]{2,1,0:T(8,128)(2,1)S(1)}, bf16[8,296,128]{2,1,0:T(8,128)(2,1)S(1)}, u32[]{:S(2)}, u32[]{:S(2)}) collective-permute-start(bf16[8,296,128]{2,1,0:T(8,128)(2,1)S(1)} %all_to_all.15), channel_id=1, source_target_pairs={{0,8},{8,0},{16,24},{24,16},{32,40},{40,32},{48,56},{56,48},{64,72... | collective-permute-start | bytes 1818632 | tf_op jit(solution)/shard_map/ppermute | solution.py:17
  31.5 0.8 or_bitcast_fusion
  32.2 1.6 %gather_fusion.1 = s32[8]{0:T(128)S(1)} fusion(s32[144,144]{1,0:T(8,128)} %param.10, s32[8]{0:T(128)S(1)} %get-tuple-element.7), kind=kCustom, calls=%fused_computation.1 | custom fusion | bytes 128 | tf_op jit(solution)/shard_map/gather | solution.py:28
  33.8 0.0 collective-permute-done
  33.8 0.1 broadcast_select_fusion
  33.9 0.0 copy-start.1
  33.9 0.8 copy-done.1
  34.8 1.1 pad_maximum_fusion
  35.9 4.4 %reshape.43 = bf16[72,64,2,64]{3,2,1,0:T(2,128)(2,1)S(1)} reshape(bf16[72,2,32,128]{3,2,1,0:T(8,128)(2,1)} %pad_maximum_fusion) | data formatting | bytes 2359296 | tf_op jit(solution)/shard_map/reshape | solution.py:23
  40.4 2.1 %copy.12 = bf16[72,2,64,64]{3,2,1,0:T(8,128)(2,1)} copy(bf16[72,2,64,64]{3,1,2,0:T(2,128)(2,1)S(1)} %bitcast.65) | data formatting | bytes 2359296 | tf_op jit(solution)/shard_map/transpose | solution.py:23
  42.4 2.2 %gather_fusion.2 = bf16[8,64,64]{2,1,0:T(8,128)(2,1)S(1)} fusion(bf16[144,64,64]{2,1,0:T(8,128)(2,1)} %bitcast.67, s32[1024]{0:T(1024)S(1)} %get-tuple-element.10), kind=kCustom, calls=%fused_computation.2 | custom fusion | bytes 131104 | tf_op jit(solution)/shard_map/gather | solution.py:26
  44.7 2.2 %gather_fusion = bf16[8,64,64]{2,1,0:T(8,128)(2,1)S(1)} fusion(bf16[144,64,64]{2,1,0:T(8,128)(2,1)} %bitcast.68, s32[1024]{0:T(1024)S(1)} %get-tuple-element.11), kind=kCustom, calls=%fused_computation | custom fusion | bytes 131104 | tf_op jit(solution)/shard_map/gather | solution.py:27
  46.9 10.4 %fusion.3 = bf16[8,64,128,64]{2,1,3,0:T(8,128)(2,1)S(1)} fusion(bf16[128,8,64,64]{0,3,2,1:T(8,128)(2,1)} %param.7, bf16[8,64,64]{2,1,0:T(8,128)(2,1)S(1)} %gather_fusion.2), kind=kOutput, calls=%fused_computation.6 | convolution fusion | flops 536870912 | bytes 16842752 | tf_op jit(solution)/shard_map/sim,lsmn->lsin/dot_general | solution.py:31
  57.3 5.0 %bitcast_convert_fusion = bf16[64,128,64]{1,0,2:T(8,128)(2,1)S(1)} fusion(bf16[8,64,128,64]{2,1,3,0:T(8,128)(2,1)S(1)} %fusion.3, bf16[8,64,64]{2,1,0:T(8,128)(2,1)S(1)} %gather_fusion, bf16[8]{0:T(256)(128)(2,1)S(1)} %and_convert_fusion), kind=kOutput, calls=%fused_computation.8 | convolution fusion | flops 537526272 | bytes 9502736 | tf_op jit(solution)/shard_map/lsin,sjn->ijl/dot_general | solution.py:34
  62.3 0.2 copy.13
  62.5 31.7 %all_to_all.16 = bf16[8,512,128]{2,1,0:T(8,128)(2,1)S(1)} all-to-all(bf16[8,512,128]{2,1,0:T(8,128)(2,1)S(1)} %bitcast.66), channel_id=1, replica_groups=mesh['pairs'=32,'coef'=8] {'coef'}, dimensions={0} | all-to-all | bytes 2097152 | tf_op jit(solution)/shard_map/all_to_all | solution.py:39
  94.2 0.8 convert_reduce_fusion
  95.0 7.5 %all-to-all-start.2 = ((f32[32,16,128]{2,1,0:T(8,128)}), f32[32,16,128]{2,1,0:T(8,128)S(1)}, u32[]{:S(2)}, u32[]{:S(2)}) async-start(f32[32,16,128]{2,1,0:T(8,128)} %bitcast.27), calls=%async_computation.2 | async-start | bytes 524288 | tf_op jit(solution)/shard_map/all_to_all | solution.py:41
  102.6 0.7 slice.35
  103.3 8.3 %all-to-all-done.2 = f32[32,16,128]{2,1,0:T(8,128)S(1)} async-done(((f32[32,16,128]{2,1,0:T(8,128)}), f32[32,16,128]{2,1,0:T(8,128)S(1)}, u32[]{:S(2)}, u32[]{:S(2)}) %all-to-all-start.2) | async-done | bytes 262176 | tf_op jit(solution)/shard_map/all_to_all | solution.py:41
  111.5 0.3 reshape.46
  111.9 0.7 convolution_bitcast_fusion.1
  112.5 1.0 convolution_bitcast_fusion
  113.6 1.3 %copy.15 = f32[16,128,128]{2,1,0:T(8,128)} copy(f32[16,128,128]{1,2,0:T(8,128)S(1)} %convolution_bitcast_fusion) | data formatting | bytes 2097152 | tf_op jit(solution)/shard_map/hxa,qhxb->qab/transpose | solution.py:47
  (8 shorter events, 0.2 us)
Async XLA Ops:
  0.0 0.9 copy-start
  28.8 5.0 %collective-permute-start = (bf16[8,296,128]{2,1,0:T(8,128)(2,1)S(1)}, bf16[8,296,128]{2,1,0:T(8,128)(2,1)S(1)}, u32[]{:S(2)}, u32[]{:S(2)}) collective-permute-start(bf16[8,296,128]{2,1,0:T(8,128)(2,1)S(1)} %all_to_all.15), channel_id=1, source_target_pairs={{0,8},{8,0},{16,24},{24,16},{32,40},{40,32},{48,56},{56,48},{64,72... | collective-permute-start | bytes 1818632 | tf_op jit(solution)/shard_map/ppermute | solution.py:17
  33.9 0.8 copy-start.1
  95.0 16.5 %all-to-all-start.2 = ((f32[32,16,128]{2,1,0:T(8,128)}), f32[32,16,128]{2,1,0:T(8,128)S(1)}, u32[]{:S(2)}, u32[]{:S(2)}) async-start(f32[32,16,128]{2,1,0:T(8,128)} %bitcast.27), calls=%async_computation.2 | async-start | bytes 524288 | tf_op jit(solution)/shard_map/all_to_all | solution.py:41

commit v2 on v0

v2 whole, which is shorter than its diff:
```python
import jax
import jax.numpy as jnp
from jax import lax
from jax.experimental import pallas as pl
from jax.experimental.pallas import tpu as pltpu
from jax.sharding import Mesh
from jax.sharding import PartitionSpec as P

f32 = jnp.float32
bf16 = jnp.bfloat16
COEF = ("zh", "zl")
BLOCK = 304
SPLIT = 160
PLACES = 0x54172630


def shift(x, k):
    return lax.ppermute(x, COEF, [(i, (i + k) % 8) for i in range(8)])


def relayout_kernel(x_ref, o_ref):
    o_ref[...] = jnp.swapaxes(x_ref[0], 0, 1)


def relayout(x):
    return pl.pallas_call(
        relayout_kernel,
        grid=(8,),
        in_specs=[pl.BlockSpec((1, 64, 64, 128), lambda s: (s, 0, 0, 0))],
        out_specs=pl.BlockSpec((64, 64, 128), lambda s: (0, s, 0)),
        out_shape=jax.ShapeDtypeStruct((64, 512, 128), bf16),
        compiler_params=pltpu.CompilerParams(vmem_limit_bytes=24 * 2**20),
        cost_estimate=pl.CostEstimate(flops=0, bytes_accessed=2**24, transcendentals=0),
    )(x)


STEP = 16
WIDE = 16


def transform_kernel(
    sc_ref, mine_ref, other_ref, x_ref, keep_ref, up1_ref, down1_ref, up2_ref, down2_ref, lhs_ref, cw_ref, q_ref
):
    n = pl.program_id(0)
    core = sc_ref[40]
    z = sc_ref[41]

    @pl.when(n == 0)
    def _():
        lane = lax.broadcasted_iota(jnp.int32, (64, 128), 1)

        def block(row, half, want):
            row = pl.multiple_of(row, 16)
            a = mine_ref[pl.ds(row, 32), :].astype(f32)
            b = other_ref[pl.ds(row, 32), :].astype(f32)
            t = jnp.concatenate([jnp.where(core == 0, a, b), jnp.where(core == 0, b, a)], axis=0)
            return jnp.where(half == want, t, pltpu.roll(t, 64, 1))

        def two(base, k):
            low = block(sc_ref[base + 2 * k], sc_ref[base + 8 + 2 * k], 0)
            high = block(sc_ref[base + 2 * k + 1], sc_ref[base + 9 + 2 * k], 1)
            return low, high

        rows, cols = [], []
        for k in range(4):
            low, high = two(0, k)
            rows.append(jnp.where(lane < 64, low, high).astype(bf16))
            low, high = two(16, k)
            low = low * sc_ref[32 + 2 * k].astype(f32)
            high = high * sc_ref[33 + 2 * k].astype(f32)
            cols.append(jnp.where(lane < 64, low, high).astype(bf16))
        rows = jnp.concatenate(rows, axis=1)
        cols = jnp.concatenate(cols, axis=1)
        r = lax.broadcasted_iota(jnp.int32, (512, 64), 0)
        c = lax.broadcasted_iota(jnp.int32, (512, 64), 1)
        spread = ((r >> 3) == c).astype(f32).astype(bf16)
        wide = jnp.dot(spread, rows, preferred_element_type=f32)
        r = lax.broadcasted_iota(jnp.int32, (512, 512), 0)
        c = lax.broadcasted_iota(jnp.int32, (512, 512), 1)
        lhs_ref[...] = jnp.where((r & 7) == (c >> 6), wide, 0.0).astype(bf16)
        order = (((r & 63) << 3) + (r >> 6) == c).astype(f32).astype(bf16)
        cw_ref[...] = jnp.dot(cols, order, preferred_element_type=f32).astype(bf16)

    def first(t, carry):
        rhs = jnp.concatenate([x_ref[WIDE * t + k] for k in range(WIDE)], axis=1)
        res = jnp.dot(lhs_ref[...], rhs, preferred_element_type=f32)
        for i in range(64):
            for k in range(WIDE // 2):
                a = res[i * 8 : i * 8 + 8, k * 256 : k * 256 + 128]
                b = res[i * 8 : i * 8 + 8, k * 256 + 128 : k * 256 + 256]
                row = pl.multiple_of(i * 512 + n * (STEP * 8) + t * (8 * WIDE) + k * 16, 16)
                q_ref[pl.ds(row, 16), :] = jnp.concatenate([a, b], axis=0).astype(bf16)
        return carry

    lax.fori_loop(0, STEP // WIDE, first, 0)

    @pl.when(n == 64 // STEP - 1)
    def _():
        cw = jnp.concatenate(
            [cw_ref[pl.ds(pl.multiple_of(lax.rem(z + e, 4) * 16, 16), 16), :] for e in range(4)], axis=0
        )

        def second(g, carry):
            rhs = jnp.concatenate(
                [q_ref[pl.ds(pl.multiple_of((g * 16 + k) * 512, 16), 512), :] for k in range(16)], axis=1
            )
            res = jnp.dot(cw, rhs, preferred_element_type=f32)
            for k in range(16):
                r = res[:, k * 128 : (k + 1) * 128]
                rows = pl.ds(pl.multiple_of(g * 256 + k * 16, 16), 16)
                keep_ref[rows, :] = r[0:16]
                up1_ref[rows, :] = r[16:32].astype(bf16)
                down1_ref[rows, :] = r[48:64].astype(bf16)

                @pl.when(g < 2)
                def _():
                    up2_ref[rows, :] = r[32:48].astype(bf16)

                @pl.when(g >= 2)
                def _():
                    rows = pl.ds(pl.multiple_of((g - 2) * 256 + k * 16, 16), 16)
                    down2_ref[rows, :] = r[32:48].astype(bf16)

            return carry

        lax.fori_loop(0, 4, second, 0)


def transform(scalars, mine, other, x):
    def whole(n, *_):
        return (0, 0)

    return pl.pallas_call(
        transform_kernel,
        grid_spec=pltpu.PrefetchScalarGridSpec(
            num_scalar_prefetch=1,
            grid=(64 // STEP,),
            in_specs=[
                pl.BlockSpec((8 * BLOCK, 128), whole),
                pl.BlockSpec((8 * BLOCK, 128), whole),
                pl.BlockSpec((STEP, 512, 128), lambda n, *_: (n, 0, 0)),
            ],
            out_specs=[pl.BlockSpec((1024, 128), whole)] * 3 + [pl.BlockSpec((512, 128), whole)] * 2,
            scratch_shapes=[
                pltpu.VMEM((512, 512), bf16),
                pltpu.VMEM((64, 512), bf16),
                pltpu.VMEM((64 * 512, 128), bf16),
            ],
        ),
        out_shape=[jax.ShapeDtypeStruct((1024, 128), f32)]
        + [jax.ShapeDtypeStruct((1024, 128), bf16)] * 2
        + [jax.ShapeDtypeStruct((512, 128), bf16)] * 2,
        compiler_params=pltpu.CompilerParams(vmem_limit_bytes=40 * 2**20),
        cost_estimate=pl.CostEstimate(flops=2**33, bytes_accessed=10 * 2**20, transcendentals=0),
    )(scalars, mine, other, x)


def split(x):
    high = x.astype(bf16)
    return high, (x - high.astype(f32)).astype(bf16)


def final_kernel(m_ref, lam_ref, sig_ref, o_ref, low_ref, high_ref):
    m = m_ref[...].astype(f32).reshape(32, 2, 16, 128)
    h = (m[:, 0] + m[:, 1]).reshape(512, 128)
    sig = sig_ref[...]
    zero = jnp.zeros_like(sig)
    pair = jnp.concatenate([jnp.concatenate([sig, zero], axis=1), jnp.concatenate([zero, sig], axis=1)], axis=0)
    pair = jnp.concatenate([pair, pair], axis=0)
    t = jnp.dot(jnp.concatenate(split(h), axis=1), pair, preferred_element_type=f32)
    low_ref[...] = t[:, :128]
    high_ref[...] = t[:, 128:]
    cols = []
    for q in range(16):
        low = low_ref[pl.ds(q, 32, stride=16), :]
        high = high_ref[pl.ds(q, 32, stride=16), :]
        cols.append(jnp.concatenate(split(jnp.concatenate([low, high], axis=0)), axis=0))
    lam = lam_ref[...]
    res = jnp.dot(jnp.concatenate([lam, lam], axis=1), jnp.concatenate(cols, axis=1), preferred_element_type=f32)
    for q in range(16):
        o_ref[q] = res[:, q * 128 : (q + 1) * 128]


def final(m, lam, sig):
    return pl.pallas_call(
        final_kernel,
        out_shape=jax.ShapeDtypeStruct((16, 128, 128), f32),
        scratch_shapes=[pltpu.VMEM((512, 128), f32)] * 2,
        compiler_params=pltpu.CompilerParams(vmem_limit_bytes=24 * 2**20),
        cost_estimate=pl.CostEstimate(flops=2**28, bytes_accessed=2**21, transcendentals=0),
    )(m, lam, sig)


def on_device(integrals, block_shells, live_counts, significance, occ_coef, lam_coef, sig_coef):
    core = lax.axis_index("pairs") % 2
    z = lax.axis_index(COEF)

    own = lax.dynamic_slice_in_dim(occ_coef.T, core * 32, 32, axis=0)
    own = own.reshape(32, 9, 128).transpose(1, 0, 2).reshape(288, 128)
    own = jnp.concatenate([own, lam_coef, sig_coef], axis=0)
    below = shift(own, 3)
    above = shift(own, -3)
    from_below = shift(jnp.concatenate([own, above, below[:SPLIT]], axis=0), 1)
    from_above = shift(jnp.concatenate([own, below, above[SPLIT:]], axis=0), -1)
    mine = jnp.concatenate(
        [own, below, above, from_above[: 2 * BLOCK], from_below, from_above[2 * BLOCK :]], axis=0
    )
    other = lax.ppermute(mine, "pairs", [(i, i ^ 1) for i in range(32)])

    x = relayout(integrals.transpose(1, 2, 3, 0))

    shells = block_shells[0].T
    owner = shells // 18
    inner = shells % 18
    place = (PLACES >> (4 * ((owner - z) % 8))) & 15
    rows = place * BLOCK + (inner // 2) * 32
    halves = inner % 2
    screened = significance[shells[0], shells[1]]
    live = ((jnp.arange(8) < live_counts[0, 0]) & (screened == 1)).astype(jnp.int32)
    scalars = jnp.concatenate(
        [rows[0], halves[0], rows[1], halves[1], live, jnp.stack([core, z]).astype(jnp.int32)]
    )

    keep, up1, down1, up2, down2 = transform(scalars, mine, other, x)
    near = shift(up1, 1).astype(f32) + shift(down1, -1).astype(f32)
    far = jnp.concatenate([shift(up2, 2), shift(down2, -2)], axis=0).astype(f32)
    summed = (keep + near + far).astype(bf16).reshape(64, 16, 128)
    moved = lax.all_to_all(summed, ("pairs", "zh"), 0, 0, tiled=True)

    panels = mine.reshape(8, BLOCK, 128)[:, 288:]
    place = (PLACES >> (4 * ((jnp.arange(8) - z) % 8))) & 15
    panels = panels[place]
    lam = panels[:, :8].reshape(32, 2, 128).transpose(2, 1, 0).reshape(128, 64)
    sig = panels[:, 8:].reshape(64, 128)
    return final(moved, lam, sig)


def solution(mesh):
    fine = Mesh(mesh.devices.reshape(32, 2, 4), ("pairs",) + COEF)
    placed = (
        P("pairs", COEF, None, None),
        P("pairs", COEF, None),
        P("pairs", COEF),
        P(),
        P(COEF, None),
        P(COEF, None),
        P(COEF, None),
    )
    return jax.shard_map(
        on_device,
        mesh=fine,
        in_specs=placed,
        out_specs=P(("pairs",) + COEF, None, None),
        check_vma=False,
    )
```

time: 164 us -> 91.8 us (0.56)
  blocking collectives: 77.8 us -> 0 us
  starting transfers between devices: 0.04 us -> 25.7 us
  matrix products: 17.7 us -> 0 us
  Pallas kernels: 0 us -> 16 us
  between operations: 14.1 us -> 0.87 us
  waiting for transfers between devices: 41.7 us -> 34 us
    all_gather x2 -> x0, blocking collectives: 42.6 us -> none  [the longest x1 21.7 us: on_device(): lax.all_gather(lam_coef, 'coef', axis=0, tiled=True)]
    all_gather x1 -> x0, waiting for transfers between devices: 40.9 us -> none  [on_device(): lax.all_gather(occ_coef, 'coef', axis=0, tiled=True)]
    all_to_all x1 -> x0, blocking collectives: 35.1 us -> none  [on_device(): lax.all_to_all(flat_sums, 'pairs', split_axis=0, concat_axis=1, tiled=True)]
    ppermute x0 -> x9, waiting for transfers between devices: none -> 18.2 us  [the longest x8 16.3 us: shift(): return lax.ppermute(x, COEF, [(i, (i + k) % 8) for i in range(8)])]
    dot_general x4 -> x0, matrix products: 17.7 us -> none  [the longest x1 10.4 us: on_device(): jnp.einsum('smi,lsmn->lsin', row_shells, integrals, preferred_element_typ...]
    pallas_call x0 -> x3, Pallas kernels: none -> 16 us  [the longest x1 10.3 us: transform(): pl.pallas_call(transform_kernel, grid_spec=pltpu.PrefetchScalarGridSpec(n...]
    all_to_all x0 -> x1, waiting for transfers between devices: none -> 15.8 us  [on_device(): moved = lax.all_to_all(summed, ('pairs', 'zh'), 0, 0, tiled=True)]
    ppermute x0 -> x9, starting transfers between devices: none -> 15.5 us  [the longest x8 15.4 us: shift(): return lax.ppermute(x, COEF, [(i, (i + k) % 8) for i in range(8)])]
  transfers between devices with their start and end apart: 2 -> 10, of which waited for: 1 -> 5; matrix products, arithmetic and copies ran while one was open for 1% -> 3% of each run, Pallas kernels for 0% -> 4%
where the time goes in v2:
time: 91.8 us; the launch traced here: 91.5 us
  waiting for transfers between devices  34 us (37%)
  starting transfers between devices  25.7 us (28%)
  Pallas kernels  16 us (17%)
  local copies, waits for them, and re-layouts  12.6 us (14%)
  other arithmetic  2.37 us (3%)
    ppermute x8, waiting for transfers between devices, shift(): return lax.ppermute(x, COEF, [(i, (i + k) % 8) for i in range(8)])  16.3 us
    all_to_all x1, waiting for transfers between devices, on_device(): moved = lax.all_to_all(summed, ('pairs', 'zh'), 0, 0, tiled=True)  15.8 us
    ppermute x8, starting transfers between devices, shift(): return lax.ppermute(x, COEF, [(i, (i + k) % 8) for i in range(8)])  15.4 us
    unnamed x23, local copies, waits for them, and re-layouts  11.1 us
    pallas_call x1, Pallas kernels, transform(): pl.pallas_call(transform_kernel, grid_spec=pltpu.PrefetchScalarGridSpec(n...  10.3 us
    all_to_all x1, starting transfers between devices, on_device(): moved = lax.all_to_all(summed, ('pairs', 'zh'), 0, 0, tiled=True)  10.2 us
    pallas_call x1, Pallas kernels, relayout(): pl.pallas_call(relayout_kernel, grid=(8,), in_specs=[pl.BlockSpec((1, 64,...  4.08 us
    ppermute x1, waiting for transfers between devices, on_device(): other = lax.ppermute(mine, 'pairs', [(i, i ^ 1) for i in range(32)])  1.89 us
  transfers between devices with their start and end apart: 10, of which 5 were waited for; matrix products, arithmetic and copies ran while one was open for 3% of the time, Pallas kernels for 4%

profile of v2, /device:TPU:32, one launch (start us, length us, event | category | flops | bytes accessed | tf_op | source)
XLA Modules:
  0.0 91.5 jit_solution(13539829002454175374)
XLA Ops:
  0.0 0.0 copy-start
  0.0 0.9 copy-done
  1.0 0.7 pad_maximum_fusion
  1.7 5.8 %collective-permute-start = (bf16[304,128]{1,0:T(8,128)(2,1)S(1)}, bf16[304,128]{1,0:T(8,128)(2,1)S(1)}, u32[]{:S(2)}, u32[]{:S(2)}) collective-permute-start(bf16[304,128]{1,0:T(8,128)(2,1)S(1)} %pad_maximum_fusion), channel_id=1, source_target_pairs={{0,3},{1,4},{2,5},{3,6},{4,7},{5,0},{6,1},{7,2},{8,11},{9,12},{10,... | collective-permute-start | bytes 233480 | tf_op jit(solution)/shard_map/ppermute | solution.py:18
  7.5 0.1 collective-permute-start.1
  7.7 0.8 fusion.16
  9.1 0.0 copy-start.1
  9.1 3.4 %copy-done.1 = bf16[128,8,64,64]{0,3,2,1:T(8,128)(2,1)S(1)} copy-done((bf16[128,8,64,64]{0,3,2,1:T(8,128)(2,1)S(1)}, bf16[128,8,64,64]{0,3,2,1:T(8,128)(2,1)}, u32[]{:S(2)}) %copy-start.1) | copy-done | bytes 8388632
  12.5 0.0 copy-start.4
  12.5 0.0 copy-start.5
  12.5 0.0 copy-start.6
  12.5 0.0 copy-start.7
  12.5 4.1 %shard_map.73.x_ref = bf16[64,512,128]{2,1,0:T(8,128)(2,1)S(1)} custom-call(bf16[8,64,64,128]{3,2,1,0:T(8,128)(2,1)S(1)} %bitcast.46), custom_call_target="tpu_custom_call" | custom-call | bytes 16777216 | tf_op jit(solution)/shard_map/pallas_call | solution.py:26
  16.6 0.0 copy-start.2
  16.6 3.3 %copy-done.2 = bf16[64,512,128]{2,1,0:T(8,128)(2,1)} copy-done((bf16[64,512,128]{2,1,0:T(8,128)(2,1)}, bf16[64,512,128]{2,1,0:T(8,128)(2,1)S(1)}, u32[]{:S(2)}) %copy-start.2) | copy-done | bytes 8388632
  19.8 0.0 copy-done.4
  19.8 0.6 gather_fusion
  20.5 0.0 copy-done.5
  20.5 0.0 copy-done.6
  20.5 0.0 collective-permute-done
  20.6 0.0 collective-permute-done.1
  20.6 1.1 %collective-permute-start.2 = (bf16[752,128]{1,0:T(8,128)(2,1)S(1)}, bf16[752,128]{1,0:T(8,128)(2,1)S(1)}, u32[]{:S(2)}, u32[]{:S(2)}) collective-permute-start(bf16[752,128]{1,0:T(8,128)(2,1)S(1)} %slice_dynamic-update-slice_fusion.3), channel_id=1, source_target_pairs={{0,7},{1,0},{2,1},{3,2},{4,3},{5,4},{6,5},{7,6},{8,15},{9,8},{10,9... | collective-permute-start | bytes 577544 | tf_op jit(solution)/shard_map/ppermute | solution.py:18
  21.7 1.1 %collective-permute-start.3 = (bf16[768,128]{1,0:T(8,128)(2,1)S(1)}, bf16[768,128]{1,0:T(8,128)(2,1)S(1)}, u32[]{:S(2)}, u32[]{:S(2)}) collective-permute-start(bf16[768,128]{1,0:T(8,128)(2,1)S(1)} %slice_dynamic-update-slice_fusion.1), channel_id=1, source_target_pairs={{0,1},{1,2},{2,3},{3,4},{4,5},{5,6},{6,7},{7,0},{8,9},{9,10},{10,1... | collective-permute-start | bytes 589832 | tf_op jit(solution)/shard_map/ppermute | solution.py:18
  22.8 4.1 %collective-permute-done.2 = bf16[752,128]{1,0:T(8,128)(2,1)S(1)} collective-permute-done((bf16[752,128]{1,0:T(8,128)(2,1)S(1)}, bf16[752,128]{1,0:T(8,128)(2,1)S(1)}, u32[]{:S(2)}, u32[]{:S(2)}) %collective-permute-start.2) | collective-permute-done | bytes 192544 | tf_op jit(solution)/shard_map/ppermute | solution.py:18
  27.0 1.7 %collective-permute-done.3 = bf16[768,128]{1,0:T(8,128)(2,1)S(1)} collective-permute-done((bf16[768,128]{1,0:T(8,128)(2,1)S(1)}, bf16[768,128]{1,0:T(8,128)(2,1)S(1)}, u32[]{:S(2)}, u32[]{:S(2)}) %collective-permute-start.3) | collective-permute-done | bytes 196640 | tf_op jit(solution)/shard_map/ppermute | solution.py:18
  28.8 0.1 collective-permute-start.4
  28.9 0.0 copy-done.7
  28.9 0.1 concatenate.25.sc_ref
  29.0 1.9 %collective-permute-done.4.other_ref = bf16[2432,128]{1,0:T(8,128)(2,1)S(1)} collective-permute-done((bf16[2432,128]{1,0:T(8,128)(2,1)S(1)}, bf16[2432,128]{1,0:T(8,128)(2,1)S(1)}, u32[]{:S(2)}, u32[]{:S(2)}) %collective-permute-start.4) | collective-permute-done | bytes 622624 | tf_op jit(solution)/shard_map/ppermute | solution.py:208
  30.9 0.0 copy-start.3
  30.9 3.4 %copy-done.3 = bf16[64,512,128]{2,1,0:T(8,128)(2,1)S(1)} copy-done((bf16[64,512,128]{2,1,0:T(8,128)(2,1)S(1)}, bf16[64,512,128]{2,1,0:T(8,128)(2,1)}, u32[]{:S(2)}) %copy-start.3) | copy-done | bytes 8388632
  34.3 10.3 %shard_map.74 = (f32[1024,128]{1,0:T(8,128)S(1)}, bf16[1024,128]{1,0:T(8,128)(2,1)S(1)}, bf16[1024,128]{1,0:T(8,128)(2,1)S(1)}, bf16[512,128]{1,0:T(8,128)(2,1)S(1)}, bf16[512,128]{1,0:T(8,128)(2,1)S(1)}) custom-call(s32[42]{0:T(128)S(1)} %concatenate.25.sc_ref, bf16[2432,128]{1,0:T(8,128)(2,1)S(1)} %slice_dynamic-update-slice_fusion.2.mine_ref, ...), custom_call_target="tpu_custom_call" | custom-call | flops 8589934592 | bytes 10485760 | tf_op jit(solution)/shard_map/pallas_call | solution.py:133
  44.6 0.3 collective-permute-start.5
  44.8 2.9 %collective-permute-start.6 = (bf16[1024,128]{1,0:T(8,128)(2,1)S(1)}, bf16[1024,128]{1,0:T(8,128)(2,1)S(1)}, u32[]{:S(2)}, u32[]{:S(2)}) collective-permute-start(bf16[1024,128]{1,0:T(8,128)(2,1)S(1)} %get-tuple-element.12), channel_id=1, source_target_pairs={{0,7},{1,0},{2,1},{3,2},{4,3},{5,4},{6,5},{7,6},{8,15},{9,8},{10,9... | collective-permute-start | bytes 786440 | tf_op jit(solution)/shard_map/ppermute | solution.py:18
  47.7 1.9 %collective-permute-start.7 = (bf16[512,128]{1,0:T(8,128)(2,1)S(1)}, bf16[512,128]{1,0:T(8,128)(2,1)S(1)}, u32[]{:S(2)}, u32[]{:S(2)}) collective-permute-start(bf16[512,128]{1,0:T(8,128)(2,1)S(1)} %get-tuple-element.13), channel_id=1, source_target_pairs={{0,2},{1,3},{2,4},{3,5},{4,6},{5,7},{6,0},{7,1},{8,10},{9,11},{10,... | collective-permute-start | bytes 393224 | tf_op jit(solution)/shard_map/ppermute | solution.py:18
  49.6 2.3 %collective-permute-start.8 = (bf16[512,128]{1,0:T(8,128)(2,1)S(1)}, bf16[512,128]{1,0:T(8,128)(2,1)S(1)}, u32[]{:S(2)}, u32[]{:S(2)}) collective-permute-start(bf16[512,128]{1,0:T(8,128)(2,1)S(1)} %get-tuple-element.14), channel_id=1, source_target_pairs={{0,6},{1,7},{2,0},{3,1},{4,2},{5,3},{6,4},{7,5},{8,14},{9,15},{10,... | collective-permute-start | bytes 393224 | tf_op jit(solution)/shard_map/ppermute | solution.py:18
  51.8 10.4 %collective-permute-done.7 = bf16[512,128]{1,0:T(8,128)(2,1)S(1)} collective-permute-done((bf16[512,128]{1,0:T(8,128)(2,1)S(1)}, bf16[512,128]{1,0:T(8,128)(2,1)S(1)}, u32[]{:S(2)}, u32[]{:S(2)}) %collective-permute-start.7) | collective-permute-done | bytes 131104 | tf_op jit(solution)/shard_map/ppermute | solution.py:18
  62.2 0.0 collective-permute-done.8
  62.2 0.0 collective-permute-done.5
  62.2 0.0 collective-permute-done.6
  62.2 0.8 add_convert_fusion
  63.1 10.2 %all-to-all-start = ((bf16[64,16,128]{2,1,0:T(8,128)(2,1)}), bf16[64,16,128]{2,1,0:T(8,128)(2,1)S(1)}, u32[]{:S(2)}, u32[]{:S(2)}) async-start(bf16[64,16,128]{2,1,0:T(8,128)(2,1)} %bitcast.17), calls=%async_computation | async-start | bytes 524288 | tf_op jit(solution)/shard_map/all_to_all | solution.py:228
  73.3 0.6 gather_fusion.1
  73.9 0.1 copy.14.lam_ref
  74.0 15.8 %all-to-all-done.m_ref = bf16[64,16,128]{2,1,0:T(8,128)(2,1)S(1)} async-done(((bf16[64,16,128]{2,1,0:T(8,128)(2,1)}), bf16[64,16,128]{2,1,0:T(8,128)(2,1)S(1)}, u32[]{:S(2)}, u32[]{:S(2)}) %all-to-all-start) | async-done | bytes 262176 | tf_op jit(solution)/shard_map/all_to_all | solution.py:228
  89.9 1.6 %shard_map.75 = f32[16,128,128]{2,1,0:T(8,128)} custom-call(bf16[64,16,128]{2,1,0:T(8,128)(2,1)S(1)} %all-to-all-done.m_ref, bf16[128,64]{1,0:T(8,128)(2,1)S(1)} %copy.14.lam_ref, bf16[64,128]{1,0:T(8,128)(2,1)S(1)} %get-tuple-element.22.sig_ref), custom_call_target="tpu_custom_call" | custom-call | flops 268435456 | bytes 2097152 | tf_op jit(solution)/shard_map/pallas_call | solution.py:185
  (21 shorter events, 0.3 us)
Async XLA Ops:
  0.0 0.9 copy-start
  1.7 18.8 %collective-permute-start = (bf16[304,128]{1,0:T(8,128)(2,1)S(1)}, bf16[304,128]{1,0:T(8,128)(2,1)S(1)}, u32[]{:S(2)}, u32[]{:S(2)}) collective-permute-start(bf16[304,128]{1,0:T(8,128)(2,1)S(1)} %pad_maximum_fusion), channel_id=1, source_target_pairs={{0,3},{1,4},{2,5},{3,6},{4,7},{5,0},{6,1},{7,2},{8,11},{9,12},{10,... | collective-permute-start | bytes 233480 | tf_op jit(solution)/shard_map/ppermute | solution.py:18
  7.5 13.0 %collective-permute-start.1 = (bf16[304,128]{1,0:T(8,128)(2,1)S(1)}, bf16[304,128]{1,0:T(8,128)(2,1)S(1)}, u32[]{:S(2)}, u32[]{:S(2)}) collective-permute-start(bf16[304,128]{1,0:T(8,128)(2,1)S(1)} %pad_maximum_fusion), channel_id=1, source_target_pairs={{0,5},{1,6},{2,7},{3,0},{4,1},{5,2},{6,3},{7,4},{8,13},{9,14},{10,... | collective-permute-start | bytes 233480 | tf_op jit(solution)/shard_map/ppermute | solution.py:18
  9.1 3.4 %copy-start.1 = (bf16[128,8,64,64]{0,3,2,1:T(8,128)(2,1)S(1)}, bf16[128,8,64,64]{0,3,2,1:T(8,128)(2,1)}, u32[]{:S(2)}) copy-start(bf16[128,8,64,64]{0,3,2,1:T(8,128)(2,1)} %param.7) | copy-start | bytes 25165828
  12.5 7.4 %copy-start.4 = (s32[144,144]{1,0:T(8,128)S(1)}, s32[144,144]{1,0:T(8,128)}, u32[]{:S(2)}) copy-start(s32[144,144]{1,0:T(8,128)} %param.10) | copy-start | bytes 248836
  12.5 8.0 %copy-start.5 = (bf16[8,128]{1,0:T(8,128)(2,1)S(1)}, bf16[8,128]{1,0:T(8,128)(2,1)}, u32[]{:S(2)}) copy-start(bf16[8,128]{1,0:T(8,128)(2,1)} %param.12) | copy-start | bytes 6148
  12.5 8.0 %copy-start.6 = (bf16[8,128]{1,0:T(8,128)(2,1)S(1)}, bf16[8,128]{1,0:T(8,128)(2,1)}, u32[]{:S(2)}) copy-start(bf16[8,128]{1,0:T(8,128)(2,1)} %param.13) | copy-start | bytes 6148
  12.5 16.4 %copy-start.7 = (s32[1,8,2]{1,2,0:T(2,128)S(1)}, s32[1,8,2]{1,2,0:T(2,128)}, u32[]{:S(2)}) copy-start(s32[1,8,2]{1,2,0:T(2,128)} %param.8) | copy-start | bytes 196
  16.6 3.3 %copy-start.2 = (bf16[64,512,128]{2,1,0:T(8,128)(2,1)}, bf16[64,512,128]{2,1,0:T(8,128)(2,1)S(1)}, u32[]{:S(2)}) copy-start(bf16[64,512,128]{2,1,0:T(8,128)(2,1)S(1)} %shard_map.73.x_ref) | copy-start | bytes 25165828
  20.6 6.4 %collective-permute-start.2 = (bf16[752,128]{1,0:T(8,128)(2,1)S(1)}, bf16[752,128]{1,0:T(8,128)(2,1)S(1)}, u32[]{:S(2)}, u32[]{:S(2)}) collective-permute-start(bf16[752,128]{1,0:T(8,128)(2,1)S(1)} %slice_dynamic-update-slice_fusion.3), channel_id=1, source_target_pairs={{0,7},{1,0},{2,1},{3,2},{4,3},{5,4},{6,5},{7,6},{8,15},{9,8},{10,9... | collective-permute-start | bytes 577544 | tf_op jit(solution)/shard_map/ppermute | solution.py:18
  21.7 7.0 %collective-permute-start.3 = (bf16[768,128]{1,0:T(8,128)(2,1)S(1)}, bf16[768,128]{1,0:T(8,128)(2,1)S(1)}, u32[]{:S(2)}, u32[]{:S(2)}) collective-permute-start(bf16[768,128]{1,0:T(8,128)(2,1)S(1)} %slice_dynamic-update-slice_fusion.1), channel_id=1, source_target_pairs={{0,1},{1,2},{2,3},{3,4},{4,5},{5,6},{6,7},{7,0},{8,9},{9,10},{10,1... | collective-permute-start | bytes 589832 | tf_op jit(solution)/shard_map/ppermute | solution.py:18
  28.8 2.1 %collective-permute-start.4 = (bf16[2432,128]{1,0:T(8,128)(2,1)S(1)}, bf16[2432,128]{1,0:T(8,128)(2,1)S(1)}, u32[]{:S(2)}, u32[]{:S(2)}) collective-permute-start(bf16[2432,128]{1,0:T(8,128)(2,1)S(1)} %slice_dynamic-update-slice_fusion.2.mine_ref), channel_id=1, source_target_pairs={{0,8},{8,0},{16,24},{24,16},{32,40},{40,32},{48,56},{56,48},{64,72... | collective-permute-start | bytes 1867784 | tf_op jit(solution)/shard_map/ppermute | solution.py:208
  30.9 3.4 %copy-start.3 = (bf16[64,512,128]{2,1,0:T(8,128)(2,1)S(1)}, bf16[64,512,128]{2,1,0:T(8,128)(2,1)}, u32[]{:S(2)}) copy-start(bf16[64,512,128]{2,1,0:T(8,128)(2,1)} %copy-done.2) | copy-start | bytes 25165828
  44.6 17.6 %collective-permute-start.5 = (bf16[1024,128]{1,0:T(8,128)(2,1)S(1)}, bf16[1024,128]{1,0:T(8,128)(2,1)S(1)}, u32[]{:S(2)}, u32[]{:S(2)}) collective-permute-start(bf16[1024,128]{1,0:T(8,128)(2,1)S(1)} %get-tuple-element.11), channel_id=1, source_target_pairs={{0,1},{1,2},{2,3},{3,4},{4,5},{5,6},{6,7},{7,0},{8,9},{9,10},{10,1... | collective-permute-start | bytes 786440 | tf_op jit(solution)/shard_map/ppermute | solution.py:18
  44.8 17.4 %collective-permute-start.6 = (bf16[1024,128]{1,0:T(8,128)(2,1)S(1)}, bf16[1024,128]{1,0:T(8,128)(2,1)S(1)}, u32[]{:S(2)}, u32[]{:S(2)}) collective-permute-start(bf16[1024,128]{1,0:T(8,128)(2,1)S(1)} %get-tuple-element.12), channel_id=1, source_target_pairs={{0,7},{1,0},{2,1},{3,2},{4,3},{5,4},{6,5},{7,6},{8,15},{9,8},{10,9... | collective-permute-start | bytes 786440 | tf_op jit(solution)/shard_map/ppermute | solution.py:18
  47.7 14.5 %collective-permute-start.7 = (bf16[512,128]{1,0:T(8,128)(2,1)S(1)}, bf16[512,128]{1,0:T(8,128)(2,1)S(1)}, u32[]{:S(2)}, u32[]{:S(2)}) collective-permute-start(bf16[512,128]{1,0:T(8,128)(2,1)S(1)} %get-tuple-element.13), channel_id=1, source_target_pairs={{0,2},{1,3},{2,4},{3,5},{4,6},{5,7},{6,0},{7,1},{8,10},{9,11},{10,... | collective-permute-start | bytes 393224 | tf_op jit(solution)/shard_map/ppermute | solution.py:18
  49.6 12.7 %collective-permute-start.8 = (bf16[512,128]{1,0:T(8,128)(2,1)S(1)}, bf16[512,128]{1,0:T(8,128)(2,1)S(1)}, u32[]{:S(2)}, u32[]{:S(2)}) collective-permute-start(bf16[512,128]{1,0:T(8,128)(2,1)S(1)} %get-tuple-element.14), channel_id=1, source_target_pairs={{0,6},{1,7},{2,0},{3,1},{4,2},{5,3},{6,4},{7,5},{8,14},{9,15},{10,... | collective-permute-start | bytes 393224 | tf_op jit(solution)/shard_map/ppermute | solution.py:18
  63.1 26.8 %all-to-all-start = ((bf16[64,16,128]{2,1,0:T(8,128)(2,1)}), bf16[64,16,128]{2,1,0:T(8,128)(2,1)S(1)}, u32[]{:S(2)}, u32[]{:S(2)}) async-start(bf16[64,16,128]{2,1,0:T(8,128)(2,1)} %bitcast.17), calls=%async_computation | async-start | bytes 524288 | tf_op jit(solution)/shard_map/all_to_all | solution.py:228

commit v3 on v0

v3 whole, which is shorter than its diff:
```python
import jax
import jax.numpy as jnp
from jax import lax
from jax.experimental import pallas as pl
from jax.experimental.pallas import tpu as pltpu
from jax.sharding import Mesh
from jax.sharding import PartitionSpec as P

f32 = jnp.float32
bf16 = jnp.bfloat16
COEF = ("zh", "zl")
BLOCK = 304
SPLIT = 160
PLACES = 0x54172630
ORDER = (0, 5, 3, 1, 6, 7, 2, 4)


def shift(x, k):
    return lax.ppermute(x, COEF, [(i, (i + k) % 8) for i in range(8)])


def relayout_kernel(x_ref, o_ref):
    s = pl.program_id(0)
    o_ref[:, pl.ds(pl.multiple_of(s * 64, 64), 64), :] = jnp.swapaxes(x_ref[0], 0, 1)


def relayout(x, part):
    return pl.pallas_call(
        relayout_kernel,
        grid=(4,),
        in_specs=[pl.BlockSpec((1, 64, 64, 128), lambda s: (4 * part + s, 0, 0, 0))],
        out_specs=pl.BlockSpec(memory_space=pltpu.VMEM),
        out_shape=jax.ShapeDtypeStruct((64, 256, 128), bf16),
        compiler_params=pltpu.CompilerParams(vmem_limit_bytes=16 * 2**20),
        cost_estimate=pl.CostEstimate(flops=0, bytes_accessed=2**23, transcendentals=0),
    )(pltpu.with_memory_space_constraint(x, pltpu.HBM))


WIDE = 16


def transform_kernel(
    shells_ref, count_ref, where_ref, screen_ref, mine_ref, other_ref, xa_ref, xb_ref,
    keep_ref, up1_ref, down1_ref, up2_ref, down2_ref, lam_ref, sig_ref,
    lhs_ref, cw_ref, q_ref,
):
    core = where_ref[0]
    z = where_ref[1]
    lane = lax.broadcasted_iota(jnp.int32, (64, 128), 1)

    def block(shell, want):
        inner = lax.rem(shell, 18)
        place = (PLACES >> (4 * ((lax.div(shell, 18) - z) & 7))) & 15
        row = pl.multiple_of(place * BLOCK + (inner >> 1) * 32, 16)
        a = mine_ref[pl.ds(row, 32), :].astype(f32)
        b = other_ref[pl.ds(row, 32), :].astype(f32)
        t = jnp.concatenate([jnp.where(core == 0, a, b), jnp.where(core == 0, b, a)], axis=0)
        return jnp.where((inner & 1) == want, t, pltpu.roll(t, 64, 1))

    def weighted(k, want):
        m = shells_ref[0, k, 0]
        n = shells_ref[0, k, 1]
        row = screen_ref[pl.ds(m, 1), :]
        at = lax.broadcasted_iota(jnp.int32, (1, 144), 1) == n
        live = jnp.sum(jnp.where(at, row, 0), axis=1, keepdims=True) == 1
        live = live & (k < count_ref[0, 0])
        return jnp.where(live, block(n, want), 0.0)

    rows, cols = [], []
    for k in range(4):
        low, high = block(shells_ref[0, 2 * k, 0], 0), block(shells_ref[0, 2 * k + 1, 0], 1)
        rows.append(jnp.where(lane < 64, low, high).astype(bf16))
        low, high = weighted(2 * k, 0), weighted(2 * k + 1, 1)
        cols.append(jnp.where(lane < 64, low, high).astype(bf16))
    rows = jnp.concatenate(rows, axis=1)
    cols = jnp.concatenate(cols, axis=1)
    r = lax.broadcasted_iota(jnp.int32, (512, 64), 0)
    c = lax.broadcasted_iota(jnp.int32, (512, 64), 1)
    spread = ((r >> 3) == c).astype(f32).astype(bf16)
    wide = jnp.dot(spread, rows, preferred_element_type=f32)
    r = lax.broadcasted_iota(jnp.int32, (512, 512), 0)
    c = lax.broadcasted_iota(jnp.int32, (512, 512), 1)
    lhs_ref[...] = jnp.where((r & 7) == (c >> 6), wide, 0.0).astype(bf16)
    r = lax.broadcasted_iota(jnp.int32, (512, 1024), 0)
    c = lax.broadcasted_iota(jnp.int32, (512, 1024), 1)
    order = (((r & 63) << 3) + (r >> 6) == ((c >> 4) << 3) + (c & 7)).astype(f32).astype(bf16)
    both = jnp.dot(cols, order, preferred_element_type=f32)
    odd = ((lax.broadcasted_iota(jnp.int32, (64, 1024), 1) >> 3) & 1) == 1
    cw_ref[0:64, :] = jnp.where(odd, 0.0, both).astype(bf16)
    cw_ref[64:128, :] = jnp.where(odd, both, 0.0).astype(bf16)
    for k, d in enumerate(ORDER):
        p = mine_ref[k * BLOCK + 288 : k * BLOCK + 304, :].astype(f32)
        to = pl.ds(pl.multiple_of(((z + d) & 7) * 8, 8), 8)
        lam_ref[to, :] = p[:8]
        sig_ref[to, :] = p[8:]

    def first(t, carry):
        rhs = jnp.concatenate(
            [
                jnp.concatenate([x_ref[WIDE * t + k] for k in range(WIDE)], axis=1)
                for x_ref in (xa_ref, xb_ref)
            ],
            axis=0,
        )
        res = jnp.dot(lhs_ref[...], rhs, preferred_element_type=f32).astype(bf16)
        for i in range(32):
            for k in range(WIDE):
                row = pl.multiple_of(i * 1024 + t * (16 * WIDE) + k * 16, 16)
                q_ref[pl.ds(row, 16), :] = res[i * 16 : (i + 1) * 16, k * 128 : (k + 1) * 128]
        return carry

    lax.fori_loop(0, 64 // WIDE, first, 0, unroll=True)

    cw = jnp.concatenate(
        [
            cw_ref[pl.ds(pl.multiple_of(h * 64 + ((z + e) & 3) * 16, 16), 16), :]
            for h in range(2)
            for e in range(4)
        ],
        axis=0,
    )
    for g in range(2):
        rhs = jnp.concatenate([q_ref[(g * 16 + k) * 1024 : (g * 16 + k + 1) * 1024, :] for k in range(16)], axis=1)
        res = jnp.dot(cw, rhs, preferred_element_type=f32)
        for k in range(16):
            for h in range(2):
                r = res[h * 64 : (h + 1) * 64, k * 128 : (k + 1) * 128]
                at = k * 32 + h * 16
                to = slice(g * 512 + at, g * 512 + at + 16)
                keep_ref[to, :] = r[0:16]
                up1_ref[to, :] = r[16:32].astype(bf16)
                down1_ref[to, :] = r[48:64].astype(bf16)
                (up2_ref, down2_ref)[g][at : at + 16, :] = r[32:48].astype(bf16)


def transform(shells, count, where, screen, mine, other, *x):
    scalar = pl.BlockSpec(memory_space=pltpu.SMEM)
    vector = pl.BlockSpec(memory_space=pltpu.VMEM)
    return pl.pallas_call(
        transform_kernel,
        in_specs=[scalar] * 3 + [vector] * 5,
        out_specs=[vector] * 7,
        scratch_shapes=[
            pltpu.VMEM((512, 512), bf16),
            pltpu.VMEM((128, 1024), bf16),
            pltpu.VMEM((32 * 1024, 128), bf16),
        ],
        out_shape=[jax.ShapeDtypeStruct((1024, 128), f32)]
        + [jax.ShapeDtypeStruct((1024, 128), bf16)] * 2
        + [jax.ShapeDtypeStruct((512, 128), bf16)] * 2
        + [jax.ShapeDtypeStruct((64, 128), f32)] * 2,
        compiler_params=pltpu.CompilerParams(vmem_limit_bytes=40 * 2**20),
        cost_estimate=pl.CostEstimate(flops=2**33, bytes_accessed=10 * 2**20, transcendentals=0),
    )(shells, count, where, screen, mine, other, *(pltpu.with_memory_space_constraint(t, pltpu.VMEM) for t in x))


def split(x):
    high = x.astype(bf16)
    return high, (x - high.astype(f32)).astype(bf16)


def final_kernel(m_ref, lam_ref, sig_ref, o_ref, low_ref, high_ref):
    m = m_ref[...].astype(f32).reshape(32, 2, 16, 128)
    h = (m[:, 0] + m[:, 1]).reshape(512, 128)
    sig = sig_ref[...].astype(bf16)
    zero = jnp.zeros_like(sig)
    pair = jnp.concatenate([jnp.concatenate([sig, zero], axis=1), jnp.concatenate([zero, sig], axis=1)], axis=0)
    pair = jnp.concatenate([pair, pair], axis=0)
    t = jnp.dot(jnp.concatenate(split(h), axis=1), pair, preferred_element_type=f32)
    low_ref[...] = t[:, :128]
    high_ref[...] = t[:, 128:]
    cols = []
    for q in range(16):
        low = low_ref[pl.ds(q, 32, stride=16), :]
        high = high_ref[pl.ds(q, 32, stride=16), :]
        cols.append(jnp.concatenate(split(jnp.concatenate([low, high], axis=0)), axis=0))
    lam = jnp.concatenate([lam_ref[pl.ds(k, 32, stride=2), :] for k in (0, 1)] * 2, axis=0).astype(bf16)
    res = lax.dot_general(lam, jnp.concatenate(cols, axis=1), (((0,), (0,)), ((), ())), preferred_element_type=f32)
    for q in range(16):
        o_ref[q] = res[:, q * 128 : (q + 1) * 128]


def final(m, lam, sig):
    return pl.pallas_call(
        final_kernel,
        out_shape=jax.ShapeDtypeStruct((16, 128, 128), f32),
        scratch_shapes=[pltpu.VMEM((512, 128), f32)] * 2,
        compiler_params=pltpu.CompilerParams(vmem_limit_bytes=24 * 2**20),
        cost_estimate=pl.CostEstimate(flops=2**28, bytes_accessed=2**21, transcendentals=0),
    )(m, lam, sig)


def on_device(integrals, block_shells, live_counts, significance, occ_coef, lam_coef, sig_coef):
    core = lax.axis_index("pairs") % 2
    z = lax.axis_index(COEF)

    own = lax.dynamic_slice_in_dim(occ_coef.T, core * 32, 32, axis=0)
    own = own.reshape(32, 9, 128).transpose(1, 0, 2).reshape(288, 128)
    own = jnp.concatenate([own, lam_coef, sig_coef], axis=0)
    below = shift(own, 3)
    above = shift(own, -3)
    x = integrals.transpose(1, 2, 3, 0)
    below, above, x_first = lax.optimization_barrier((below, above, relayout(x, 0)))
    from_below = shift(jnp.concatenate([own, above, below[:SPLIT]], axis=0), 1)
    from_above = shift(jnp.concatenate([own, below, above[SPLIT:]], axis=0), -1)
    from_below, from_above, x_second = lax.optimization_barrier((from_below, from_above, relayout(x, 1)))
    mine = jnp.concatenate(
        [own, below, above, from_above[: 2 * BLOCK], from_below, from_above[2 * BLOCK :]], axis=0
    )
    other = lax.ppermute(mine, "pairs", [(i, i ^ 1) for i in range(32)])

    where = jnp.stack([core, z]).astype(jnp.int32)
    keep, up1, down1, up2, down2, lam, sig = transform(
        block_shells, live_counts, where, significance, mine, other, x_first, x_second
    )
    near = shift(up1, 1).astype(f32) + shift(down1, -1).astype(f32)
    far = jnp.concatenate([shift(up2, 2), shift(down2, -2)], axis=0).astype(f32)
    summed = (keep + near + far).astype(bf16).reshape(64, 16, 128)
    moved = lax.all_to_all(summed, ("pairs", "zh"), 0, 0, tiled=True)

    return final(moved, lam, sig)


def solution(mesh):
    fine = Mesh(mesh.devices.reshape(32, 2, 4), ("pairs",) + COEF)
    placed = (
        P("pairs", COEF, None, None),
        P("pairs", COEF, None),
        P("pairs", COEF),
        P(),
        P(COEF, None),
        P(COEF, None),
        P(COEF, None),
    )
    return jax.shard_map(
        on_device,
        mesh=fine,
        in_specs=placed,
        out_specs=P(("pairs",) + COEF, None, None),
        check_vma=False,
    )
```

time: 164 us -> 82.8 us (0.50)
  the two profiles are of different devices: /device:TPU:32 before, /device:TPU:1 now
where the time goes in v3:
time: 82.8 us; the launch traced here: 81.4 us
  blocking collectives  23.9 us (29%)
  starting transfers between devices  18.1 us (22%)
  Pallas kernels  16.1 us (19%)
  waiting for transfers between devices  12 us (14%)
  local copies, waits for them, and re-layouts  9.56 us (12%)
  other arithmetic  0.91 us (1%)
  between operations  0.84 us (1%)
    all_to_all x1, blocking collectives, on_device(): moved = lax.all_to_all(summed, ('pairs', 'zh'), 0, 0, tiled=True)  23.9 us
    ppermute x8, starting transfers between devices, shift(): return lax.ppermute(x, COEF, [(i, (i + k) % 8) for i in range(8)])  16.4 us
    ppermute x8, waiting for transfers between devices, shift(): return lax.ppermute(x, COEF, [(i, (i + k) % 8) for i in range(8)])  11.2 us
    unnamed x26, local copies, waits for them, and re-layouts  9.45 us
    pallas_call x2, Pallas kernels, relayout(): pl.pallas_call(relayout_kernel, grid=(4,), in_specs=[pl.BlockSpec((1, 64,...  7.72 us
    pallas_call x1, Pallas kernels, transform(): pl.pallas_call(transform_kernel, in_specs=[scalar] * 3 + [vector] * 5, ou...  6.78 us
  transfers between devices with their start and end apart: 9, of which 3 were waited for; matrix products, arithmetic and copies ran while one was open for 0% of the time, Pallas kernels for 9%

profile of v3, /device:TPU:1, one launch (start us, length us, event | category | flops | bytes accessed | tf_op | source)
XLA Modules:
  0.0 81.4 jit_solution(15731003858782393707)
XLA Ops:
  0.0 0.0 copy-start
  0.0 0.9 %copy-done = bf16[1152,64]{0,1:T(8,128)(2,1)S(1)} copy-done((bf16[1152,64]{0,1:T(8,128)(2,1)S(1)}, bf16[1152,64]{0,1:T(8,128)(2,1)}, u32[]{:S(2)}) %copy-start) | copy-done | bytes 147480
  1.0 0.7 pad_maximum_fusion
  1.7 7.3 %collective-permute-start.1 = (bf16[304,128]{1,0:T(8,128)(2,1)S(1)}, bf16[304,128]{1,0:T(8,128)(2,1)S(1)}, u32[]{:S(2)}, u32[]{:S(2)}) collective-permute-start(bf16[304,128]{1,0:T(8,128)(2,1)S(1)} %pad_maximum_fusion), channel_id=1, source_target_pairs={{0,5},{1,6},{2,7},{3,0},{4,1},{5,2},{6,3},{7,4},{8,13},{9,14},{10,... | collective-permute-start | bytes 233480 | tf_op jit(solution)/shard_map/ppermute | solution.py:19
  9.0 0.0 collective-permute-start
  9.0 0.0 copy-start.6
  9.0 0.0 copy-start.7
  9.1 3.9 %shard_map.73.xa_ref = bf16[64,256,128]{2,1,0:T(8,128)(2,1)S(1)} custom-call(bf16[8,64,64,128]{3,2,1,0:T(8,128)(2,1)} %bitcast.8), custom_call_target="tpu_custom_call" | custom-call | bytes 8388608 | tf_op jit(solution)/shard_map/pallas_call | solution.py:28
  12.9 0.0 copy-start.1
  12.9 1.9 %copy-done.1 = bf16[64,256,128]{2,1,0:T(8,128)(2,1)} copy-done((bf16[64,256,128]{2,1,0:T(8,128)(2,1)}, bf16[64,256,128]{2,1,0:T(8,128)(2,1)S(1)}, u32[]{:S(2)}) %copy-start.1) | copy-done | bytes 4194328
  14.9 0.0 copy-done.6
  14.9 0.0 copy-done.7
  14.9 0.0 collective-permute-done.1
  14.9 3.6 %collective-permute-done = bf16[304,128]{1,0:T(8,128)(2,1)S(1)} collective-permute-done((bf16[304,128]{1,0:T(8,128)(2,1)S(1)}, bf16[304,128]{1,0:T(8,128)(2,1)S(1)}, u32[]{:S(2)}, u32[]{:S(2)}) %collective-permute-start) | collective-permute-done | bytes 77856 | tf_op jit(solution)/shard_map/ppermute | solution.py:19
  18.5 0.1 collective-permute-start.2
  18.6 0.0 copy-start.8
  18.6 0.0 copy-start.5
  18.7 2.7 %collective-permute-start.3 = (bf16[752,128]{1,0:T(8,128)(2,1)S(1)}, bf16[752,128]{1,0:T(8,128)(2,1)S(1)}, u32[]{:S(2)}, u32[]{:S(2)}) collective-permute-start(bf16[752,128]{1,0:T(8,128)(2,1)S(1)} %constant_dynamic-update-slice_fusion.4), channel_id=1, source_target_pairs={{0,7},{1,0},{2,1},{3,2},{4,3},{5,4},{6,5},{7,6},{8,15},{9,8},{10,9... | collective-permute-start | bytes 577544 | tf_op jit(solution)/shard_map/ppermute | solution.py:19
  21.4 3.9 %shard_map.74.xb_ref = bf16[64,256,128]{2,1,0:T(8,128)(2,1)S(1)} custom-call(bf16[8,64,64,128]{3,2,1,0:T(8,128)(2,1)} %bitcast.9), custom_call_target="tpu_custom_call" | custom-call | bytes 8388608 | tf_op jit(solution)/shard_map/pallas_call | solution.py:28
  25.2 0.0 copy-start.3
  25.3 2.0 %copy-done.3 = bf16[64,256,128]{2,1,0:T(8,128)(2,1)} copy-done((bf16[64,256,128]{2,1,0:T(8,128)(2,1)}, bf16[64,256,128]{2,1,0:T(8,128)(2,1)S(1)}, u32[]{:S(2)}) %copy-start.3) | copy-done | bytes 4194328
  27.3 0.0 collective-permute-done.3
  27.3 0.0 collective-permute-done.2
  27.3 1.6 %collective-permute-start.4 = (bf16[2432,128]{1,0:T(8,128)(2,1)S(1)}, bf16[2432,128]{1,0:T(8,128)(2,1)S(1)}, u32[]{:S(2)}, u32[]{:S(2)}) collective-permute-start(bf16[2432,128]{1,0:T(8,128)(2,1)S(1)} %constant_dynamic-update-slice_fusion.9.mine_ref), channel_id=1, source_target_pairs={{0,8},{8,0},{16,24},{24,16},{32,40},{40,32},{48,56},{56,48},{64,72... | collective-permute-start | bytes 1867784 | tf_op jit(solution)/shard_map/ppermute | solution.py:210
  29.6 0.0 copy-done.8
  29.6 0.1 copy.11.shells_ref
  29.7 0.1 pad_add_fusion.where_ref
  29.8 0.9 %collective-permute-done.4.other_ref = bf16[2432,128]{1,0:T(8,128)(2,1)S(1)} collective-permute-done((bf16[2432,128]{1,0:T(8,128)(2,1)S(1)}, bf16[2432,128]{1,0:T(8,128)(2,1)S(1)}, u32[]{:S(2)}, u32[]{:S(2)}) %collective-permute-start.4) | collective-permute-done | bytes 622624 | tf_op jit(solution)/shard_map/ppermute | solution.py:210
  30.7 0.0 copy-done.5
  30.7 0.0 copy-start.2
  30.7 2.2 %copy-done.2 = bf16[64,256,128]{2,1,0:T(8,128)(2,1)S(1)} copy-done((bf16[64,256,128]{2,1,0:T(8,128)(2,1)S(1)}, bf16[64,256,128]{2,1,0:T(8,128)(2,1)}, u32[]{:S(2)}) %copy-start.2) | copy-done | bytes 4194328
  32.9 0.0 copy-start.4
  32.9 2.2 %copy-done.4 = bf16[64,256,128]{2,1,0:T(8,128)(2,1)S(1)} copy-done((bf16[64,256,128]{2,1,0:T(8,128)(2,1)S(1)}, bf16[64,256,128]{2,1,0:T(8,128)(2,1)}, u32[]{:S(2)}) %copy-start.4) | copy-done | bytes 4194328
  35.0 6.8 %shard_map.75 = (f32[1024,128]{1,0:T(8,128)S(1)}, bf16[1024,128]{1,0:T(8,128)(2,1)S(1)}, bf16[1024,128]{1,0:T(8,128)(2,1)S(1)}, bf16[512,128]{1,0:T(8,128)(2,1)S...) custom-call(s32[1,8,2]{2,1,0:T(8,128)S(1)} %copy.11.shells_ref, ...), custom_call_target="tpu_custom_call" | custom-call | flops 8589934592 | bytes 10485760 | tf_op jit(solution)/shard_map/pallas_call | solution.py:139
  41.8 0.1 collective-permute-start.5
  41.9 2.7 %collective-permute-start.6 = (bf16[1024,128]{1,0:T(8,128)(2,1)S(1)}, bf16[1024,128]{1,0:T(8,128)(2,1)S(1)}, u32[]{:S(2)}, u32[]{:S(2)}) collective-permute-start(bf16[1024,128]{1,0:T(8,128)(2,1)S(1)} %get-tuple-element.26), channel_id=1, source_target_pairs={{0,7},{1,0},{2,1},{3,2},{4,3},{5,4},{6,5},{7,6},{8,15},{9,8},{10,9... | collective-permute-start | bytes 786440 | tf_op jit(solution)/shard_map/ppermute | solution.py:19
  44.6 0.0 collective-permute-start.7
  44.6 3.6 %collective-permute-start.8 = (bf16[512,128]{1,0:T(8,128)(2,1)S(1)}, bf16[512,128]{1,0:T(8,128)(2,1)S(1)}, u32[]{:S(2)}, u32[]{:S(2)}) collective-permute-start(bf16[512,128]{1,0:T(8,128)(2,1)S(1)} %get-tuple-element.28), channel_id=1, source_target_pairs={{0,6},{1,7},{2,0},{3,1},{4,2},{5,3},{6,4},{7,5},{8,14},{9,15},{10,... | collective-permute-start | bytes 393224 | tf_op jit(solution)/shard_map/ppermute | solution.py:19
  48.2 7.6 %collective-permute-done.7 = bf16[512,128]{1,0:T(8,128)(2,1)S(1)} collective-permute-done((bf16[512,128]{1,0:T(8,128)(2,1)S(1)}, bf16[512,128]{1,0:T(8,128)(2,1)S(1)}, u32[]{:S(2)}, u32[]{:S(2)}) %collective-permute-start.7) | collective-permute-done | bytes 131104 | tf_op jit(solution)/shard_map/ppermute | solution.py:19
  55.8 0.0 collective-permute-done.8
  55.8 0.0 collective-permute-done.5
  55.8 0.0 collective-permute-done.6
  55.8 0.1 add_convert_fusion
  55.9 23.9 %all_to_all.5.m_ref = bf16[64,16,128]{2,1,0:T(8,128)(2,1)S(1)} all-to-all(bf16[64,16,128]{2,1,0:T(8,128)(2,1)S(1)} %bitcast.10), channel_id=1, replica_groups=mesh['pairs'=32,'zh'=2,'zl'=4] {'pairs','zh'}, dimensions={0} | all-to-all | bytes 524288 | tf_op jit(solution)/shard_map/all_to_all | solution.py:219
  79.8 1.6 %shard_map.76 = f32[16,128,128]{2,1,0:T(8,128)} custom-call(bf16[64,16,128]{2,1,0:T(8,128)(2,1)S(1)} %all_to_all.5.m_ref, f32[64,128]{1,0:T(8,128)S(1)} %get-tuple-element.29.lam_ref, f32[64,128]{1,0:T(8,128)S(1)} %get-tuple-element.30.sig_ref), custom_call_target="tpu_custom_call" | custom-call | flops 268435456 | bytes 2097152 | tf_op jit(solution)/shard_map/pallas_call | solution.py:184
  (13 shorter events, 0.2 us)
Async XLA Ops:
  0.0 0.9 %copy-start = (bf16[1152,64]{0,1:T(8,128)(2,1)S(1)}, bf16[1152,64]{0,1:T(8,128)(2,1)}, u32[]{:S(2)}) copy-start(bf16[1152,64]{0,1:T(8,128)(2,1)} %param.11) | copy-start | bytes 442372
  1.7 13.2 %collective-permute-start.1 = (bf16[304,128]{1,0:T(8,128)(2,1)S(1)}, bf16[304,128]{1,0:T(8,128)(2,1)S(1)}, u32[]{:S(2)}, u32[]{:S(2)}) collective-permute-start(bf16[304,128]{1,0:T(8,128)(2,1)S(1)} %pad_maximum_fusion), channel_id=1, source_target_pairs={{0,5},{1,6},{2,7},{3,0},{4,1},{5,2},{6,3},{7,4},{8,13},{9,14},{10,... | collective-permute-start | bytes 233480 | tf_op jit(solution)/shard_map/ppermute | solution.py:19
  9.0 9.4 %collective-permute-start = (bf16[304,128]{1,0:T(8,128)(2,1)S(1)}, bf16[304,128]{1,0:T(8,128)(2,1)S(1)}, u32[]{:S(2)}, u32[]{:S(2)}) collective-permute-start(bf16[304,128]{1,0:T(8,128)(2,1)S(1)} %pad_maximum_fusion), channel_id=1, source_target_pairs={{0,3},{1,4},{2,5},{3,6},{4,7},{5,0},{6,1},{7,2},{8,11},{9,12},{10,... | collective-permute-start | bytes 233480 | tf_op jit(solution)/shard_map/ppermute | solution.py:19
  9.0 5.8 %copy-start.6 = (bf16[8,128]{1,0:T(8,128)(2,1)S(1)}, bf16[8,128]{1,0:T(8,128)(2,1)}, u32[]{:S(2)}) copy-start(bf16[8,128]{1,0:T(8,128)(2,1)} %param.12) | copy-start | bytes 6148
  9.0 5.8 %copy-start.7 = (bf16[8,128]{1,0:T(8,128)(2,1)S(1)}, bf16[8,128]{1,0:T(8,128)(2,1)}, u32[]{:S(2)}) copy-start(bf16[8,128]{1,0:T(8,128)(2,1)} %param.13) | copy-start | bytes 6148
  12.9 1.9 %copy-start.1 = (bf16[64,256,128]{2,1,0:T(8,128)(2,1)}, bf16[64,256,128]{2,1,0:T(8,128)(2,1)S(1)}, u32[]{:S(2)}) copy-start(bf16[64,256,128]{2,1,0:T(8,128)(2,1)S(1)} %shard_map.73.xa_ref) | copy-start | bytes 12582916
  18.5 8.7 %collective-permute-start.2 = (bf16[768,128]{1,0:T(8,128)(2,1)S(1)}, bf16[768,128]{1,0:T(8,128)(2,1)S(1)}, u32[]{:S(2)}, u32[]{:S(2)}) collective-permute-start(bf16[768,128]{1,0:T(8,128)(2,1)S(1)} %slice_dynamic-update-slice_fusion.1), channel_id=1, source_target_pairs={{0,1},{1,2},{2,3},{3,4},{4,5},{5,6},{6,7},{7,0},{8,9},{9,10},{10,1... | collective-permute-start | bytes 589832 | tf_op jit(solution)/shard_map/ppermute | solution.py:19
  18.6 11.0 %copy-start.8 = (s32[1,8,2]{1,2,0:T(2,128)S(1)}, s32[1,8,2]{1,2,0:T(2,128)}, u32[]{:S(2)}) copy-start(s32[1,8,2]{1,2,0:T(2,128)} %param.8) | copy-start | bytes 196
  18.6 12.0 %copy-start.5 = (s32[144,144]{1,0:T(8,128)S(1)}, s32[144,144]{1,0:T(8,128)}, u32[]{:S(2)}) copy-start(s32[144,144]{1,0:T(8,128)} %screen_ref.1) | copy-start | bytes 248836
  18.7 8.6 %collective-permute-start.3 = (bf16[752,128]{1,0:T(8,128)(2,1)S(1)}, bf16[752,128]{1,0:T(8,128)(2,1)S(1)}, u32[]{:S(2)}, u32[]{:S(2)}) collective-permute-start(bf16[752,128]{1,0:T(8,128)(2,1)S(1)} %constant_dynamic-update-slice_fusion.4), channel_id=1, source_target_pairs={{0,7},{1,0},{2,1},{3,2},{4,3},{5,4},{6,5},{7,6},{8,15},{9,8},{10,9... | collective-permute-start | bytes 577544 | tf_op jit(solution)/shard_map/ppermute | solution.py:19
  25.2 2.0 %copy-start.3 = (bf16[64,256,128]{2,1,0:T(8,128)(2,1)}, bf16[64,256,128]{2,1,0:T(8,128)(2,1)S(1)}, u32[]{:S(2)}) copy-start(bf16[64,256,128]{2,1,0:T(8,128)(2,1)S(1)} %shard_map.74.xb_ref) | copy-start | bytes 12582916
  27.3 3.3 %collective-permute-start.4 = (bf16[2432,128]{1,0:T(8,128)(2,1)S(1)}, bf16[2432,128]{1,0:T(8,128)(2,1)S(1)}, u32[]{:S(2)}, u32[]{:S(2)}) collective-permute-start(bf16[2432,128]{1,0:T(8,128)(2,1)S(1)} %constant_dynamic-update-slice_fusion.9.mine_ref), channel_id=1, source_target_pairs={{0,8},{8,0},{16,24},{24,16},{32,40},{40,32},{48,56},{56,48},{64,72... | collective-permute-start | bytes 1867784 | tf_op jit(solution)/shard_map/ppermute | solution.py:210
  30.7 2.2 %copy-start.2 = (bf16[64,256,128]{2,1,0:T(8,128)(2,1)S(1)}, bf16[64,256,128]{2,1,0:T(8,128)(2,1)}, u32[]{:S(2)}) copy-start(bf16[64,256,128]{2,1,0:T(8,128)(2,1)} %copy-done.1) | copy-start | bytes 12582916
  32.9 2.2 %copy-start.4 = (bf16[64,256,128]{2,1,0:T(8,128)(2,1)S(1)}, bf16[64,256,128]{2,1,0:T(8,128)(2,1)}, u32[]{:S(2)}) copy-start(bf16[64,256,128]{2,1,0:T(8,128)(2,1)} %copy-done.3) | copy-start | bytes 12582916
  41.8 13.9 %collective-permute-start.5 = (bf16[1024,128]{1,0:T(8,128)(2,1)S(1)}, bf16[1024,128]{1,0:T(8,128)(2,1)S(1)}, u32[]{:S(2)}, u32[]{:S(2)}) collective-permute-start(bf16[1024,128]{1,0:T(8,128)(2,1)S(1)} %get-tuple-element.25), channel_id=1, source_target_pairs={{0,1},{1,2},{2,3},{3,4},{4,5},{5,6},{6,7},{7,0},{8,9},{9,10},{10,1... | collective-permute-start | bytes 786440 | tf_op jit(solution)/shard_map/ppermute | solution.py:19
  41.9 13.9 %collective-permute-start.6 = (bf16[1024,128]{1,0:T(8,128)(2,1)S(1)}, bf16[1024,128]{1,0:T(8,128)(2,1)S(1)}, u32[]{:S(2)}, u32[]{:S(2)}) collective-permute-start(bf16[1024,128]{1,0:T(8,128)(2,1)S(1)} %get-tuple-element.26), channel_id=1, source_target_pairs={{0,7},{1,0},{2,1},{3,2},{4,3},{5,4},{6,5},{7,6},{8,15},{9,8},{10,9... | collective-permute-start | bytes 786440 | tf_op jit(solution)/shard_map/ppermute | solution.py:19
  44.6 11.2 %collective-permute-start.7 = (bf16[512,128]{1,0:T(8,128)(2,1)S(1)}, bf16[512,128]{1,0:T(8,128)(2,1)S(1)}, u32[]{:S(2)}, u32[]{:S(2)}) collective-permute-start(bf16[512,128]{1,0:T(8,128)(2,1)S(1)} %get-tuple-element.27), channel_id=1, source_target_pairs={{0,2},{1,3},{2,4},{3,5},{4,6},{5,7},{6,0},{7,1},{8,10},{9,11},{10,... | collective-permute-start | bytes 393224 | tf_op jit(solution)/shard_map/ppermute | solution.py:19
  44.6 11.2 %collective-permute-start.8 = (bf16[512,128]{1,0:T(8,128)(2,1)S(1)}, bf16[512,128]{1,0:T(8,128)(2,1)S(1)}, u32[]{:S(2)}, u32[]{:S(2)}) collective-permute-start(bf16[512,128]{1,0:T(8,128)(2,1)S(1)} %get-tuple-element.28), channel_id=1, source_target_pairs={{0,6},{1,7},{2,0},{3,1},{4,2},{5,3},{6,4},{7,5},{8,14},{9,15},{10,... | collective-permute-start | bytes 393224 | tf_op jit(solution)/shard_map/ppermute | solution.py:19

commit v4 on v3

--- a/solution.py
+++ b/solution.py
@@ -19,21 +19,25 @@
     return lax.ppermute(x, COEF, [(i, (i + k) % 8) for i in range(8)])
 
 
-def relayout_kernel(x_ref, o_ref):
+def relayout_kernel(where_ref, x_ref, o_ref):
+    del where_ref
     s = pl.program_id(0)
     o_ref[:, pl.ds(pl.multiple_of(s * 64, 64), 64), :] = jnp.swapaxes(x_ref[0], 0, 1)
 
 
-def relayout(x, part):
+def relayout(where, x, part):
     return pl.pallas_call(
         relayout_kernel,
         grid=(4,),
-        in_specs=[pl.BlockSpec((1, 64, 64, 128), lambda s: (4 * part + s, 0, 0, 0))],
+        in_specs=[
+            pl.BlockSpec(memory_space=pltpu.SMEM),
+            pl.BlockSpec((1, 64, 64, 128), lambda s: (4 * part + s, 0, 0, 0)),
+        ],
         out_specs=pl.BlockSpec(memory_space=pltpu.VMEM),
         out_shape=jax.ShapeDtypeStruct((64, 256, 128), bf16),
         compiler_params=pltpu.CompilerParams(vmem_limit_bytes=16 * 2**20),
         cost_estimate=pl.CostEstimate(flops=0, bytes_accessed=2**23, transcendentals=0),
-    )(pltpu.with_memory_space_constraint(x, pltpu.HBM))
+    )(where, pltpu.with_memory_space_constraint(x, pltpu.HBM))
 
 
 WIDE = 16
@@ -58,8 +62,8 @@
         return jnp.where((inner & 1) == want, t, pltpu.roll(t, 64, 1))
 
     def weighted(k, want):
-        m = shells_ref[0, k, 0]
-        n = shells_ref[0, k, 1]
+        m = shells_ref[0, 0, k]
+        n = shells_ref[0, 1, k]
         row = screen_ref[pl.ds(m, 1), :]
         at = lax.broadcasted_iota(jnp.int32, (1, 144), 1) == n
         live = jnp.sum(jnp.where(at, row, 0), axis=1, keepdims=True) == 1
@@ -68,7 +72,7 @@
 
     rows, cols = [], []
     for k in range(4):
-        low, high = block(shells_ref[0, 2 * k, 0], 0), block(shells_ref[0, 2 * k + 1, 0], 1)
+        low, high = block(shells_ref[0, 0, 2 * k], 0), block(shells_ref[0, 0, 2 * k + 1], 1)
         rows.append(jnp.where(lane < 64, low, high).astype(bf16))
         low, high = weighted(2 * k, 0), weighted(2 * k + 1, 1)
         cols.append(jnp.where(lane < 64, low, high).astype(bf16))
@@ -193,6 +197,7 @@
 def on_device(integrals, block_shells, live_counts, significance, occ_coef, lam_coef, sig_coef):
     core = lax.axis_index("pairs") % 2
     z = lax.axis_index(COEF)
+    where = jnp.stack([core, z]).astype(jnp.int32)
 
     own = lax.dynamic_slice_in_dim(occ_coef.T, core * 32, 32, axis=0)
     own = own.reshape(32, 9, 128).transpose(1, 0, 2).reshape(288, 128)
@@ -200,18 +205,17 @@
     below = shift(own, 3)
     above = shift(own, -3)
     x = integrals.transpose(1, 2, 3, 0)
-    below, above, x_first = lax.optimization_barrier((below, above, relayout(x, 0)))
+    below, above, x_first = lax.optimization_barrier((below, above, relayout(where, x, 0)))
     from_below = shift(jnp.concatenate([own, above, below[:SPLIT]], axis=0), 1)
     from_above = shift(jnp.concatenate([own, below, above[SPLIT:]], axis=0), -1)
-    from_below, from_above, x_second = lax.optimization_barrier((from_below, from_above, relayout(x, 1)))
+    from_below, from_above, x_second = lax.optimization_barrier((from_below, from_above, relayout(where, x, 1)))
     mine = jnp.concatenate(
         [own, below, above, from_above[: 2 * BLOCK], from_below, from_above[2 * BLOCK :]], axis=0
     )
     other = lax.ppermute(mine, "pairs", [(i, i ^ 1) for i in range(32)])
 
-    where = jnp.stack([core, z]).astype(jnp.int32)
     keep, up1, down1, up2, down2, lam, sig = transform(
-        block_shells, live_counts, where, significance, mine, other, x_first, x_second
+        block_shells.transpose(0, 2, 1), live_counts, where, significance, mine, other, x_first, x_second
     )
     near = shift(up1, 1).astype(f32) + shift(down1, -1).astype(f32)
     far = jnp.concatenate([shift(up2, 2), shift(down2, -2)], axis=0).astype(f32)

time: 82.8 us -> 78.4 us (0.947)
  local copies, waits for them, and re-layouts: 9.56 us -> 1.18 us
  waiting for transfers between devices: 12 us -> 15.6 us
    unnamed x26 -> x17, local copies, waits for them, and re-layouts: 9.45 us -> 1.07 us
    ppermute x8, waiting for transfers between devices: 11.2 us -> 14.6 us  [shift(): return lax.ppermute(x, COEF, [(i, (i + k) % 8) for i in range(8)])]
  transfers between devices with their start and end apart: 9 -> 9, of which waited for: 3 -> 4; matrix products, arithmetic and copies ran while one was open for 0% -> 0% of each run, Pallas kernels for 9% -> 10%
where the time goes in v4:
time: 78.4 us; the launch traced here: 77.1 us
  blocking collectives  23.9 us (30%)
  starting transfers between devices  18.4 us (23%)
  Pallas kernels  16.2 us (21%)
  waiting for transfers between devices  15.6 us (20%)
  local copies, waits for them, and re-layouts  1.18 us (2%)
  other arithmetic  0.91 us (1%)
  between operations  0.83 us (1%)
    all_to_all x1, blocking collectives, on_device(): moved = lax.all_to_all(summed, ('pairs', 'zh'), 0, 0, tiled=True)  23.9 us
    ppermute x8, starting transfers between devices, shift(): return lax.ppermute(x, COEF, [(i, (i + k) % 8) for i in range(8)])  16.5 us
    ppermute x8, waiting for transfers between devices, shift(): return lax.ppermute(x, COEF, [(i, (i + k) % 8) for i in range(8)])  14.6 us
    pallas_call x2, Pallas kernels, relayout(): pl.pallas_call(relayout_kernel, grid=(4,), in_specs=[pl.BlockSpec(memory_...  7.81 us
    pallas_call x1, Pallas kernels, transform(): pl.pallas_call(transform_kernel, in_specs=[scalar] * 3 + [vector] * 5, ou...  6.76 us
    ppermute x1, starting transfers between devices, on_device(): other = lax.ppermute(mine, 'pairs', [(i, i ^ 1) for i in range(32)])  1.91 us
    pallas_call x1, Pallas kernels, final(): pl.pallas_call(final_kernel, out_shape=jax.ShapeDtypeStruct((16, 128, 128...  1.64 us
  transfers between devices with their start and end apart: 9, of which 4 were waited for; matrix products, arithmetic and copies ran while one was open for 0% of the time, Pallas kernels for 10%

profile of v4, /device:TPU:1, one launch (start us, length us, event | category | flops | bytes accessed | tf_op | source)
XLA Modules:
  0.0 77.1 jit_solution(10852970614983851353)
XLA Ops:
  0.0 0.0 copy-start
  0.0 0.9 %copy-done = bf16[1152,64]{0,1:T(8,128)(2,1)S(1)} copy-done((bf16[1152,64]{0,1:T(8,128)(2,1)S(1)}, bf16[1152,64]{0,1:T(8,128)(2,1)}, u32[]{:S(2)}) %copy-start) | copy-done | bytes 147480
  1.0 0.7 pad_maximum_fusion
  1.7 7.3 %collective-permute-start.1 = (bf16[304,128]{1,0:T(8,128)(2,1)S(1)}, bf16[304,128]{1,0:T(8,128)(2,1)S(1)}, u32[]{:S(2)}, u32[]{:S(2)}) collective-permute-start(bf16[304,128]{1,0:T(8,128)(2,1)S(1)} %pad_maximum_fusion), channel_id=1, source_target_pairs={{0,5},{1,6},{2,7},{3,0},{4,1},{5,2},{6,3},{7,4},{8,13},{9,14},{10,... | collective-permute-start | bytes 233480 | tf_op jit(solution)/shard_map/ppermute | solution.py:19
  9.0 0.0 collective-permute-start
  9.0 0.1 pad_add_fusion.where_ref
  9.1 0.0 copy-start.3
  9.1 0.0 copy-start.4
  9.1 3.9 %shard_map.73.xa_ref = bf16[64,256,128]{2,1,0:T(8,128)(2,1)S(1)} custom-call(s32[2]{0:T(128)S(1)} %pad_add_fusion.where_ref, bf16[8,64,64,128]{3,2,1,0:T(8,128)(2,1)} %bitcast.10), custom_call_target="tpu_custom_call" | custom-call | bytes 8388608 | tf_op jit(solution)/shard_map/pallas_call | solution.py:29
  13.0 0.0 copy-done.3
  13.1 0.0 copy-done.4
  13.1 0.7 collective-permute-done.1
  13.8 4.6 %collective-permute-done = bf16[304,128]{1,0:T(8,128)(2,1)S(1)} collective-permute-done((bf16[304,128]{1,0:T(8,128)(2,1)S(1)}, bf16[304,128]{1,0:T(8,128)(2,1)S(1)}, u32[]{:S(2)}, u32[]{:S(2)}) %collective-permute-start) | collective-permute-done | bytes 77856 | tf_op jit(solution)/shard_map/ppermute | solution.py:19
  18.5 0.1 collective-permute-start.2
  18.6 0.0 copy-start.1
  18.6 0.0 copy-start.2
  18.7 2.7 %collective-permute-start.3 = (bf16[752,128]{1,0:T(8,128)(2,1)S(1)}, bf16[752,128]{1,0:T(8,128)(2,1)S(1)}, u32[]{:S(2)}, u32[]{:S(2)}) collective-permute-start(bf16[752,128]{1,0:T(8,128)(2,1)S(1)} %constant_dynamic-update-slice_fusion.4), channel_id=1, source_target_pairs={{0,7},{1,0},{2,1},{3,2},{4,3},{5,4},{6,5},{7,6},{8,15},{9,8},{10,9... | collective-permute-start | bytes 577544 | tf_op jit(solution)/shard_map/ppermute | solution.py:19
  21.4 3.9 %shard_map.74.xb_ref = bf16[64,256,128]{2,1,0:T(8,128)(2,1)S(1)} custom-call(s32[2]{0:T(128)S(1)} %pad_add_fusion.where_ref, bf16[8,64,64,128]{3,2,1,0:T(8,128)(2,1)} %bitcast.11), custom_call_target="tpu_custom_call" | custom-call | bytes 8388608 | tf_op jit(solution)/shard_map/pallas_call | solution.py:29
  25.3 0.0 collective-permute-done.3
  25.3 0.0 collective-permute-done.2
  25.4 1.9 %collective-permute-start.4 = (bf16[2432,128]{1,0:T(8,128)(2,1)S(1)}, bf16[2432,128]{1,0:T(8,128)(2,1)S(1)}, u32[]{:S(2)}, u32[]{:S(2)}) collective-permute-start(bf16[2432,128]{1,0:T(8,128)(2,1)S(1)} %constant_dynamic-update-slice_fusion.9.mine_ref), channel_id=1, source_target_pairs={{0,8},{8,0},{16,24},{24,16},{32,40},{40,32},{48,56},{56,48},{64,72... | collective-permute-start | bytes 1867784 | tf_op jit(solution)/shard_map/ppermute | solution.py:215
  27.9 1.0 %collective-permute-done.4.other_ref = bf16[2432,128]{1,0:T(8,128)(2,1)S(1)} collective-permute-done((bf16[2432,128]{1,0:T(8,128)(2,1)S(1)}, bf16[2432,128]{1,0:T(8,128)(2,1)S(1)}, u32[]{:S(2)}, u32[]{:S(2)}) %collective-permute-start.4) | collective-permute-done | bytes 622624 | tf_op jit(solution)/shard_map/ppermute | solution.py:215
  29.0 0.0 copy-done.1
  29.0 0.0 copy-done.2
  29.0 6.8 %shard_map.75 = (f32[1024,128]{1,0:T(8,128)S(1)}, bf16[1024,128]{1,0:T(8,128)(2,1)S(1)}, bf16[1024,128]{1,0:T(8,128)(2,1)S(1)}, bf16[512,128]{1,0:T(8,128)(2,1)S...) custom-call(s32[1,2,8]{2,1,0:T(2,128)S(1)} %bitcast.9, ...), custom_call_target="tpu_custom_call" | custom-call | flops 8589934592 | bytes 10485760 | tf_op jit(solution)/shard_map/pallas_call | solution.py:143
  35.7 0.1 collective-permute-start.5
  35.8 2.8 %collective-permute-start.6 = (bf16[1024,128]{1,0:T(8,128)(2,1)S(1)}, bf16[1024,128]{1,0:T(8,128)(2,1)S(1)}, u32[]{:S(2)}, u32[]{:S(2)}) collective-permute-start(bf16[1024,128]{1,0:T(8,128)(2,1)S(1)} %get-tuple-element.26), channel_id=1, source_target_pairs={{0,7},{1,0},{2,1},{3,2},{4,3},{5,4},{6,5},{7,6},{8,15},{9,8},{10,9... | collective-permute-start | bytes 786440 | tf_op jit(solution)/shard_map/ppermute | solution.py:19
  38.6 0.0 collective-permute-start.7
  38.6 3.6 %collective-permute-start.8 = (bf16[512,128]{1,0:T(8,128)(2,1)S(1)}, bf16[512,128]{1,0:T(8,128)(2,1)S(1)}, u32[]{:S(2)}, u32[]{:S(2)}) collective-permute-start(bf16[512,128]{1,0:T(8,128)(2,1)S(1)} %get-tuple-element.28), channel_id=1, source_target_pairs={{0,6},{1,7},{2,0},{3,1},{4,2},{5,3},{6,4},{7,5},{8,14},{9,15},{10,... | collective-permute-start | bytes 393224 | tf_op jit(solution)/shard_map/ppermute | solution.py:19
  42.2 9.2 %collective-permute-done.7 = bf16[512,128]{1,0:T(8,128)(2,1)S(1)} collective-permute-done((bf16[512,128]{1,0:T(8,128)(2,1)S(1)}, bf16[512,128]{1,0:T(8,128)(2,1)S(1)}, u32[]{:S(2)}, u32[]{:S(2)}) %collective-permute-start.7) | collective-permute-done | bytes 131104 | tf_op jit(solution)/shard_map/ppermute | solution.py:19
  51.4 0.0 collective-permute-done.8
  51.4 0.0 collective-permute-done.5
  51.4 0.0 collective-permute-done.6
  51.4 0.1 add_convert_fusion
  51.5 23.9 %all_to_all.5.m_ref = bf16[64,16,128]{2,1,0:T(8,128)(2,1)S(1)} all-to-all(bf16[64,16,128]{2,1,0:T(8,128)(2,1)S(1)} %bitcast.12), channel_id=1, replica_groups=mesh['pairs'=32,'zh'=2,'zl'=4] {'pairs','zh'}, dimensions={0} | all-to-all | bytes 524288 | tf_op jit(solution)/shard_map/all_to_all | solution.py:223
  75.4 1.6 %shard_map.76 = f32[16,128,128]{2,1,0:T(8,128)} custom-call(bf16[64,16,128]{2,1,0:T(8,128)(2,1)S(1)} %all_to_all.5.m_ref, f32[64,128]{1,0:T(8,128)S(1)} %get-tuple-element.29.lam_ref, f32[64,128]{1,0:T(8,128)S(1)} %get-tuple-element.30.sig_ref), custom_call_target="tpu_custom_call" | custom-call | flops 268435456 | bytes 2097152 | tf_op jit(solution)/shard_map/pallas_call | solution.py:188
  (13 shorter events, 0.3 us)
Async XLA Ops:
  0.0 0.9 %copy-start = (bf16[1152,64]{0,1:T(8,128)(2,1)S(1)}, bf16[1152,64]{0,1:T(8,128)(2,1)}, u32[]{:S(2)}) copy-start(bf16[1152,64]{0,1:T(8,128)(2,1)} %param.11) | copy-start | bytes 442372
  1.7 12.1 %collective-permute-start.1 = (bf16[304,128]{1,0:T(8,128)(2,1)S(1)}, bf16[304,128]{1,0:T(8,128)(2,1)S(1)}, u32[]{:S(2)}, u32[]{:S(2)}) collective-permute-start(bf16[304,128]{1,0:T(8,128)(2,1)S(1)} %pad_maximum_fusion), channel_id=1, source_target_pairs={{0,5},{1,6},{2,7},{3,0},{4,1},{5,2},{6,3},{7,4},{8,13},{9,14},{10,... | collective-permute-start | bytes 233480 | tf_op jit(solution)/shard_map/ppermute | solution.py:19
  9.0 9.4 %collective-permute-start = (bf16[304,128]{1,0:T(8,128)(2,1)S(1)}, bf16[304,128]{1,0:T(8,128)(2,1)S(1)}, u32[]{:S(2)}, u32[]{:S(2)}) collective-permute-start(bf16[304,128]{1,0:T(8,128)(2,1)S(1)} %pad_maximum_fusion), channel_id=1, source_target_pairs={{0,3},{1,4},{2,5},{3,6},{4,7},{5,0},{6,1},{7,2},{8,11},{9,12},{10,... | collective-permute-start | bytes 233480 | tf_op jit(solution)/shard_map/ppermute | solution.py:19
  9.1 3.9 %copy-start.3 = (bf16[8,128]{1,0:T(8,128)(2,1)S(1)}, bf16[8,128]{1,0:T(8,128)(2,1)}, u32[]{:S(2)}) copy-start(bf16[8,128]{1,0:T(8,128)(2,1)} %param.12) | copy-start | bytes 6148
  9.1 4.0 %copy-start.4 = (bf16[8,128]{1,0:T(8,128)(2,1)S(1)}, bf16[8,128]{1,0:T(8,128)(2,1)}, u32[]{:S(2)}) copy-start(bf16[8,128]{1,0:T(8,128)(2,1)} %param.13) | copy-start | bytes 6148
  18.5 6.8 %collective-permute-start.2 = (bf16[768,128]{1,0:T(8,128)(2,1)S(1)}, bf16[768,128]{1,0:T(8,128)(2,1)S(1)}, u32[]{:S(2)}, u32[]{:S(2)}) collective-permute-start(bf16[768,128]{1,0:T(8,128)(2,1)S(1)} %slice_dynamic-update-slice_fusion.1), channel_id=1, source_target_pairs={{0,1},{1,2},{2,3},{3,4},{4,5},{5,6},{6,7},{7,0},{8,9},{9,10},{10,1... | collective-permute-start | bytes 589832 | tf_op jit(solution)/shard_map/ppermute | solution.py:19
  18.6 10.3 %copy-start.1 = (s32[144,144]{1,0:T(8,128)S(1)}, s32[144,144]{1,0:T(8,128)}, u32[]{:S(2)}) copy-start(s32[144,144]{1,0:T(8,128)} %screen_ref.1) | copy-start | bytes 248836
  18.6 10.3 %copy-start.2 = (s32[1,8,2]{1,2,0:T(2,128)S(1)}, s32[1,8,2]{1,2,0:T(2,128)}, u32[]{:S(2)}) copy-start(s32[1,8,2]{1,2,0:T(2,128)} %param.8) | copy-start | bytes 196
  18.7 6.6 %collective-permute-start.3 = (bf16[752,128]{1,0:T(8,128)(2,1)S(1)}, bf16[752,128]{1,0:T(8,128)(2,1)S(1)}, u32[]{:S(2)}, u32[]{:S(2)}) collective-permute-start(bf16[752,128]{1,0:T(8,128)(2,1)S(1)} %constant_dynamic-update-slice_fusion.4), channel_id=1, source_target_pairs={{0,7},{1,0},{2,1},{3,2},{4,3},{5,4},{6,5},{7,6},{8,15},{9,8},{10,9... | collective-permute-start | bytes 577544 | tf_op jit(solution)/shard_map/ppermute | solution.py:19
  25.4 3.6 %collective-permute-start.4 = (bf16[2432,128]{1,0:T(8,128)(2,1)S(1)}, bf16[2432,128]{1,0:T(8,128)(2,1)S(1)}, u32[]{:S(2)}, u32[]{:S(2)}) collective-permute-start(bf16[2432,128]{1,0:T(8,128)(2,1)S(1)} %constant_dynamic-update-slice_fusion.9.mine_ref), channel_id=1, source_target_pairs={{0,8},{8,0},{16,24},{24,16},{32,40},{40,32},{48,56},{56,48},{64,72... | collective-permute-start | bytes 1867784 | tf_op jit(solution)/shard_map/ppermute | solution.py:215
  35.7 15.6 %collective-permute-start.5 = (bf16[1024,128]{1,0:T(8,128)(2,1)S(1)}, bf16[1024,128]{1,0:T(8,128)(2,1)S(1)}, u32[]{:S(2)}, u32[]{:S(2)}) collective-permute-start(bf16[1024,128]{1,0:T(8,128)(2,1)S(1)} %get-tuple-element.25), channel_id=1, source_target_pairs={{0,1},{1,2},{2,3},{3,4},{4,5},{5,6},{6,7},{7,0},{8,9},{9,10},{10,1... | collective-permute-start | bytes 786440 | tf_op jit(solution)/shard_map/ppermute | solution.py:19
  35.8 15.6 %collective-permute-start.6 = (bf16[1024,128]{1,0:T(8,128)(2,1)S(1)}, bf16[1024,128]{1,0:T(8,128)(2,1)S(1)}, u32[]{:S(2)}, u32[]{:S(2)}) collective-permute-start(bf16[1024,128]{1,0:T(8,128)(2,1)S(1)} %get-tuple-element.26), channel_id=1, source_target_pairs={{0,7},{1,0},{2,1},{3,2},{4,3},{5,4},{6,5},{7,6},{8,15},{9,8},{10,9... | collective-permute-start | bytes 786440 | tf_op jit(solution)/shard_map/ppermute | solution.py:19
  38.6 12.8 %collective-permute-start.7 = (bf16[512,128]{1,0:T(8,128)(2,1)S(1)}, bf16[512,128]{1,0:T(8,128)(2,1)S(1)}, u32[]{:S(2)}, u32[]{:S(2)}) collective-permute-start(bf16[512,128]{1,0:T(8,128)(2,1)S(1)} %get-tuple-element.27), channel_id=1, source_target_pairs={{0,2},{1,3},{2,4},{3,5},{4,6},{5,7},{6,0},{7,1},{8,10},{9,11},{10,... | collective-permute-start | bytes 393224 | tf_op jit(solution)/shard_map/ppermute | solution.py:19
  38.6 12.8 %collective-permute-start.8 = (bf16[512,128]{1,0:T(8,128)(2,1)S(1)}, bf16[512,128]{1,0:T(8,128)(2,1)S(1)}, u32[]{:S(2)}, u32[]{:S(2)}) collective-permute-start(bf16[512,128]{1,0:T(8,128)(2,1)S(1)} %get-tuple-element.28), channel_id=1, source_target_pairs={{0,6},{1,7},{2,0},{3,1},{4,2},{5,3},{6,4},{7,5},{8,14},{9,15},{10,... | collective-permute-start | bytes 393224 | tf_op jit(solution)/shard_map/ppermute | solution.py:19

commit v5 on v4

v5 whole, which is shorter than its diff:
```python
import jax
import jax.numpy as jnp
from jax import lax
from jax.experimental import pallas as pl
from jax.experimental.pallas import tpu as pltpu
from jax.sharding import Mesh
from jax.sharding import PartitionSpec as P

f32 = jnp.float32
bf16 = jnp.bfloat16
COEF = ("zh", "zl")
BLOCK = 304
SPLIT = 160
PLACES = 0x54172630
ORDER = (0, 5, 3, 1, 6, 7, 2, 4)


def shift(x, k):
    return lax.ppermute(x, COEF, [(i, (i + k) % 8) for i in range(8)])


def relayout_kernel(where_ref, x_ref, o_ref):
    del where_ref
    s = pl.program_id(0)
    o_ref[:, pl.ds(pl.multiple_of(s * 64, 64), 64), :] = jnp.swapaxes(x_ref[0], 0, 1)


def relayout(where, x, part):
    return pl.pallas_call(
        relayout_kernel,
        grid=(4,),
        in_specs=[
            pl.BlockSpec(memory_space=pltpu.SMEM),
            pl.BlockSpec((1, 64, 64, 128), lambda s: (4 * part + s, 0, 0, 0)),
        ],
        out_specs=pl.BlockSpec(memory_space=pltpu.VMEM),
        out_shape=jax.ShapeDtypeStruct((64, 256, 128), bf16),
        compiler_params=pltpu.CompilerParams(vmem_limit_bytes=16 * 2**20),
        cost_estimate=pl.CostEstimate(flops=0, bytes_accessed=2**23, transcendentals=0),
    )(where, pltpu.with_memory_space_constraint(x, pltpu.HBM))


WIDE = 16


def shell_block(shell, z, table_ref, want):
    inner = lax.rem(shell, 18)
    place = (PLACES >> (4 * ((lax.div(shell, 18) - z) & 7))) & 15
    row = pl.multiple_of(place * BLOCK + (inner >> 1) * 32, 16)
    t = table_ref[pl.ds(row, 32), :].astype(f32)
    return jnp.where((inner & 1) == want, t, pltpu.roll(t, 64, 1))


def first_product(shells_ref, z, table_ref, xa_ref, xb_ref, lhs_ref, q_ref):
    lane = lax.broadcasted_iota(jnp.int32, (32, 128), 1)
    rows = []
    for k in range(4):
        low = shell_block(shells_ref[0, 0, 2 * k], z, table_ref, 0)
        high = shell_block(shells_ref[0, 0, 2 * k + 1], z, table_ref, 1)
        rows.append(jnp.where(lane < 64, low, high).astype(bf16))
    rows = jnp.concatenate(rows, axis=1)
    r = lax.broadcasted_iota(jnp.int32, (256, 32), 0)
    c = lax.broadcasted_iota(jnp.int32, (256, 32), 1)
    spread = ((r >> 3) == c).astype(f32).astype(bf16)
    wide = jnp.dot(spread, rows, preferred_element_type=f32)
    r = lax.broadcasted_iota(jnp.int32, (256, 512), 0)
    c = lax.broadcasted_iota(jnp.int32, (256, 512), 1)
    lhs_ref[...] = jnp.where((r & 7) == (c >> 6), wide, 0.0).astype(bf16)

    def step(t, carry):
        rhs = jnp.concatenate(
            [
                jnp.concatenate([x_ref[WIDE * t + k] for k in range(WIDE)], axis=1)
                for x_ref in (xa_ref, xb_ref)
            ],
            axis=0,
        )
        res = jnp.dot(lhs_ref[...], rhs, preferred_element_type=f32).astype(bf16)
        for i in range(16):
            for k in range(WIDE):
                row = pl.multiple_of(i * 1024 + t * (16 * WIDE) + k * 16, 16)
                q_ref[pl.ds(row, 16), :] = res[i * 16 : (i + 1) * 16, k * 128 : (k + 1) * 128]
        return carry

    lax.fori_loop(0, 64 // WIDE, step, 0, unroll=True)


def second_product(z, cw_ref, q_ref, keep_ref, up, down):
    cw = jnp.concatenate(
        [cw_ref[pl.ds(pl.multiple_of(((z + d) & 7) * 16, 16), 16), :] for d in range(8)], axis=0
    )
    rhs = jnp.concatenate([q_ref[k * 1024 : (k + 1) * 1024, :] for k in range(16)], axis=1)
    res = jnp.dot(cw, rhs, preferred_element_type=f32)
    for k in range(16):
        for d in range(8):
            r = res[d * 16 : (d + 1) * 16, k * 128 : (k + 1) * 128]
            for ref, ds in ((keep_ref, (0, 3, 5)), up, down):
                if d in ds:
                    at = ds.index(d) * 256 + k * 16
                    ref[at : at + 16, :] = r.astype(ref.dtype)


SMEM = pl.BlockSpec(memory_space=pltpu.SMEM)
VMEM = pl.BlockSpec(memory_space=pltpu.VMEM)


def own_kernel(shells_ref, where_ref, mine_ref, xa_ref, xb_ref, q_ref, lam_ref, sig_ref, lhs_ref):
    z = where_ref[1]
    first_product(shells_ref, z, mine_ref, xa_ref, xb_ref, lhs_ref, q_ref)
    for k, d in enumerate(ORDER):
        p = mine_ref[k * BLOCK + 288 : k * BLOCK + 304, :].astype(f32)
        to = pl.ds(pl.multiple_of(((z + d) & 7) * 8, 8), 8)
        lam_ref[to, :] = p[:8]
        sig_ref[to, :] = p[8:]


def own_first(shells, where, mine, *x):
    return pl.pallas_call(
        own_kernel,
        in_specs=[SMEM] * 2 + [VMEM] * 3,
        out_specs=[VMEM] * 3,
        scratch_shapes=[pltpu.VMEM((256, 512), bf16)],
        out_shape=[jax.ShapeDtypeStruct((16 * 1024, 128), bf16)] + [jax.ShapeDtypeStruct((64, 128), f32)] * 2,
        compiler_params=pltpu.CompilerParams(vmem_limit_bytes=16 * 2**20),
        cost_estimate=pl.CostEstimate(flops=2**32, bytes_accessed=2**20, transcendentals=0),
    )(shells, where, mine, *(pltpu.with_memory_space_constraint(t, pltpu.VMEM) for t in x))


UP_OWN, DOWN_OWN = (1, 6, 4), (7, 2)
UP_OTHER, DOWN_OTHER = (1, 6), (7, 2, 4)


def columns_kernel(
    shells_ref, count_ref, where_ref, screen_ref, mine_ref, other_ref, q_ref, keep_ref, up_ref, down_ref, cw_ref
):
    core = where_ref[0]
    z = where_ref[1]
    lane = lax.broadcasted_iota(jnp.int32, (64, 128), 1)

    def weighted(k, want):
        m = shells_ref[0, 0, k]
        n = shells_ref[0, 1, k]
        row = screen_ref[pl.ds(m, 1), :]
        at = lax.broadcasted_iota(jnp.int32, (1, 144), 1) == n
        live = jnp.sum(jnp.where(at, row, 0), axis=1, keepdims=True) == 1
        live = live & (k < count_ref[0, 0])
        a = shell_block(n, z, mine_ref, want)
        b = shell_block(n, z, other_ref, want)
        t = jnp.concatenate([jnp.where(core == 0, a, b), jnp.where(core == 0, b, a)], axis=0)
        return jnp.where(live, t, 0.0)

    cols = []
    for k in range(4):
        low, high = weighted(2 * k, 0), weighted(2 * k + 1, 1)
        cols.append(jnp.where(lane < 64, low, high).astype(bf16))
    cols = jnp.concatenate(cols, axis=1)
    r = lax.broadcasted_iota(jnp.int32, (512, 1024), 0)
    c = lax.broadcasted_iota(jnp.int32, (512, 1024), 1)
    order = (((r & 63) << 3) + (r >> 6) == ((c >> 4) << 3) + (c & 7)).astype(f32).astype(bf16)
    both = jnp.dot(cols, order, preferred_element_type=f32)
    odd = ((lax.broadcasted_iota(jnp.int32, (64, 1024), 1) >> 3) & 1) == 1
    cw_ref[0:64, :] = jnp.where(odd, 0.0, both).astype(bf16)
    cw_ref[64:128, :] = jnp.where(odd, both, 0.0).astype(bf16)
    second_product(z, cw_ref, q_ref, keep_ref, (up_ref, UP_OWN), (down_ref, DOWN_OWN))


def own_second(shells, count, where, screen, mine, other, q):
    return pl.pallas_call(
        columns_kernel,
        in_specs=[SMEM] * 3 + [VMEM] * 4,
        out_specs=[VMEM] * 4,
        out_shape=[
            jax.ShapeDtypeStruct((768, 128), f32),
            jax.ShapeDtypeStruct((256 * len(UP_OWN), 128), bf16),
            jax.ShapeDtypeStruct((256 * len(DOWN_OWN), 128), bf16),
            jax.ShapeDtypeStruct((128, 1024), bf16),
        ],
        compiler_params=pltpu.CompilerParams(vmem_limit_bytes=16 * 2**20),
        cost_estimate=pl.CostEstimate(flops=2**31, bytes_accessed=2**20, transcendentals=0),
    )(shells, count, where, screen, mine, other, pltpu.with_memory_space_constraint(q, pltpu.VMEM))


def other_kernel(
    shells_ref, where_ref, other_ref, cw_ref, xa_ref, xb_ref, keep_ref, up_ref, down_ref, lhs_ref, q_ref
):
    z = where_ref[1]
    first_product(shells_ref, z, other_ref, xa_ref, xb_ref, lhs_ref, q_ref)
    second_product(z, cw_ref, q_ref, keep_ref, (up_ref, UP_OTHER), (down_ref, DOWN_OTHER))


def other_both(shells, where, other, cw, *x):
    return pl.pallas_call(
        other_kernel,
        in_specs=[SMEM] * 2 + [VMEM] * 4,
        out_specs=[VMEM] * 3,
        out_shape=[
            jax.ShapeDtypeStruct((768, 128), f32),
            jax.ShapeDtypeStruct((256 * len(UP_OTHER), 128), bf16),
            jax.ShapeDtypeStruct((256 * len(DOWN_OTHER), 128), bf16),
        ],
        scratch_shapes=[pltpu.VMEM((256, 512), bf16), pltpu.VMEM((16 * 1024, 128), bf16)],
        compiler_params=pltpu.CompilerParams(vmem_limit_bytes=24 * 2**20),
        cost_estimate=pl.CostEstimate(flops=2**33, bytes_accessed=2**20, transcendentals=0),
    )(shells, where, other, cw, *(pltpu.with_memory_space_constraint(t, pltpu.VMEM) for t in x))


def first_round(up, down):
    return shift(up, 1), shift(down, -1)


def second_round(keep, up_ds, from_below, down_ds, from_above):
    total = {0: keep[:256], 3: keep[256:512], 5: keep[512:]}
    for ds, got, step in ((up_ds, from_below, -1), (down_ds, from_above, 1)):
        for k, d in enumerate(ds):
            to = (d + step) % 8
            total[to] = total[to] + got[k * 256 : (k + 1) * 256].astype(f32)
    return total[0], shift(total[3].astype(bf16), 3), shift(total[5].astype(bf16), -3)


def reduced(total, from_below, from_above):
    return total + from_below.astype(f32) + from_above.astype(f32)


def split(x):
    high = x.astype(bf16)
    return high, (x - high.astype(f32)).astype(bf16)


def final_kernel(m_ref, lam_ref, sig_ref, o_ref, low_ref, high_ref):
    h = m_ref[...].reshape(512, 128)
    sig = sig_ref[...].astype(bf16)
    zero = jnp.zeros_like(sig)
    pair = jnp.concatenate([jnp.concatenate([sig, zero], axis=1), jnp.concatenate([zero, sig], axis=1)], axis=0)
    pair = jnp.concatenate([pair, pair], axis=0)
    t = jnp.dot(jnp.concatenate(split(h), axis=1), pair, preferred_element_type=f32)
    low_ref[...] = t[:, :128]
    high_ref[...] = t[:, 128:]
    cols = []
    for q in range(16):
        low = low_ref[pl.ds(q, 32, stride=16), :]
        high = high_ref[pl.ds(q, 32, stride=16), :]
        cols.append(jnp.concatenate(split(jnp.concatenate([low, high], axis=0)), axis=0))
    lam = jnp.concatenate([lam_ref[pl.ds(k, 32, stride=2), :] for k in (0, 1)] * 2, axis=0).astype(bf16)
    res = lax.dot_general(lam, jnp.concatenate(cols, axis=1), (((0,), (0,)), ((), ())), preferred_element_type=f32)
    for q in range(16):
        o_ref[q] = res[:, q * 128 : (q + 1) * 128]


def final(m, lam, sig):
    return pl.pallas_call(
        final_kernel,
        out_shape=jax.ShapeDtypeStruct((16, 128, 128), f32),
        scratch_shapes=[pltpu.VMEM((512, 128), f32)] * 2,
        compiler_params=pltpu.CompilerParams(vmem_limit_bytes=24 * 2**20),
        cost_estimate=pl.CostEstimate(flops=2**28, bytes_accessed=2**21, transcendentals=0),
    )(m, lam, sig)


def on_device(integrals, block_shells, live_counts, significance, occ_coef, lam_coef, sig_coef):
    core = lax.axis_index("pairs") % 2
    z = lax.axis_index(COEF)
    where = jnp.stack([core, z]).astype(jnp.int32)

    own = lax.dynamic_slice_in_dim(occ_coef.T, core * 32, 32, axis=0)
    own = own.reshape(32, 9, 128).transpose(1, 0, 2).reshape(288, 128)
    own = jnp.concatenate([own, lam_coef, sig_coef], axis=0)
    below = shift(own, 3)
    above = shift(own, -3)
    x = integrals.transpose(1, 2, 3, 0)
    below, above, x_first = lax.optimization_barrier((below, above, relayout(where, x, 0)))
    from_below = shift(jnp.concatenate([own, above, below[:SPLIT]], axis=0), 1)
    from_above = shift(jnp.concatenate([own, below, above[SPLIT:]], axis=0), -1)
    from_below, from_above, x_second = lax.optimization_barrier((from_below, from_above, relayout(where, x, 1)))
    mine = jnp.concatenate(
        [own, below, above, from_above[: 2 * BLOCK], from_below, from_above[2 * BLOCK :]], axis=0
    )
    other = lax.ppermute(mine, "pairs", [(i, i ^ 1) for i in range(32)])

    shells = block_shells.transpose(0, 2, 1)
    q, lam, sig = own_first(shells, where, mine, x_first, x_second)
    keep, up, down, cw = own_second(shells, live_counts, where, significance, mine, other, q)
    own_got = first_round(up, down)
    keep_other, up, down = other_both(shells, where, other, cw, x_first, x_second)
    other_got = first_round(up, down)
    own_half = second_round(keep, UP_OWN, own_got[0], DOWN_OWN, own_got[1])
    other_half = second_round(keep_other, UP_OTHER, other_got[0], DOWN_OTHER, other_got[1])
    a = reduced(*own_half)
    b = reduced(*other_half)
    summed = jnp.concatenate([jnp.where(core == 0, a, b), jnp.where(core == 0, b, a)], axis=0)
    moved = lax.all_to_all(summed.reshape(32, 16, 128), "pairs", 0, 0, tiled=True)

    return final(moved, lam, sig)


def solution(mesh):
    fine = Mesh(mesh.devices.reshape(32, 2, 4), ("pairs",) + COEF)
    placed = (
        P("pairs", COEF, None, None),
        P("pairs", COEF, None),
        P("pairs", COEF),
        P(),
        P(COEF, None),
        P(COEF, None),
        P(COEF, None),
    )
    return jax.shard_map(
        on_device,
        mesh=fine,
        in_specs=placed,
        out_specs=P(("pairs",) + COEF, None, None),
        check_vma=False,
    )
```

time: 78.4 us -> 75.4 us (0.962); the launches traced: 77.1 us -> 74.9 us
  starting transfers between devices: 18.4 us -> 26.7 us
  waiting for transfers between devices: 15.6 us -> 8.81 us
  blocking collectives: 23.9 us -> 18.4 us
  Pallas kernels: 16.2 us -> 18 us
    ppermute x8 -> x12, starting transfers between devices: 16.5 us -> 24.8 us  [shift(): return lax.ppermute(x, COEF, [(i, (i + k) % 8) for i in range(8)])]
    ppermute x8 -> x12, waiting for transfers between devices: 14.6 us -> 8.81 us  [shift(): return lax.ppermute(x, COEF, [(i, (i + k) % 8) for i in range(8)])]
    all_to_all x1, blocking collectives: 23.9 us -> 18.4 us  [on_device(): lax.all_to_all(summed.reshape(32, 16, 128), 'pairs', 0, 0, tiled=True)]
    pallas_call x1 -> x3, Pallas kernels: 6.76 us -> 8.51 us  [the longest x1 3.69 us: other_both(): pl.pallas_call(other_kernel, in_specs=[SMEM] * 2 + [VMEM] * 4, out_specs=...]
    ppermute x1, waiting for transfers between devices: 1.03 us -> 0.01 us  [on_device(): other = lax.ppermute(mine, 'pairs', [(i, i ^ 1) for i in range(32)])]
  transfers between devices with their start and end apart: 9 -> 13, of which waited for: 4 -> 4; matrix products, arithmetic and copies ran while one was open for 0% -> 0% of each run, Pallas kernels for 10% -> 20%
where the time goes in v5:
time: 75.4 us; the launch traced here: 74.9 us
  starting transfers between devices  26.7 us (35%)
  blocking collectives  18.4 us (24%)
  Pallas kernels  18 us (24%)
  waiting for transfers between devices  8.81 us (12%)
  local copies, waits for them, and re-layouts  1.18 us (2%)
  other arithmetic  0.96 us (1%)
  between operations  0.89 us (1%)
    ppermute x12, starting transfers between devices, shift(): return lax.ppermute(x, COEF, [(i, (i + k) % 8) for i in range(8)])  24.8 us
    all_to_all x1, blocking collectives, on_device(): lax.all_to_all(summed.reshape(32, 16, 128), 'pairs', 0, 0, tiled=True)  18.4 us
    ppermute x12, waiting for transfers between devices, shift(): return lax.ppermute(x, COEF, [(i, (i + k) % 8) for i in range(8)])  8.81 us
    pallas_call x2, Pallas kernels, relayout(): pl.pallas_call(relayout_kernel, grid=(4,), in_specs=[pl.BlockSpec(memory_...  7.81 us
    pallas_call x1, Pallas kernels, other_both(): pl.pallas_call(other_kernel, in_specs=[SMEM] * 2 + [VMEM] * 4, out_specs=...  3.69 us
    pallas_call x1, Pallas kernels, own_first(): pl.pallas_call(own_kernel, in_specs=[SMEM] * 2 + [VMEM] * 3, out_specs=[V...  3.19 us
    ppermute x1, starting transfers between devices, on_device(): other = lax.ppermute(mine, 'pairs', [(i, i ^ 1) for i in range(32)])  1.92 us
    pallas_call x1, Pallas kernels, final(): pl.pallas_call(final_kernel, out_shape=jax.ShapeDtypeStruct((16, 128, 128...  1.64 us
  transfers between devices with their start and end apart: 13, of which 4 were waited for; matrix products, arithmetic and copies ran while one was open for 0% of the time, Pallas kernels for 20%

profile of v5, /device:TPU:1, one launch (start us, length us, event | category | flops | bytes accessed | tf_op | source)
XLA Modules:
  0.0 74.9 jit_solution(10213099852584501827)
XLA Ops:
  0.0 0.0 copy-start
  0.0 0.9 %copy-done = bf16[1152,64]{0,1:T(8,128)(2,1)S(1)} copy-done((bf16[1152,64]{0,1:T(8,128)(2,1)S(1)}, bf16[1152,64]{0,1:T(8,128)(2,1)}, u32[]{:S(2)}) %copy-start) | copy-done | bytes 147480
  1.0 0.7 pad_maximum_fusion.1
  1.7 7.3 %collective-permute-start.1 = (bf16[304,128]{1,0:T(8,128)(2,1)S(1)}, bf16[304,128]{1,0:T(8,128)(2,1)S(1)}, u32[]{:S(2)}, u32[]{:S(2)}) collective-permute-start(bf16[304,128]{1,0:T(8,128)(2,1)S(1)} %pad_maximum_fusion.1), channel_id=1, source_target_pairs={{0,5},{1,6},{2,7},{3,0},{4,1},{5,2},{6,3},{7,4},{8,13},{9,14},{10,... | collective-permute-start | bytes 233480 | tf_op jit(solution)/shard_map/ppermute | solution.py:19
  9.0 0.0 collective-permute-start
  9.0 0.1 pad_add_fusion.where_ref
  9.1 0.0 copy-start.3
  9.1 0.0 copy-start.4
  9.1 3.9 %shard_map.73.xa_ref = bf16[64,256,128]{2,1,0:T(8,128)(2,1)S(1)} custom-call(s32[2]{0:T(128)S(1)} %pad_add_fusion.where_ref, bf16[8,64,64,128]{3,2,1,0:T(8,128)(2,1)} %bitcast.12), custom_call_target="tpu_custom_call" | custom-call | bytes 8388608 | tf_op jit(solution)/shard_map/pallas_call | solution.py:29
  13.0 0.0 copy-done.3
  13.1 0.0 copy-done.4
  13.1 0.7 collective-permute-done.1
  13.8 4.6 %collective-permute-done = bf16[304,128]{1,0:T(8,128)(2,1)S(1)} collective-permute-done((bf16[304,128]{1,0:T(8,128)(2,1)S(1)}, bf16[304,128]{1,0:T(8,128)(2,1)S(1)}, u32[]{:S(2)}, u32[]{:S(2)}) %collective-permute-start) | collective-permute-done | bytes 77856 | tf_op jit(solution)/shard_map/ppermute | solution.py:19
  18.5 0.1 collective-permute-start.2
  18.6 0.0 copy-start.2
  18.6 2.7 %collective-permute-start.3 = (bf16[752,128]{1,0:T(8,128)(2,1)S(1)}, bf16[752,128]{1,0:T(8,128)(2,1)S(1)}, u32[]{:S(2)}, u32[]{:S(2)}) collective-permute-start(bf16[752,128]{1,0:T(8,128)(2,1)S(1)} %constant_dynamic-update-slice_fusion.4), channel_id=1, source_target_pairs={{0,7},{1,0},{2,1},{3,2},{4,3},{5,4},{6,5},{7,6},{8,15},{9,8},{10,9... | collective-permute-start | bytes 577544 | tf_op jit(solution)/shard_map/ppermute | solution.py:19
  21.4 3.9 %shard_map.74.xb_ref = bf16[64,256,128]{2,1,0:T(8,128)(2,1)S(1)} custom-call(s32[2]{0:T(128)S(1)} %pad_add_fusion.where_ref, bf16[8,64,64,128]{3,2,1,0:T(8,128)(2,1)} %bitcast.13), custom_call_target="tpu_custom_call" | custom-call | bytes 8388608 | tf_op jit(solution)/shard_map/pallas_call | solution.py:29
  25.3 0.0 collective-permute-done.3
  25.3 0.0 collective-permute-done.2
  25.4 1.9 %collective-permute-start.4 = (bf16[2432,128]{1,0:T(8,128)(2,1)S(1)}, bf16[2432,128]{1,0:T(8,128)(2,1)S(1)}, u32[]{:S(2)}, u32[]{:S(2)}) collective-permute-start(bf16[2432,128]{1,0:T(8,128)(2,1)S(1)} %constant_dynamic-update-slice_fusion.9.mine_ref), channel_id=1, source_target_pairs={{0,8},{8,0},{16,24},{24,16},{32,40},{40,32},{48,56},{56,48},{64,72... | collective-permute-start | bytes 1867784 | tf_op jit(solution)/shard_map/ppermute | solution.py:277
  27.9 0.0 copy-done.2
  28.0 0.0 copy-start.1
  28.0 3.2 %shard_map.75 = (bf16[16384,128]{1,0:T(8,128)(2,1)S(1)}, f32[64,128]{1,0:T(8,128)S(1)}, f32[64,128]{1,0:T(8,128)S(1)}) custom-call(s32[1,2,8]{2,1,0:T(2,128)S(1)} %bitcast.9, s32[2]{0:T(128)S(1)} %pad_add_fusion.where_ref, bf16[2432,128]{1,0:T(8,128)(2,1)S(1)} %constant_dynamic-update-slice_fusion.9.mine_ref, bf16[64,256,128]{2,1,0:T(8,128)(2,1)S(1)} %shard_map.73.xa_ref, ...), custom_call_target="tpu_custom_call" | custom-call | flops 4294967296 | bytes 1048576 | tf_op jit(solution)/shard_map/pallas_call | solution.py:118
  31.2 0.0 collective-permute-done.4.other_ref
  31.2 0.0 copy-done.1
  31.2 1.6 %shard_map.76 = (f32[768,128]{1,0:T(8,128)S(1)}, bf16[768,128]{1,0:T(8,128)(2,1)S(1)}, bf16[512,128]{1,0:T(8,128)(2,1)S(1)}, bf16[128,1024]{1,0:T(8,128)(2,1)S(1)}) custom-call(s32[1,2,8]{2,1,0:T(2,128)S(1)} %bitcast.10, s32[1,1]{1,0:T(1,128)S(6)} %copy.25.count_ref, s32[2]{0:T(128)S(1)} %pad_add_fusion.where_ref, s32[144,144]{1,0:T(8,128)S(1)} %copy-done.1, ...), custom_call_target="tpu_custom_call" | custom-call | flops 2147483648 | bytes 1048576 | tf_op jit(solution)/shard_map/pallas_call | solution.py:168
  32.8 2.8 %collective-permute-start.6 = (bf16[512,128]{1,0:T(8,128)(2,1)S(1)}, bf16[512,128]{1,0:T(8,128)(2,1)S(1)}, u32[]{:S(2)}, u32[]{:S(2)}) collective-permute-start(bf16[512,128]{1,0:T(8,128)(2,1)S(1)} %get-tuple-element.30), channel_id=1, source_target_pairs={{0,7},{1,0},{2,1},{3,2},{4,3},{5,4},{6,5},{7,6},{8,15},{9,8},{10,9... | collective-permute-start | bytes 393224 | tf_op jit(solution)/shard_map/ppermute | solution.py:19
  35.6 0.0 collective-permute-start.5
  35.6 3.7 %shard_map.77 = (f32[768,128]{1,0:T(8,128)S(1)}, bf16[512,128]{1,0:T(8,128)(2,1)S(1)}, bf16[768,128]{1,0:T(8,128)(2,1)S(1)}) custom-call(s32[1,2,8]{2,1,0:T(2,128)S(1)} %bitcast.11, s32[2]{0:T(128)S(1)} %pad_add_fusion.where_ref, bf16[2432,128]{1,0:T(8,128)(2,1)S(1)} %collective-permute-done.4.other_ref, bf16[128,1024]{1,0:T(8,128)(2,1)S(1)} %get-tuple-element.31.cw_ref, ...), custom_call_target="tpu_custom_call" | custom-call | flops 8589934592 | bytes 1048576 | tf_op jit(solution)/shard_map/pallas_call | solution.py:192
  39.3 0.1 collective-permute-start.9
  39.4 2.7 %collective-permute-start.10 = (bf16[768,128]{1,0:T(8,128)(2,1)S(1)}, bf16[768,128]{1,0:T(8,128)(2,1)S(1)}, u32[]{:S(2)}, u32[]{:S(2)}) collective-permute-start(bf16[768,128]{1,0:T(8,128)(2,1)S(1)} %get-tuple-element.34), channel_id=1, source_target_pairs={{0,7},{1,0},{2,1},{3,2},{4,3},{5,4},{6,5},{7,6},{8,15},{9,8},{10,9... | collective-permute-start | bytes 589832 | tf_op jit(solution)/shard_map/ppermute | solution.py:19
  42.1 0.0 collective-permute-done.6
  42.1 0.9 %collective-permute-done.5 = bf16[768,128]{1,0:T(8,128)(2,1)S(1)} collective-permute-done((bf16[768,128]{1,0:T(8,128)(2,1)S(1)}, bf16[768,128]{1,0:T(8,128)(2,1)S(1)}, u32[]{:S(2)}, u32[]{:S(2)}) %collective-permute-start.5) | collective-permute-done | bytes 196640 | tf_op jit(solution)/shard_map/ppermute | solution.py:19
  43.0 0.1 collective-permute-start.7
  43.1 4.5 %collective-permute-start.8 = (bf16[256,128]{1,0:T(8,128)(2,1)S(1)}, bf16[256,128]{1,0:T(8,128)(2,1)S(1)}, u32[]{:S(2)}, u32[]{:S(2)}) collective-permute-start(bf16[256,128]{1,0:T(8,128)(2,1)S(1)} %get-tuple-element.42), channel_id=1, source_target_pairs={{0,5},{1,6},{2,7},{3,0},{4,1},{5,2},{6,3},{7,4},{8,13},{9,14},{10,... | collective-permute-start | bytes 196616 | tf_op jit(solution)/shard_map/ppermute | solution.py:19
  47.6 0.0 collective-permute-done.9
  47.6 0.0 collective-permute-done.10
  47.6 0.1 collective-permute-start.11
  47.7 4.5 %collective-permute-start.12 = (bf16[256,128]{1,0:T(8,128)(2,1)S(1)}, bf16[256,128]{1,0:T(8,128)(2,1)S(1)}, u32[]{:S(2)}, u32[]{:S(2)}) collective-permute-start(bf16[256,128]{1,0:T(8,128)(2,1)S(1)} %get-tuple-element.40), channel_id=1, source_target_pairs={{0,5},{1,6},{2,7},{3,0},{4,1},{5,2},{6,3},{7,4},{8,13},{9,14},{10,... | collective-permute-start | bytes 196616 | tf_op jit(solution)/shard_map/ppermute | solution.py:19
  52.2 0.0 collective-permute-done.7
  52.2 0.0 collective-permute-done.8
  52.2 2.6 %collective-permute-done.11 = bf16[256,128]{1,0:T(8,128)(2,1)S(1)} collective-permute-done((bf16[256,128]{1,0:T(8,128)(2,1)S(1)}, bf16[256,128]{1,0:T(8,128)(2,1)S(1)}, u32[]{:S(2)}, u32[]{:S(2)}) %collective-permute-start.11) | collective-permute-done | bytes 65568 | tf_op jit(solution)/shard_map/ppermute | solution.py:19
  54.8 0.0 collective-permute-done.12
  54.8 0.1 broadcast_select_fusion.1
  54.9 18.4 %all_to_all.5.m_ref = f32[32,16,128]{2,1,0:T(8,128)S(1)} all-to-all(f32[32,16,128]{2,1,0:T(8,128)S(1)} %bitcast.14), channel_id=1, replica_groups=mesh['pairs'=32,'zh'=2,'zl'=4] {'pairs'}, dimensions={0} | all-to-all | bytes 524288 | tf_op jit(solution)/shard_map/all_to_all | solution.py:290
  73.3 1.6 %shard_map.78 = f32[16,128,128]{2,1,0:T(8,128)} custom-call(f32[32,16,128]{2,1,0:T(8,128)S(1)} %all_to_all.5.m_ref, f32[64,128]{1,0:T(8,128)S(1)} %get-tuple-element.35.lam_ref, f32[64,128]{1,0:T(8,128)S(1)} %get-tuple-element.36.sig_ref), custom_call_target="tpu_custom_call" | custom-call | flops 268435456 | bytes 2097152 | tf_op jit(solution)/shard_map/pallas_call | solution.py:250
  (16 shorter events, 0.4 us)
Async XLA Ops:
  0.0 0.9 %copy-start = (bf16[1152,64]{0,1:T(8,128)(2,1)S(1)}, bf16[1152,64]{0,1:T(8,128)(2,1)}, u32[]{:S(2)}) copy-start(bf16[1152,64]{0,1:T(8,128)(2,1)} %param.11) | copy-start | bytes 442372
  1.7 12.1 %collective-permute-start.1 = (bf16[304,128]{1,0:T(8,128)(2,1)S(1)}, bf16[304,128]{1,0:T(8,128)(2,1)S(1)}, u32[]{:S(2)}, u32[]{:S(2)}) collective-permute-start(bf16[304,128]{1,0:T(8,128)(2,1)S(1)} %pad_maximum_fusion.1), channel_id=1, source_target_pairs={{0,5},{1,6},{2,7},{3,0},{4,1},{5,2},{6,3},{7,4},{8,13},{9,14},{10,... | collective-permute-start | bytes 233480 | tf_op jit(solution)/shard_map/ppermute | solution.py:19
  9.0 9.4 %collective-permute-start = (bf16[304,128]{1,0:T(8,128)(2,1)S(1)}, bf16[304,128]{1,0:T(8,128)(2,1)S(1)}, u32[]{:S(2)}, u32[]{:S(2)}) collective-permute-start(bf16[304,128]{1,0:T(8,128)(2,1)S(1)} %pad_maximum_fusion.1), channel_id=1, source_target_pairs={{0,3},{1,4},{2,5},{3,6},{4,7},{5,0},{6,1},{7,2},{8,11},{9,12},{10,... | collective-permute-start | bytes 233480 | tf_op jit(solution)/shard_map/ppermute | solution.py:19
  9.1 3.9 %copy-start.3 = (bf16[8,128]{1,0:T(8,128)(2,1)S(1)}, bf16[8,128]{1,0:T(8,128)(2,1)}, u32[]{:S(2)}) copy-start(bf16[8,128]{1,0:T(8,128)(2,1)} %param.12) | copy-start | bytes 6148
  9.1 4.0 %copy-start.4 = (bf16[8,128]{1,0:T(8,128)(2,1)S(1)}, bf16[8,128]{1,0:T(8,128)(2,1)}, u32[]{:S(2)}) copy-start(bf16[8,128]{1,0:T(8,128)(2,1)} %param.13) | copy-start | bytes 6148
  18.5 6.8 %collective-permute-start.2 = (bf16[768,128]{1,0:T(8,128)(2,1)S(1)}, bf16[768,128]{1,0:T(8,128)(2,1)S(1)}, u32[]{:S(2)}, u32[]{:S(2)}) collective-permute-start(bf16[768,128]{1,0:T(8,128)(2,1)S(1)} %slice_dynamic-update-slice_fusion.1), channel_id=1, source_target_pairs={{0,1},{1,2},{2,3},{3,4},{4,5},{5,6},{6,7},{7,0},{8,9},{9,10},{10,1... | collective-permute-start | bytes 589832 | tf_op jit(solution)/shard_map/ppermute | solution.py:19
  18.6 9.3 %copy-start.2 = (s32[1,8,2]{1,2,0:T(2,128)S(1)}, s32[1,8,2]{1,2,0:T(2,128)}, u32[]{:S(2)}) copy-start(s32[1,8,2]{1,2,0:T(2,128)} %param.8) | copy-start | bytes 196
  18.6 6.6 %collective-permute-start.3 = (bf16[752,128]{1,0:T(8,128)(2,1)S(1)}, bf16[752,128]{1,0:T(8,128)(2,1)S(1)}, u32[]{:S(2)}, u32[]{:S(2)}) collective-permute-start(bf16[752,128]{1,0:T(8,128)(2,1)S(1)} %constant_dynamic-update-slice_fusion.4), channel_id=1, source_target_pairs={{0,7},{1,0},{2,1},{3,2},{4,3},{5,4},{6,5},{7,6},{8,15},{9,8},{10,9... | collective-permute-start | bytes 577544 | tf_op jit(solution)/shard_map/ppermute | solution.py:19
  25.4 5.8 %collective-permute-start.4 = (bf16[2432,128]{1,0:T(8,128)(2,1)S(1)}, bf16[2432,128]{1,0:T(8,128)(2,1)S(1)}, u32[]{:S(2)}, u32[]{:S(2)}) collective-permute-start(bf16[2432,128]{1,0:T(8,128)(2,1)S(1)} %constant_dynamic-update-slice_fusion.9.mine_ref), channel_id=1, source_target_pairs={{0,8},{8,0},{16,24},{24,16},{32,40},{40,32},{48,56},{56,48},{64,72... | collective-permute-start | bytes 1867784 | tf_op jit(solution)/shard_map/ppermute | solution.py:277
  28.0 3.2 %copy-start.1 = (s32[144,144]{1,0:T(8,128)S(1)}, s32[144,144]{1,0:T(8,128)}, u32[]{:S(2)}) copy-start(s32[144,144]{1,0:T(8,128)} %screen_ref.1) | copy-start | bytes 248836
  32.8 9.3 %collective-permute-start.6 = (bf16[512,128]{1,0:T(8,128)(2,1)S(1)}, bf16[512,128]{1,0:T(8,128)(2,1)S(1)}, u32[]{:S(2)}, u32[]{:S(2)}) collective-permute-start(bf16[512,128]{1,0:T(8,128)(2,1)S(1)} %get-tuple-element.30), channel_id=1, source_target_pairs={{0,7},{1,0},{2,1},{3,2},{4,3},{5,4},{6,5},{7,6},{8,15},{9,8},{10,9... | collective-permute-start | bytes 393224 | tf_op jit(solution)/shard_map/ppermute | solution.py:19
  35.6 7.4 %collective-permute-start.5 = (bf16[768,128]{1,0:T(8,128)(2,1)S(1)}, bf16[768,128]{1,0:T(8,128)(2,1)S(1)}, u32[]{:S(2)}, u32[]{:S(2)}) collective-permute-start(bf16[768,128]{1,0:T(8,128)(2,1)S(1)} %get-tuple-element.29), channel_id=1, source_target_pairs={{0,1},{1,2},{2,3},{3,4},{4,5},{5,6},{6,7},{7,0},{8,9},{9,10},{10,1... | collective-permute-start | bytes 589832 | tf_op jit(solution)/shard_map/ppermute | solution.py:19
  39.3 8.3 %collective-permute-start.9 = (bf16[512,128]{1,0:T(8,128)(2,1)S(1)}, bf16[512,128]{1,0:T(8,128)(2,1)S(1)}, u32[]{:S(2)}, u32[]{:S(2)}) collective-permute-start(bf16[512,128]{1,0:T(8,128)(2,1)S(1)} %get-tuple-element.33), channel_id=1, source_target_pairs={{0,1},{1,2},{2,3},{3,4},{4,5},{5,6},{6,7},{7,0},{8,9},{9,10},{10,1... | collective-permute-start | bytes 393224 | tf_op jit(solution)/shard_map/ppermute | solution.py:19
  39.4 8.2 %collective-permute-start.10 = (bf16[768,128]{1,0:T(8,128)(2,1)S(1)}, bf16[768,128]{1,0:T(8,128)(2,1)S(1)}, u32[]{:S(2)}, u32[]{:S(2)}) collective-permute-start(bf16[768,128]{1,0:T(8,128)(2,1)S(1)} %get-tuple-element.34), channel_id=1, source_target_pairs={{0,7},{1,0},{2,1},{3,2},{4,3},{5,4},{6,5},{7,6},{8,15},{9,8},{10,9... | collective-permute-start | bytes 589832 | tf_op jit(solution)/shard_map/ppermute | solution.py:19
  43.0 9.2 %collective-permute-start.7 = (bf16[256,128]{1,0:T(8,128)(2,1)S(1)}, bf16[256,128]{1,0:T(8,128)(2,1)S(1)}, u32[]{:S(2)}, u32[]{:S(2)}) collective-permute-start(bf16[256,128]{1,0:T(8,128)(2,1)S(1)} %get-tuple-element.41), channel_id=1, source_target_pairs={{0,3},{1,4},{2,5},{3,6},{4,7},{5,0},{6,1},{7,2},{8,11},{9,12},{10,... | collective-permute-start | bytes 196616 | tf_op jit(solution)/shard_map/ppermute | solution.py:19
  43.1 9.1 %collective-permute-start.8 = (bf16[256,128]{1,0:T(8,128)(2,1)S(1)}, bf16[256,128]{1,0:T(8,128)(2,1)S(1)}, u32[]{:S(2)}, u32[]{:S(2)}) collective-permute-start(bf16[256,128]{1,0:T(8,128)(2,1)S(1)} %get-tuple-element.42), channel_id=1, source_target_pairs={{0,5},{1,6},{2,7},{3,0},{4,1},{5,2},{6,3},{7,4},{8,13},{9,14},{10,... | collective-permute-start | bytes 196616 | tf_op jit(solution)/shard_map/ppermute | solution.py:19
  47.6 7.1 %collective-permute-start.11 = (bf16[256,128]{1,0:T(8,128)(2,1)S(1)}, bf16[256,128]{1,0:T(8,128)(2,1)S(1)}, u32[]{:S(2)}, u32[]{:S(2)}) collective-permute-start(bf16[256,128]{1,0:T(8,128)(2,1)S(1)} %get-tuple-element.39), channel_id=1, source_target_pairs={{0,3},{1,4},{2,5},{3,6},{4,7},{5,0},{6,1},{7,2},{8,11},{9,12},{10,... | collective-permute-start | bytes 196616 | tf_op jit(solution)/shard_map/ppermute | solution.py:19
  47.7 7.0 %collective-permute-start.12 = (bf16[256,128]{1,0:T(8,128)(2,1)S(1)}, bf16[256,128]{1,0:T(8,128)(2,1)S(1)}, u32[]{:S(2)}, u32[]{:S(2)}) collective-permute-start(bf16[256,128]{1,0:T(8,128)(2,1)S(1)} %get-tuple-element.40), channel_id=1, source_target_pairs={{0,5},{1,6},{2,7},{3,0},{4,1},{5,2},{6,3},{7,4},{8,13},{9,14},{10,... | collective-permute-start | bytes 196616 | tf_op jit(solution)/shard_map/ppermute | solution.py:19

commit v6 on v5

v6 whole, which is shorter than its diff:
```python
import jax
import jax.numpy as jnp
from jax import lax
from jax.experimental import pallas as pl
from jax.experimental.pallas import tpu as pltpu
from jax.sharding import Mesh
from jax.sharding import PartitionSpec as P

f32 = jnp.float32
bf16 = jnp.bfloat16
COEF = ("zh", "zl")
BLOCK = 304
SPLIT = 160
PLACES = 0x54172630
ORDER = (0, 5, 3, 1, 6, 7, 2, 4)


def swap(x, k):
    pairs = []
    for p in range(32):
        for z in range(8):
            way = 1 - 2 * ((z + p) % 2)
            pairs.append((p * 8 + z, p * 8 + (z + way * k) % 8))
    return lax.ppermute(x, ("pairs",) + COEF, pairs)


def relayout_kernel(where_ref, x_ref, o_ref):
    del where_ref
    s = pl.program_id(0)
    o_ref[:, pl.ds(pl.multiple_of(s * 64, 64), 64), :] = jnp.swapaxes(x_ref[0], 0, 1)


def relayout(where, x, part):
    return pl.pallas_call(
        relayout_kernel,
        grid=(4,),
        in_specs=[
            pl.BlockSpec(memory_space=pltpu.SMEM),
            pl.BlockSpec((1, 64, 64, 128), lambda s: (4 * part + s, 0, 0, 0)),
        ],
        out_specs=pl.BlockSpec(memory_space=pltpu.VMEM),
        out_shape=jax.ShapeDtypeStruct((64, 256, 128), bf16),
        compiler_params=pltpu.CompilerParams(vmem_limit_bytes=16 * 2**20),
        cost_estimate=pl.CostEstimate(flops=0, bytes_accessed=2**23, transcendentals=0),
    )(where, pltpu.with_memory_space_constraint(x, pltpu.HBM))


WIDE = 16


def shell_block(shell, z, way, table_ref, want):
    inner = lax.rem(shell, 18)
    place = (PLACES >> (4 * ((way * (lax.div(shell, 18) - z)) & 7))) & 15
    row = pl.multiple_of(place * BLOCK + (inner >> 1) * 32, 16)
    t = table_ref[pl.ds(row, 32), :].astype(f32)
    return jnp.where((inner & 1) == want, t, pltpu.roll(t, 64, 1))


def first_product(shells_ref, z, way, table_ref, xa_ref, xb_ref, lhs_ref, q_ref):
    lane = lax.broadcasted_iota(jnp.int32, (32, 128), 1)
    rows = []
    for k in range(4):
        low = shell_block(shells_ref[0, 0, 2 * k], z, way, table_ref, 0)
        high = shell_block(shells_ref[0, 0, 2 * k + 1], z, way, table_ref, 1)
        rows.append(jnp.where(lane < 64, low, high).astype(bf16))
    r = lax.broadcasted_iota(jnp.int32, (128, 32), 0)
    c = lax.broadcasted_iota(jnp.int32, (128, 32), 1)
    spread = ((r >> 2) == c).astype(f32).astype(bf16)
    r = lax.broadcasted_iota(jnp.int32, (128, 256), 0)
    c = lax.broadcasted_iota(jnp.int32, (128, 256), 1)
    for half in range(2):
        four = jnp.concatenate(rows[2 * half : 2 * half + 2], axis=1)
        wide = jnp.dot(spread, four, preferred_element_type=f32)
        lhs_ref[half * 128 : (half + 1) * 128, :] = jnp.where((r & 3) == (c >> 6), wide, 0.0).astype(bf16)

    def step(t, carry):
        for half, x_ref in enumerate((xa_ref, xb_ref)):
            rhs = jnp.concatenate([x_ref[WIDE * t + k] for k in range(WIDE)], axis=1)
            lhs = lhs_ref[half * 128 : (half + 1) * 128, :]
            res = jnp.dot(lhs, rhs, preferred_element_type=f32).astype(bf16)
            for g in range(8):
                for k in range(WIDE):
                    row = pl.multiple_of(g * 2048 + half * 1024 + t * (16 * WIDE) + k * 16, 16)
                    q_ref[pl.ds(row, 16), :] = res[g * 16 : (g + 1) * 16, k * 128 : (k + 1) * 128]
        return carry

    lax.fori_loop(0, 64 // WIDE, step, 0, unroll=True)


def second_product(z, way, cw_ref, q_ref, keep_ref, up, down):
    cw = jnp.concatenate(
        [
            cw_ref[pl.ds(pl.multiple_of(b * 128 + ((z + way * d) & 7) * 16, 16), 16), :]
            for b in range(2)
            for d in range(8)
        ],
        axis=0,
    )
    rhs = jnp.concatenate([q_ref[g * 2048 : (g + 1) * 2048, :] for g in range(8)], axis=1)
    res = jnp.dot(cw, rhs, preferred_element_type=f32)
    for g in range(8):
        for b in range(2):
            for d in range(8):
                r = res[b * 128 + d * 16 : b * 128 + (d + 1) * 16, g * 128 : (g + 1) * 128]
                for ref, ds in ((keep_ref, (0, 3, 5)), up, down):
                    if d in ds:
                        at = ds.index(d) * 256 + (g * 2 + b) * 16
                        ref[at : at + 16, :] = r.astype(ref.dtype)


SMEM = pl.BlockSpec(memory_space=pltpu.SMEM)
VMEM = pl.BlockSpec(memory_space=pltpu.VMEM)


def own_kernel(shells_ref, where_ref, mine_ref, xa_ref, xb_ref, q_ref, lam_ref, sig_ref, lhs_ref):
    z = where_ref[1]
    way = where_ref[2]
    first_product(shells_ref, z, way, mine_ref, xa_ref, xb_ref, lhs_ref, q_ref)
    for k, d in enumerate(ORDER):
        p = mine_ref[k * BLOCK + 288 : k * BLOCK + 304, :].astype(f32)
        to = pl.ds(pl.multiple_of(((z + way * d) & 7) * 8, 8), 8)
        lam_ref[to, :] = p[:8]
        sig_ref[to, :] = p[8:]


def own_first(shells, where, mine, *x):
    return pl.pallas_call(
        own_kernel,
        in_specs=[SMEM] * 2 + [VMEM] * 3,
        out_specs=[VMEM] * 3,
        scratch_shapes=[pltpu.VMEM((256, 256), bf16)],
        out_shape=[jax.ShapeDtypeStruct((16 * 1024, 128), bf16)] + [jax.ShapeDtypeStruct((64, 128), f32)] * 2,
        compiler_params=pltpu.CompilerParams(vmem_limit_bytes=16 * 2**20),
        cost_estimate=pl.CostEstimate(flops=2**32, bytes_accessed=2**20, transcendentals=0),
    )(shells, where, mine, *(pltpu.with_memory_space_constraint(t, pltpu.VMEM) for t in x))


UP_OWN, DOWN_OWN = (1, 6, 4), (7, 2)
UP_OTHER, DOWN_OTHER = UP_OWN, DOWN_OWN


def columns_kernel(
    shells_ref, count_ref, where_ref, screen_ref, mine_ref, other_ref, q_ref, keep_ref, up_ref, down_ref, cw_ref
):
    core = where_ref[0]
    z = where_ref[1]
    way = where_ref[2]
    lane = lax.broadcasted_iota(jnp.int32, (64, 128), 1)

    def weighted(k, want):
        m = shells_ref[0, 0, k]
        n = shells_ref[0, 1, k]
        row = screen_ref[pl.ds(m, 1), :]
        at = lax.broadcasted_iota(jnp.int32, (1, 144), 1) == n
        live = jnp.sum(jnp.where(at, row, 0), axis=1, keepdims=True) == 1
        live = live & (k < count_ref[0, 0])
        a = shell_block(n, z, way, mine_ref, want)
        b = shell_block(n, z, -way, other_ref, want)
        t = jnp.concatenate([jnp.where(core == 0, a, b), jnp.where(core == 0, b, a)], axis=0)
        return jnp.where(live, t, 0.0)

    cols = []
    for k in range(4):
        low, high = weighted(2 * k, 0), weighted(2 * k + 1, 1)
        cols.append(jnp.where(lane < 64, low, high).astype(bf16))
    r = lax.broadcasted_iota(jnp.int32, (256, 1024), 0)
    c = lax.broadcasted_iota(jnp.int32, (256, 1024), 1)
    order = (((r & 63) << 2) + (r >> 6) == ((c >> 4) << 2) + (c & 3)).astype(f32).astype(bf16)
    column = (lax.broadcasted_iota(jnp.int32, (64, 1024), 1) >> 2) & 3
    for half in range(2):
        four = jnp.concatenate(cols[2 * half : 2 * half + 2], axis=1)
        wide = jnp.dot(four, order, preferred_element_type=f32)
        for i in range(4):
            cw_ref[i * 64 : (i + 1) * 64, half * 1024 : (half + 1) * 1024] = jnp.where(
                column == i, wide, 0.0
            ).astype(bf16)
    second_product(z, way, cw_ref, q_ref, keep_ref, (up_ref, UP_OWN), (down_ref, DOWN_OWN))


def own_second(shells, count, where, screen, mine, other, q):
    return pl.pallas_call(
        columns_kernel,
        in_specs=[SMEM] * 3 + [VMEM] * 4,
        out_specs=[VMEM] * 4,
        out_shape=[
            jax.ShapeDtypeStruct((768, 128), f32),
            jax.ShapeDtypeStruct((256 * len(UP_OWN), 128), bf16),
            jax.ShapeDtypeStruct((256 * len(DOWN_OWN), 128), bf16),
            jax.ShapeDtypeStruct((256, 2048), bf16),
        ],
        compiler_params=pltpu.CompilerParams(vmem_limit_bytes=16 * 2**20),
        cost_estimate=pl.CostEstimate(flops=2**31, bytes_accessed=2**20, transcendentals=0),
    )(shells, count, where, screen, mine, other, pltpu.with_memory_space_constraint(q, pltpu.VMEM))


def other_kernel(
    shells_ref, where_ref, other_ref, cw_ref, xa_ref, xb_ref, keep_ref, up_ref, down_ref, lhs_ref, q_ref
):
    z = where_ref[1]
    way = where_ref[2]
    first_product(shells_ref, z, -way, other_ref, xa_ref, xb_ref, lhs_ref, q_ref)
    second_product(z, way, cw_ref, q_ref, keep_ref, (up_ref, UP_OTHER), (down_ref, DOWN_OTHER))


def other_both(shells, where, other, cw, *x):
    return pl.pallas_call(
        other_kernel,
        in_specs=[SMEM] * 2 + [VMEM] * 4,
        out_specs=[VMEM] * 3,
        out_shape=[
            jax.ShapeDtypeStruct((768, 128), f32),
            jax.ShapeDtypeStruct((256 * len(UP_OTHER), 128), bf16),
            jax.ShapeDtypeStruct((256 * len(DOWN_OTHER), 128), bf16),
        ],
        scratch_shapes=[pltpu.VMEM((256, 256), bf16), pltpu.VMEM((16 * 1024, 128), bf16)],
        compiler_params=pltpu.CompilerParams(vmem_limit_bytes=24 * 2**20),
        cost_estimate=pl.CostEstimate(flops=2**33, bytes_accessed=2**20, transcendentals=0),
    )(shells, where, other, cw, *(pltpu.with_memory_space_constraint(t, pltpu.VMEM) for t in x))


def first_round(up, down):
    return swap(up, 1), swap(down, -1)


def second_round(keep, up_ds, from_ahead, down_ds, from_behind):
    total = {0: keep[:256], 3: keep[256:512], 5: keep[512:]}
    for ds, got, step in ((up_ds, from_ahead, 1), (down_ds, from_behind, -1)):
        for k, d in enumerate(ds):
            to = (step - d) % 8
            total[to] = total[to] + got[k * 256 : (k + 1) * 256].astype(f32)
    return total[0], swap(total[3].astype(bf16), 3), swap(total[5].astype(bf16), -3)


def reduced(total, from_ahead, from_behind):
    return total + from_ahead.astype(f32) + from_behind.astype(f32)


def split(x):
    high = x.astype(bf16)
    return high, (x - high.astype(f32)).astype(bf16)


def final_kernel(m_ref, lam_ref, sig_ref, o_ref, low_ref, high_ref):
    h = m_ref[...].reshape(512, 128)
    sig = sig_ref[...].astype(bf16)
    zero = jnp.zeros_like(sig)
    pair = jnp.concatenate([jnp.concatenate([sig, zero], axis=1), jnp.concatenate([zero, sig], axis=1)], axis=0)
    pair = jnp.concatenate([pair, pair], axis=0)
    t = jnp.dot(jnp.concatenate(split(h), axis=1), pair, preferred_element_type=f32)
    low_ref[...] = t[:, :128]
    high_ref[...] = t[:, 128:]
    cols = []
    for q in range(16):
        low = low_ref[pl.ds(q, 32, stride=16), :]
        high = high_ref[pl.ds(q, 32, stride=16), :]
        cols.append(jnp.concatenate(split(jnp.concatenate([low, high], axis=0)), axis=0))
    lam = jnp.concatenate([lam_ref[pl.ds(k, 32, stride=2), :] for k in (0, 1)] * 2, axis=0).astype(bf16)
    res = lax.dot_general(lam, jnp.concatenate(cols, axis=1), (((0,), (0,)), ((), ())), preferred_element_type=f32)
    for q in range(16):
        o_ref[q] = res[:, q * 128 : (q + 1) * 128]


def final(m, lam, sig):
    return pl.pallas_call(
        final_kernel,
        out_shape=jax.ShapeDtypeStruct((16, 128, 128), f32),
        scratch_shapes=[pltpu.VMEM((512, 128), f32)] * 2,
        compiler_params=pltpu.CompilerParams(vmem_limit_bytes=24 * 2**20),
        cost_estimate=pl.CostEstimate(flops=2**28, bytes_accessed=2**21, transcendentals=0),
    )(m, lam, sig)


def on_device(integrals, block_shells, live_counts, significance, occ_coef, lam_coef, sig_coef):
    core = lax.axis_index("pairs") % 2
    z = lax.axis_index(COEF)
    where = jnp.stack([core, z, 1 - 2 * ((z + core) % 2)]).astype(jnp.int32)

    own = lax.dynamic_slice_in_dim(occ_coef.T, core * 32, 32, axis=0)
    own = own.reshape(32, 9, 128).transpose(1, 0, 2).reshape(288, 128)
    own = jnp.concatenate([own, lam_coef, sig_coef], axis=0)
    ahead = swap(own, 3)
    behind = swap(own, -3)
    x = integrals.transpose(1, 2, 3, 0)
    ahead, behind, x_first = lax.optimization_barrier((ahead, behind, relayout(where, x, 0)))
    from_ahead = swap(jnp.concatenate([own, ahead, behind[:SPLIT]], axis=0), 1)
    from_behind = swap(jnp.concatenate([own, behind, ahead[SPLIT:]], axis=0), -1)
    from_ahead, from_behind, x_second = lax.optimization_barrier((from_ahead, from_behind, relayout(where, x, 1)))
    near = 2 * BLOCK
    mine = jnp.concatenate(
        [own, behind, ahead, from_ahead[:near], from_behind[:near], from_ahead[near:], from_behind[near:]], axis=0
    )
    other = lax.ppermute(mine, "pairs", [(i, i ^ 1) for i in range(32)])

    shells = block_shells.transpose(0, 2, 1)
    q, lam, sig = own_first(shells, where, mine, x_first, x_second)
    keep, up, down, cw = own_second(shells, live_counts, where, significance, mine, other, q)
    own_got = first_round(up, down)
    keep_other, up, down = other_both(shells, where, other, cw, x_first, x_second)
    other_got = first_round(up, down)
    own_half = second_round(keep, UP_OWN, own_got[0], DOWN_OWN, own_got[1])
    other_half = second_round(keep_other, UP_OTHER, other_got[0], DOWN_OTHER, other_got[1])
    a = reduced(*own_half)
    b = reduced(*other_half)
    summed = jnp.concatenate([jnp.where(core == 0, a, b), jnp.where(core == 0, b, a)], axis=0)
    moved = lax.all_to_all(summed.reshape(32, 16, 128), "pairs", 0, 0, tiled=True)

    return final(moved, lam, sig)


def solution(mesh):
    fine = Mesh(mesh.devices.reshape(32, 2, 4), ("pairs",) + COEF)
    placed = (
        P("pairs", COEF, None, None),
        P("pairs", COEF, None),
        P("pairs", COEF),
        P(),
        P(COEF, None),
        P(COEF, None),
        P(COEF, None),
    )
    return jax.shard_map(
        on_device,
        mesh=fine,
        in_specs=placed,
        out_specs=P(("pairs",) + COEF, None, None),
        check_vma=False,
    )
```

time: 75.4 us -> 71.8 us (0.952)
  starting transfers between devices: 26.7 us -> 23.1 us
  waiting for transfers between devices: 8.81 us -> 10.3 us
  Pallas kernels: 18 us -> 16.8 us
    ppermute x12, starting transfers between devices: 24.8 us -> 20.6 us  [swap(): return lax.ppermute(x, ('pairs',) + COEF, pairs)]
    ppermute x12, waiting for transfers between devices: 8.81 us -> 10.3 us  [swap(): return lax.ppermute(x, ('pairs',) + COEF, pairs)]
    pallas_call x1, Pallas kernels: 3.19 us -> 2.02 us  [own_first(): pl.pallas_call(own_kernel, in_specs=[SMEM] * 2 + [VMEM] * 3, out_specs=[V...]
  transfers between devices with their start and end apart: 13 -> 13, of which waited for: 4 -> 6; matrix products, arithmetic and copies ran while one was open for 0% -> 0% of each run, Pallas kernels for 20% -> 18%
where the time goes in v6:
time: 71.8 us; the launch traced here: 71.5 us
  starting transfers between devices  23.1 us (32%)
  blocking collectives  18.3 us (25%)
  Pallas kernels  16.8 us (23%)
  waiting for transfers between devices  10.3 us (14%)
  local copies, waits for them, and re-layouts  1.18 us (2%)
  other arithmetic  0.96 us (1%)
  between operations  0.86 us (1%)
    ppermute x12, starting transfers between devices, swap(): return lax.ppermute(x, ('pairs',) + COEF, pairs)  20.6 us
    all_to_all x1, blocking collectives, on_device(): lax.all_to_all(summed.reshape(32, 16, 128), 'pairs', 0, 0, tiled=True)  18.3 us
    ppermute x12, waiting for transfers between devices, swap(): return lax.ppermute(x, ('pairs',) + COEF, pairs)  10.3 us
    pallas_call x2, Pallas kernels, relayout(): pl.pallas_call(relayout_kernel, grid=(4,), in_specs=[pl.BlockSpec(memory_...  7.81 us
    pallas_call x1, Pallas kernels, other_both(): pl.pallas_call(other_kernel, in_specs=[SMEM] * 2 + [VMEM] * 4, out_specs=...  3.11 us
    ppermute x1, starting transfers between devices, on_device(): other = lax.ppermute(mine, 'pairs', [(i, i ^ 1) for i in range(32)])  2.49 us
    pallas_call x1, Pallas kernels, own_second(): pl.pallas_call(columns_kernel, in_specs=[SMEM] * 3 + [VMEM] * 4, out_spec...  2.18 us
    pallas_call x1, Pallas kernels, own_first(): pl.pallas_call(own_kernel, in_specs=[SMEM] * 2 + [VMEM] * 3, out_specs=[V...  2.02 us
  transfers between devices with their start and end apart: 13, of which 6 were waited for; matrix products, arithmetic and copies ran while one was open for 0% of the time, Pallas kernels for 18%

profile of v6, /device:TPU:1, one launch (start us, length us, event | category | flops | bytes accessed | tf_op | source)
XLA Modules:
  0.0 71.5 jit_solution(637260923796366699)
XLA Ops:
  0.0 0.0 copy-start
  0.0 0.9 %copy-done = bf16[1152,64]{0,1:T(8,128)(2,1)S(1)} copy-done((bf16[1152,64]{0,1:T(8,128)(2,1)S(1)}, bf16[1152,64]{0,1:T(8,128)(2,1)}, u32[]{:S(2)}) %copy-start) | copy-done | bytes 147480
  1.0 0.7 pad_maximum_fusion.1
  1.7 5.2 %collective-permute-start.1 = (bf16[304,128]{1,0:T(8,128)(2,1)S(1)}, bf16[304,128]{1,0:T(8,128)(2,1)S(1)}, u32[]{:S(2)}, u32[]{:S(2)}) collective-permute-start(bf16[304,128]{1,0:T(8,128)(2,1)S(1)} %pad_maximum_fusion.1), channel_id=1, source_target_pairs={{0,5},{1,4},{2,7},{3,6},{4,1},{5,0},{6,3},{7,2},{8,11},{9,14},{10,... | collective-permute-start | bytes 233480 | tf_op jit(solution)/shard_map/ppermute | solution.py:24
  6.9 2.2 %collective-permute-start = (bf16[304,128]{1,0:T(8,128)(2,1)S(1)}, bf16[304,128]{1,0:T(8,128)(2,1)S(1)}, u32[]{:S(2)}, u32[]{:S(2)}) collective-permute-start(bf16[304,128]{1,0:T(8,128)(2,1)S(1)} %pad_maximum_fusion.1), channel_id=1, source_target_pairs={{0,3},{1,6},{2,5},{3,0},{4,7},{5,2},{6,1},{7,4},{8,13},{9,12},{10,... | collective-permute-start | bytes 233480 | tf_op jit(solution)/shard_map/ppermute | solution.py:24
  9.1 0.1 pad_add_fusion.where_ref
  9.2 0.0 copy-start.3
  9.2 0.0 copy-start.4
  9.2 3.9 %shard_map.73.xa_ref = bf16[64,256,128]{2,1,0:T(8,128)(2,1)S(1)} custom-call(s32[3]{0:T(128)S(1)} %pad_add_fusion.where_ref, bf16[8,64,64,128]{3,2,1,0:T(8,128)(2,1)} %bitcast.13), custom_call_target="tpu_custom_call" | custom-call | bytes 8388608 | tf_op jit(solution)/shard_map/pallas_call | solution.py:34
  13.1 0.0 copy-done.3
  13.2 0.0 copy-done.4
  13.2 0.0 collective-permute-done.1
  13.2 1.6 %collective-permute-done = bf16[304,128]{1,0:T(8,128)(2,1)S(1)} collective-permute-done((bf16[304,128]{1,0:T(8,128)(2,1)S(1)}, bf16[304,128]{1,0:T(8,128)(2,1)S(1)}, u32[]{:S(2)}, u32[]{:S(2)}) %collective-permute-start) | collective-permute-done | bytes 77856 | tf_op jit(solution)/shard_map/ppermute | solution.py:24
  14.9 2.0 %collective-permute-start.2 = (bf16[768,128]{1,0:T(8,128)(2,1)S(1)}, bf16[768,128]{1,0:T(8,128)(2,1)S(1)}, u32[]{:S(2)}, u32[]{:S(2)}) collective-permute-start(bf16[768,128]{1,0:T(8,128)(2,1)S(1)} %constant_dynamic-update-slice_fusion), channel_id=1, source_target_pairs={{0,1},{1,0},{2,3},{3,2},{4,5},{5,4},{6,7},{7,6},{8,15},{9,10},{10,... | collective-permute-start | bytes 589832 | tf_op jit(solution)/shard_map/ppermute | solution.py:24
  16.9 0.0 copy-start.2
  16.9 0.5 collective-permute-start.3
  17.4 3.9 %shard_map.74.xb_ref = bf16[64,256,128]{2,1,0:T(8,128)(2,1)S(1)} custom-call(s32[3]{0:T(128)S(1)} %pad_add_fusion.where_ref, bf16[8,64,64,128]{3,2,1,0:T(8,128)(2,1)} %bitcast.14), custom_call_target="tpu_custom_call" | custom-call | bytes 8388608 | tf_op jit(solution)/shard_map/pallas_call | solution.py:34
  21.3 2.0 %collective-permute-done.3 = bf16[752,128]{1,0:T(8,128)(2,1)S(1)} collective-permute-done((bf16[752,128]{1,0:T(8,128)(2,1)S(1)}, bf16[752,128]{1,0:T(8,128)(2,1)S(1)}, u32[]{:S(2)}, u32[]{:S(2)}) %collective-permute-start.3) | collective-permute-done | bytes 192544 | tf_op jit(solution)/shard_map/ppermute | solution.py:24
  23.3 0.0 collective-permute-done.2
  23.4 2.5 %collective-permute-start.4 = (bf16[2432,128]{1,0:T(8,128)(2,1)S(1)}, bf16[2432,128]{1,0:T(8,128)(2,1)S(1)}, u32[]{:S(2)}, u32[]{:S(2)}) collective-permute-start(bf16[2432,128]{1,0:T(8,128)(2,1)S(1)} %constant_dynamic-update-slice_fusion.10.mine_ref), channel_id=1, source_target_pairs={{0,8},{8,0},{16,24},{24,16},{32,40},{40,32},{48,56},{56,48},{64,72... | collective-permute-start | bytes 1867784 | tf_op jit(solution)/shard_map/ppermute | solution.py:292
  26.5 0.0 copy-done.2
  26.5 0.0 copy-start.1
  26.5 2.0 %shard_map.75 = (bf16[16384,128]{1,0:T(8,128)(2,1)S(1)}, f32[64,128]{1,0:T(8,128)S(1)}, f32[64,128]{1,0:T(8,128)S(1)}) custom-call(s32[1,2,8]{2,1,0:T(2,128)S(1)} %bitcast.10, s32[3]{0:T(128)S(1)} %pad_add_fusion.where_ref, bf16[2432,128]{1,0:T(8,128)(2,1)S(1)} %constant_dynamic-update-slice_fusion.10.mine_ref, bf16[64,256,128]{2,1,0:T(8,128)(2,1)S(1)} %shard_map.73.xa_ref, ...), custom_call_target="tpu_custom_call" | custom-call | flops 4294967296 | bytes 1048576 | tf_op jit(solution)/shard_map/pallas_call | solution.py:127
  28.6 0.0 collective-permute-done.4.other_ref
  28.6 0.0 copy-done.1
  28.6 2.2 %shard_map.76 = (f32[768,128]{1,0:T(8,128)S(1)}, bf16[768,128]{1,0:T(8,128)(2,1)S(1)}, bf16[512,128]{1,0:T(8,128)(2,1)S(1)}, bf16[256,2048]{1,0:T(8,128)(2,1)S(1)}) custom-call(s32[1,2,8]{2,1,0:T(2,128)S(1)} %bitcast.11, s32[1,1]{1,0:T(1,128)S(6)} %copy.26.count_ref, s32[3]{0:T(128)S(1)} %pad_add_fusion.where_ref, s32[144,144]{1,0:T(8,128)S(1)} %copy-done.1, ...), custom_call_target="tpu_custom_call" | custom-call | flops 2147483648 | bytes 1048576 | tf_op jit(solution)/shard_map/pallas_call | solution.py:181
  30.8 0.1 collective-permute-start.6
  30.9 1.8 %collective-permute-start.5 = (bf16[768,128]{1,0:T(8,128)(2,1)S(1)}, bf16[768,128]{1,0:T(8,128)(2,1)S(1)}, u32[]{:S(2)}, u32[]{:S(2)}) collective-permute-start(bf16[768,128]{1,0:T(8,128)(2,1)S(1)} %get-tuple-element.29), channel_id=1, source_target_pairs={{0,1},{1,0},{2,3},{3,2},{4,5},{5,4},{6,7},{7,6},{8,15},{9,10},{10,... | collective-permute-start | bytes 589832 | tf_op jit(solution)/shard_map/ppermute | solution.py:24
  32.7 3.1 %shard_map.77 = (f32[768,128]{1,0:T(8,128)S(1)}, bf16[768,128]{1,0:T(8,128)(2,1)S(1)}, bf16[512,128]{1,0:T(8,128)(2,1)S(1)}) custom-call(s32[1,2,8]{2,1,0:T(2,128)S(1)} %bitcast.12, s32[3]{0:T(128)S(1)} %pad_add_fusion.where_ref, bf16[2432,128]{1,0:T(8,128)(2,1)S(1)} %collective-permute-done.4.other_ref, bf16[256,2048]{1,0:T(8,128)(2,1)S(1)} %get-tuple-element.31.cw_ref, ...), custom_call_target="tpu_custom_call" | custom-call | flops 8589934592 | bytes 1048576 | tf_op jit(solution)/shard_map/pallas_call | solution.py:206
  35.9 0.4 collective-permute-start.10
  36.3 1.7 %collective-permute-start.9 = (bf16[768,128]{1,0:T(8,128)(2,1)S(1)}, bf16[768,128]{1,0:T(8,128)(2,1)S(1)}, u32[]{:S(2)}, u32[]{:S(2)}) collective-permute-start(bf16[768,128]{1,0:T(8,128)(2,1)S(1)} %get-tuple-element.33), channel_id=1, source_target_pairs={{0,1},{1,0},{2,3},{3,2},{4,5},{5,4},{6,7},{7,6},{8,15},{9,10},{10,... | collective-permute-start | bytes 589832 | tf_op jit(solution)/shard_map/ppermute | solution.py:24
  38.0 0.0 collective-permute-done.6
  38.0 0.1 collective-permute-done.5
  38.1 1.2 %collective-permute-start.7 = (bf16[256,128]{1,0:T(8,128)(2,1)S(1)}, bf16[256,128]{1,0:T(8,128)(2,1)S(1)}, u32[]{:S(2)}, u32[]{:S(2)}) collective-permute-start(bf16[256,128]{1,0:T(8,128)(2,1)S(1)} %get-tuple-element.41), channel_id=1, source_target_pairs={{0,3},{1,6},{2,5},{3,0},{4,7},{5,2},{6,1},{7,4},{8,13},{9,12},{10,... | collective-permute-start | bytes 196616 | tf_op jit(solution)/shard_map/ppermute | solution.py:24
  39.4 1.6 %collective-permute-start.8 = (bf16[256,128]{1,0:T(8,128)(2,1)S(1)}, bf16[256,128]{1,0:T(8,128)(2,1)S(1)}, u32[]{:S(2)}, u32[]{:S(2)}) collective-permute-start(bf16[256,128]{1,0:T(8,128)(2,1)S(1)} %get-tuple-element.42), channel_id=1, source_target_pairs={{0,5},{1,4},{2,7},{3,6},{4,1},{5,0},{6,3},{7,2},{8,11},{9,14},{10,... | collective-permute-start | bytes 196616 | tf_op jit(solution)/shard_map/ppermute | solution.py:24
  41.0 0.0 collective-permute-done.10
  41.0 2.4 %collective-permute-done.9 = bf16[768,128]{1,0:T(8,128)(2,1)S(1)} collective-permute-done((bf16[768,128]{1,0:T(8,128)(2,1)S(1)}, bf16[768,128]{1,0:T(8,128)(2,1)S(1)}, u32[]{:S(2)}, u32[]{:S(2)}) %collective-permute-start.9) | collective-permute-done | bytes 196640 | tf_op jit(solution)/shard_map/ppermute | solution.py:24
  43.5 2.0 %collective-permute-start.11 = (bf16[256,128]{1,0:T(8,128)(2,1)S(1)}, bf16[256,128]{1,0:T(8,128)(2,1)S(1)}, u32[]{:S(2)}, u32[]{:S(2)}) collective-permute-start(bf16[256,128]{1,0:T(8,128)(2,1)S(1)} %get-tuple-element.39), channel_id=1, source_target_pairs={{0,3},{1,6},{2,5},{3,0},{4,7},{5,2},{6,1},{7,4},{8,13},{9,12},{10,... | collective-permute-start | bytes 196616 | tf_op jit(solution)/shard_map/ppermute | solution.py:24
  45.5 1.6 %collective-permute-start.12 = (bf16[256,128]{1,0:T(8,128)(2,1)S(1)}, bf16[256,128]{1,0:T(8,128)(2,1)S(1)}, u32[]{:S(2)}, u32[]{:S(2)}) collective-permute-start(bf16[256,128]{1,0:T(8,128)(2,1)S(1)} %get-tuple-element.40), channel_id=1, source_target_pairs={{0,5},{1,4},{2,7},{3,6},{4,1},{5,0},{6,3},{7,2},{8,11},{9,14},{10,... | collective-permute-start | bytes 196616 | tf_op jit(solution)/shard_map/ppermute | solution.py:24
  47.1 0.0 collective-permute-done.7
  47.1 0.0 collective-permute-done.8
  47.1 3.5 %collective-permute-done.11 = bf16[256,128]{1,0:T(8,128)(2,1)S(1)} collective-permute-done((bf16[256,128]{1,0:T(8,128)(2,1)S(1)}, bf16[256,128]{1,0:T(8,128)(2,1)S(1)}, u32[]{:S(2)}, u32[]{:S(2)}) %collective-permute-start.11) | collective-permute-done | bytes 65568 | tf_op jit(solution)/shard_map/ppermute | solution.py:24
  50.6 0.8 %collective-permute-done.12 = bf16[256,128]{1,0:T(8,128)(2,1)S(1)} collective-permute-done((bf16[256,128]{1,0:T(8,128)(2,1)S(1)}, bf16[256,128]{1,0:T(8,128)(2,1)S(1)}, u32[]{:S(2)}, u32[]{:S(2)}) %collective-permute-start.12) | collective-permute-done | bytes 65568 | tf_op jit(solution)/shard_map/ppermute | solution.py:24
  51.4 0.1 broadcast_select_fusion.1
  51.5 18.3 %all_to_all.5.m_ref = f32[32,16,128]{2,1,0:T(8,128)S(1)} all-to-all(f32[32,16,128]{2,1,0:T(8,128)S(1)} %bitcast.15), channel_id=1, replica_groups=mesh['pairs'=32,'zh'=2,'zl'=4] {'pairs'}, dimensions={0} | all-to-all | bytes 524288 | tf_op jit(solution)/shard_map/all_to_all | solution.py:305
  69.9 1.6 %shard_map.78 = f32[16,128,128]{2,1,0:T(8,128)} custom-call(f32[32,16,128]{2,1,0:T(8,128)S(1)} %all_to_all.5.m_ref, f32[64,128]{1,0:T(8,128)S(1)} %get-tuple-element.35.lam_ref, f32[64,128]{1,0:T(8,128)S(1)} %get-tuple-element.36.sig_ref), custom_call_target="tpu_custom_call" | custom-call | flops 268435456 | bytes 2097152 | tf_op jit(solution)/shard_map/pallas_call | solution.py:264
  (17 shorter events, 0.4 us)
Async XLA Ops:
  0.0 0.9 %copy-start = (bf16[1152,64]{0,1:T(8,128)(2,1)S(1)}, bf16[1152,64]{0,1:T(8,128)(2,1)}, u32[]{:S(2)}) copy-start(bf16[1152,64]{0,1:T(8,128)(2,1)} %param.11) | copy-start | bytes 442372
  1.7 11.5 %collective-permute-start.1 = (bf16[304,128]{1,0:T(8,128)(2,1)S(1)}, bf16[304,128]{1,0:T(8,128)(2,1)S(1)}, u32[]{:S(2)}, u32[]{:S(2)}) collective-permute-start(bf16[304,128]{1,0:T(8,128)(2,1)S(1)} %pad_maximum_fusion.1), channel_id=1, source_target_pairs={{0,5},{1,4},{2,7},{3,6},{4,1},{5,0},{6,3},{7,2},{8,11},{9,14},{10,... | collective-permute-start | bytes 233480 | tf_op jit(solution)/shard_map/ppermute | solution.py:24
  6.9 7.9 %collective-permute-start = (bf16[304,128]{1,0:T(8,128)(2,1)S(1)}, bf16[304,128]{1,0:T(8,128)(2,1)S(1)}, u32[]{:S(2)}, u32[]{:S(2)}) collective-permute-start(bf16[304,128]{1,0:T(8,128)(2,1)S(1)} %pad_maximum_fusion.1), channel_id=1, source_target_pairs={{0,3},{1,6},{2,5},{3,0},{4,7},{5,2},{6,1},{7,4},{8,13},{9,12},{10,... | collective-permute-start | bytes 233480 | tf_op jit(solution)/shard_map/ppermute | solution.py:24
  9.2 3.9 %copy-start.3 = (bf16[8,128]{1,0:T(8,128)(2,1)S(1)}, bf16[8,128]{1,0:T(8,128)(2,1)}, u32[]{:S(2)}) copy-start(bf16[8,128]{1,0:T(8,128)(2,1)} %param.12) | copy-start | bytes 6148
  9.2 4.0 %copy-start.4 = (bf16[8,128]{1,0:T(8,128)(2,1)S(1)}, bf16[8,128]{1,0:T(8,128)(2,1)}, u32[]{:S(2)}) copy-start(bf16[8,128]{1,0:T(8,128)(2,1)} %param.13) | copy-start | bytes 6148
  14.9 8.4 %collective-permute-start.2 = (bf16[768,128]{1,0:T(8,128)(2,1)S(1)}, bf16[768,128]{1,0:T(8,128)(2,1)S(1)}, u32[]{:S(2)}, u32[]{:S(2)}) collective-permute-start(bf16[768,128]{1,0:T(8,128)(2,1)S(1)} %constant_dynamic-update-slice_fusion), channel_id=1, source_target_pairs={{0,1},{1,0},{2,3},{3,2},{4,5},{5,4},{6,7},{7,6},{8,15},{9,10},{10,... | collective-permute-start | bytes 589832 | tf_op jit(solution)/shard_map/ppermute | solution.py:24
  16.9 9.6 %copy-start.2 = (s32[1,8,2]{1,2,0:T(2,128)S(1)}, s32[1,8,2]{1,2,0:T(2,128)}, u32[]{:S(2)}) copy-start(s32[1,8,2]{1,2,0:T(2,128)} %param.8) | copy-start | bytes 196
  16.9 6.4 %collective-permute-start.3 = (bf16[752,128]{1,0:T(8,128)(2,1)S(1)}, bf16[752,128]{1,0:T(8,128)(2,1)S(1)}, u32[]{:S(2)}, u32[]{:S(2)}) collective-permute-start(bf16[752,128]{1,0:T(8,128)(2,1)S(1)} %constant_dynamic-update-slice_fusion.5), channel_id=1, source_target_pairs={{0,7},{1,2},{2,1},{3,4},{4,3},{5,6},{6,5},{7,0},{8,9},{9,8},{10,11... | collective-permute-start | bytes 577544 | tf_op jit(solution)/shard_map/ppermute | solution.py:24
  23.4 5.2 %collective-permute-start.4 = (bf16[2432,128]{1,0:T(8,128)(2,1)S(1)}, bf16[2432,128]{1,0:T(8,128)(2,1)S(1)}, u32[]{:S(2)}, u32[]{:S(2)}) collective-permute-start(bf16[2432,128]{1,0:T(8,128)(2,1)S(1)} %constant_dynamic-update-slice_fusion.10.mine_ref), channel_id=1, source_target_pairs={{0,8},{8,0},{16,24},{24,16},{32,40},{40,32},{48,56},{56,48},{64,72... | collective-permute-start | bytes 1867784 | tf_op jit(solution)/shard_map/ppermute | solution.py:292
  26.5 2.1 %copy-start.1 = (s32[144,144]{1,0:T(8,128)S(1)}, s32[144,144]{1,0:T(8,128)}, u32[]{:S(2)}) copy-start(s32[144,144]{1,0:T(8,128)} %screen_ref.1) | copy-start | bytes 248836
  30.8 7.3 %collective-permute-start.6 = (bf16[512,128]{1,0:T(8,128)(2,1)S(1)}, bf16[512,128]{1,0:T(8,128)(2,1)S(1)}, u32[]{:S(2)}, u32[]{:S(2)}) collective-permute-start(bf16[512,128]{1,0:T(8,128)(2,1)S(1)} %get-tuple-element.30), channel_id=1, source_target_pairs={{0,7},{1,2},{2,1},{3,4},{4,3},{5,6},{6,5},{7,0},{8,9},{9,8},{10,11... | collective-permute-start | bytes 393224 | tf_op jit(solution)/shard_map/ppermute | solution.py:24
  30.9 7.2 %collective-permute-start.5 = (bf16[768,128]{1,0:T(8,128)(2,1)S(1)}, bf16[768,128]{1,0:T(8,128)(2,1)S(1)}, u32[]{:S(2)}, u32[]{:S(2)}) collective-permute-start(bf16[768,128]{1,0:T(8,128)(2,1)S(1)} %get-tuple-element.29), channel_id=1, source_target_pairs={{0,1},{1,0},{2,3},{3,2},{4,5},{5,4},{6,7},{7,6},{8,15},{9,10},{10,... | collective-permute-start | bytes 589832 | tf_op jit(solution)/shard_map/ppermute | solution.py:24
  35.9 5.2 %collective-permute-start.10 = (bf16[512,128]{1,0:T(8,128)(2,1)S(1)}, bf16[512,128]{1,0:T(8,128)(2,1)S(1)}, u32[]{:S(2)}, u32[]{:S(2)}) collective-permute-start(bf16[512,128]{1,0:T(8,128)(2,1)S(1)} %get-tuple-element.34), channel_id=1, source_target_pairs={{0,7},{1,2},{2,1},{3,4},{4,3},{5,6},{6,5},{7,0},{8,9},{9,8},{10,11... | collective-permute-start | bytes 393224 | tf_op jit(solution)/shard_map/ppermute | solution.py:24
  36.3 7.1 %collective-permute-start.9 = (bf16[768,128]{1,0:T(8,128)(2,1)S(1)}, bf16[768,128]{1,0:T(8,128)(2,1)S(1)}, u32[]{:S(2)}, u32[]{:S(2)}) collective-permute-start(bf16[768,128]{1,0:T(8,128)(2,1)S(1)} %get-tuple-element.33), channel_id=1, source_target_pairs={{0,1},{1,0},{2,3},{3,2},{4,5},{5,4},{6,7},{7,6},{8,15},{9,10},{10,... | collective-permute-start | bytes 589832 | tf_op jit(solution)/shard_map/ppermute | solution.py:24
  38.1 9.0 %collective-permute-start.7 = (bf16[256,128]{1,0:T(8,128)(2,1)S(1)}, bf16[256,128]{1,0:T(8,128)(2,1)S(1)}, u32[]{:S(2)}, u32[]{:S(2)}) collective-permute-start(bf16[256,128]{1,0:T(8,128)(2,1)S(1)} %get-tuple-element.41), channel_id=1, source_target_pairs={{0,3},{1,6},{2,5},{3,0},{4,7},{5,2},{6,1},{7,4},{8,13},{9,12},{10,... | collective-permute-start | bytes 196616 | tf_op jit(solution)/shard_map/ppermute | solution.py:24
  39.4 7.8 %collective-permute-start.8 = (bf16[256,128]{1,0:T(8,128)(2,1)S(1)}, bf16[256,128]{1,0:T(8,128)(2,1)S(1)}, u32[]{:S(2)}, u32[]{:S(2)}) collective-permute-start(bf16[256,128]{1,0:T(8,128)(2,1)S(1)} %get-tuple-element.42), channel_id=1, source_target_pairs={{0,5},{1,4},{2,7},{3,6},{4,1},{5,0},{6,3},{7,2},{8,11},{9,14},{10,... | collective-permute-start | bytes 196616 | tf_op jit(solution)/shard_map/ppermute | solution.py:24
  43.5 7.1 %collective-permute-start.11 = (bf16[256,128]{1,0:T(8,128)(2,1)S(1)}, bf16[256,128]{1,0:T(8,128)(2,1)S(1)}, u32[]{:S(2)}, u32[]{:S(2)}) collective-permute-start(bf16[256,128]{1,0:T(8,128)(2,1)S(1)} %get-tuple-element.39), channel_id=1, source_target_pairs={{0,3},{1,6},{2,5},{3,0},{4,7},{5,2},{6,1},{7,4},{8,13},{9,12},{10,... | collective-permute-start | bytes 196616 | tf_op jit(solution)/shard_map/ppermute | solution.py:24
  45.5 5.9 %collective-permute-start.12 = (bf16[256,128]{1,0:T(8,128)(2,1)S(1)}, bf16[256,128]{1,0:T(8,128)(2,1)S(1)}, u32[]{:S(2)}, u32[]{:S(2)}) collective-permute-start(bf16[256,128]{1,0:T(8,128)(2,1)S(1)} %get-tuple-element.40), channel_id=1, source_target_pairs={{0,5},{1,4},{2,7},{3,6},{4,1},{5,0},{6,3},{7,2},{8,11},{9,14},{10,... | collective-permute-start | bytes 196616 | tf_op jit(solution)/shard_map/ppermute | solution.py:24

commit v7 on v6

--- a/solution.py
+++ b/solution.py
@@ -10,7 +10,7 @@
 bf16 = jnp.bfloat16
 COEF = ("zh", "zl")
 BLOCK = 304
-SPLIT = 160
+SPLIT = 304
 PLACES = 0x54172630
 ORDER = (0, 5, 3, 1, 6, 7, 2, 4)
 

time: 71.8 us -> 71.8 us (level)
  waiting for transfers between devices: 10.3 us -> 9.48 us
    ppermute x12, waiting for transfers between devices: 10.3 us -> 9.48 us  [swap(): return lax.ppermute(x, ('pairs',) + COEF, pairs)]
    ppermute x1, starting transfers between devices: 2.49 us -> 1.72 us  [on_device(): other = lax.ppermute(mine, 'pairs', [(i, i ^ 1) for i in range(32)])]
    ppermute x12, starting transfers between devices: 20.6 us -> 21.3 us  [swap(): return lax.ppermute(x, ('pairs',) + COEF, pairs)]
    unnamed x18 -> x17, local copies, waits for them, and re-layouts: 1.08 us -> 1.71 us
  transfers between devices with their start and end apart: 13 -> 13, of which waited for: 6 -> 6; matrix products, arithmetic and copies ran while one was open for 0% -> 1% of each run, Pallas kernels for 18% -> 18%
where the time goes in v7:
time: 71.8 us; the launch traced here: 71.5 us
  starting transfers between devices  23.1 us (32%)
  blocking collectives  18.5 us (26%)
  Pallas kernels  16.8 us (23%)
  waiting for transfers between devices  9.48 us (13%)
  local copies, waits for them, and re-layouts  1.83 us (3%)
  other arithmetic  0.97 us (1%)
  between operations  0.86 us (1%)
    ppermute x12, starting transfers between devices, swap(): return lax.ppermute(x, ('pairs',) + COEF, pairs)  21.3 us
    all_to_all x1, blocking collectives, on_device(): lax.all_to_all(summed.reshape(32, 16, 128), 'pairs', 0, 0, tiled=True)  18.5 us
    ppermute x12, waiting for transfers between devices, swap(): return lax.ppermute(x, ('pairs',) + COEF, pairs)  9.48 us
    pallas_call x2, Pallas kernels, relayout(): pl.pallas_call(relayout_kernel, grid=(4,), in_specs=[pl.BlockSpec(memory_...  7.82 us
    pallas_call x1, Pallas kernels, other_both(): pl.pallas_call(other_kernel, in_specs=[SMEM] * 2 + [VMEM] * 4, out_specs=...  3.12 us
    pallas_call x1, Pallas kernels, own_second(): pl.pallas_call(columns_kernel, in_specs=[SMEM] * 3 + [VMEM] * 4, out_spec...  2.18 us
    pallas_call x1, Pallas kernels, own_first(): pl.pallas_call(own_kernel, in_specs=[SMEM] * 2 + [VMEM] * 3, out_specs=[V...  2.03 us
    ppermute x1, starting transfers between devices, on_device(): other = lax.ppermute(mine, 'pairs', [(i, i ^ 1) for i in range(32)])  1.72 us
  transfers between devices with their start and end apart: 13, of which 6 were waited for; matrix products, arithmetic and copies ran while one was open for 1% of the time, Pallas kernels for 18%

profile of v7, /device:TPU:1, one launch (start us, length us, event | category | flops | bytes accessed | tf_op | source)
XLA Modules:
  0.0 71.5 jit_solution(1639568045888817297)
XLA Ops:
  0.0 0.0 copy-start
  0.0 0.9 %copy-done = bf16[1152,64]{0,1:T(8,128)(2,1)S(1)} copy-done((bf16[1152,64]{0,1:T(8,128)(2,1)S(1)}, bf16[1152,64]{0,1:T(8,128)(2,1)}, u32[]{:S(2)}) %copy-start) | copy-done | bytes 147480
  1.0 0.7 pad_maximum_fusion.2
  1.7 5.2 %collective-permute-start.1 = (bf16[304,128]{1,0:T(8,128)(2,1)S(1)}, bf16[304,128]{1,0:T(8,128)(2,1)S(1)}, u32[]{:S(2)}, u32[]{:S(2)}) collective-permute-start(bf16[304,128]{1,0:T(8,128)(2,1)S(1)} %pad_maximum_fusion.2), channel_id=1, source_target_pairs={{0,5},{1,4},{2,7},{3,6},{4,1},{5,0},{6,3},{7,2},{8,11},{9,14},{10,... | collective-permute-start | bytes 233480 | tf_op jit(solution)/shard_map/ppermute | solution.py:24
  6.9 2.2 %collective-permute-start = (bf16[304,128]{1,0:T(8,128)(2,1)S(1)}, bf16[304,128]{1,0:T(8,128)(2,1)S(1)}, u32[]{:S(2)}, u32[]{:S(2)}) collective-permute-start(bf16[304,128]{1,0:T(8,128)(2,1)S(1)} %pad_maximum_fusion.2), channel_id=1, source_target_pairs={{0,3},{1,6},{2,5},{3,0},{4,7},{5,2},{6,1},{7,4},{8,13},{9,12},{10,... | collective-permute-start | bytes 233480 | tf_op jit(solution)/shard_map/ppermute | solution.py:24
  9.1 0.7 constant_dynamic-update-slice_fusion.3
  9.8 0.1 pad_add_fusion.where_ref
  9.9 0.0 copy-start.4
  9.9 0.0 copy-start.3
  9.9 3.9 %shard_map.73.xa_ref = bf16[64,256,128]{2,1,0:T(8,128)(2,1)S(1)} custom-call(s32[3]{0:T(128)S(1)} %pad_add_fusion.where_ref, bf16[8,64,64,128]{3,2,1,0:T(8,128)(2,1)} %bitcast.13), custom_call_target="tpu_custom_call" | custom-call | bytes 8388608 | tf_op jit(solution)/shard_map/pallas_call | solution.py:34
  13.8 0.0 copy-done.4
  13.8 0.0 collective-permute-done.1
  13.9 0.9 %collective-permute-done = bf16[304,128]{1,0:T(8,128)(2,1)S(1)} collective-permute-done((bf16[304,128]{1,0:T(8,128)(2,1)S(1)}, bf16[304,128]{1,0:T(8,128)(2,1)S(1)}, u32[]{:S(2)}, u32[]{:S(2)}) %collective-permute-start) | collective-permute-done | bytes 77856 | tf_op jit(solution)/shard_map/ppermute | solution.py:24
  14.8 2.6 %collective-permute-start.2 = (bf16[912,128]{1,0:T(8,128)(2,1)S(1)}, bf16[912,128]{1,0:T(8,128)(2,1)S(1)}, u32[]{:S(2)}, u32[]{:S(2)}) collective-permute-start(bf16[912,128]{1,0:T(8,128)(2,1)S(1)} %get-tuple-element.43), channel_id=1, source_target_pairs={{0,1},{1,0},{2,3},{3,2},{4,5},{5,4},{6,7},{7,6},{8,15},{9,10},{10,... | collective-permute-start | bytes 700424 | tf_op jit(solution)/shard_map/ppermute | solution.py:24
  17.5 0.0 copy-done.3
  17.5 0.0 copy-start.2
  17.5 0.1 collective-permute-start.3
  17.6 3.9 %shard_map.74.xb_ref = bf16[64,256,128]{2,1,0:T(8,128)(2,1)S(1)} custom-call(s32[3]{0:T(128)S(1)} %pad_add_fusion.where_ref, bf16[8,64,64,128]{3,2,1,0:T(8,128)(2,1)} %bitcast.14), custom_call_target="tpu_custom_call" | custom-call | bytes 8388608 | tf_op jit(solution)/shard_map/pallas_call | solution.py:34
  21.5 2.1 %collective-permute-done.3 = bf16[608,128]{1,0:T(8,128)(2,1)S(1)} collective-permute-done((bf16[608,128]{1,0:T(8,128)(2,1)S(1)}, bf16[608,128]{1,0:T(8,128)(2,1)S(1)}, u32[]{:S(2)}, u32[]{:S(2)}) %collective-permute-start.3) | collective-permute-done | bytes 155680 | tf_op jit(solution)/shard_map/ppermute | solution.py:24
  23.6 0.0 collective-permute-done.2
  23.7 1.7 %collective-permute-start.4 = (bf16[2432,128]{1,0:T(8,128)(2,1)S(1)}, bf16[2432,128]{1,0:T(8,128)(2,1)S(1)}, u32[]{:S(2)}, u32[]{:S(2)}) collective-permute-start(bf16[2432,128]{1,0:T(8,128)(2,1)S(1)} %slice_dynamic-update-slice_fusion.1.mine_ref), channel_id=1, source_target_pairs={{0,8},{8,0},{16,24},{24,16},{32,40},{40,32},{48,56},{56,48},{64,72... | collective-permute-start | bytes 1867784 | tf_op jit(solution)/shard_map/ppermute | solution.py:292
  26.1 0.0 copy-done.2
  26.1 0.0 copy-start.1
  26.1 2.0 %shard_map.75 = (bf16[16384,128]{1,0:T(8,128)(2,1)S(1)}, f32[64,128]{1,0:T(8,128)S(1)}, f32[64,128]{1,0:T(8,128)S(1)}) custom-call(s32[1,2,8]{2,1,0:T(2,128)S(1)} %bitcast.10, s32[3]{0:T(128)S(1)} %pad_add_fusion.where_ref, bf16[2432,128]{1,0:T(8,128)(2,1)S(1)} %slice_dynamic-update-slice_fusion.1.mine_ref, bf16[64,256,128]{2,1,0:T(8,128)(2,1)S(1)} %shard_map.73.xa_ref, ...), custom_call_target="tpu_custom_call" | custom-call | flops 4294967296 | bytes 1048576 | tf_op jit(solution)/shard_map/pallas_call | solution.py:127
  28.2 0.0 collective-permute-done.4.other_ref
  28.2 0.0 copy-done.1
  28.2 2.2 %shard_map.76 = (f32[768,128]{1,0:T(8,128)S(1)}, bf16[768,128]{1,0:T(8,128)(2,1)S(1)}, bf16[512,128]{1,0:T(8,128)(2,1)S(1)}, bf16[256,2048]{1,0:T(8,128)(2,1)S(1)}) custom-call(s32[1,2,8]{2,1,0:T(2,128)S(1)} %bitcast.11, s32[1,1]{1,0:T(1,128)S(6)} %copy.21.count_ref, s32[3]{0:T(128)S(1)} %pad_add_fusion.where_ref, s32[144,144]{1,0:T(8,128)S(1)} %copy-done.1, ...), custom_call_target="tpu_custom_call" | custom-call | flops 2147483648 | bytes 1048576 | tf_op jit(solution)/shard_map/pallas_call | solution.py:181
  30.4 0.1 collective-permute-start.6
  30.5 2.0 %collective-permute-start.5 = (bf16[768,128]{1,0:T(8,128)(2,1)S(1)}, bf16[768,128]{1,0:T(8,128)(2,1)S(1)}, u32[]{:S(2)}, u32[]{:S(2)}) collective-permute-start(bf16[768,128]{1,0:T(8,128)(2,1)S(1)} %get-tuple-element.29), channel_id=1, source_target_pairs={{0,1},{1,0},{2,3},{3,2},{4,5},{5,4},{6,7},{7,6},{8,15},{9,10},{10,... | collective-permute-start | bytes 589832 | tf_op jit(solution)/shard_map/ppermute | solution.py:24
  32.5 3.1 %shard_map.77 = (f32[768,128]{1,0:T(8,128)S(1)}, bf16[768,128]{1,0:T(8,128)(2,1)S(1)}, bf16[512,128]{1,0:T(8,128)(2,1)S(1)}) custom-call(s32[1,2,8]{2,1,0:T(2,128)S(1)} %bitcast.12, s32[3]{0:T(128)S(1)} %pad_add_fusion.where_ref, bf16[2432,128]{1,0:T(8,128)(2,1)S(1)} %collective-permute-done.4.other_ref, bf16[256,2048]{1,0:T(8,128)(2,1)S(1)} %get-tuple-element.31.cw_ref, ...), custom_call_target="tpu_custom_call" | custom-call | flops 8589934592 | bytes 1048576 | tf_op jit(solution)/shard_map/pallas_call | solution.py:206
  35.6 0.3 collective-permute-start.10
  35.9 1.7 %collective-permute-start.9 = (bf16[768,128]{1,0:T(8,128)(2,1)S(1)}, bf16[768,128]{1,0:T(8,128)(2,1)S(1)}, u32[]{:S(2)}, u32[]{:S(2)}) collective-permute-start(bf16[768,128]{1,0:T(8,128)(2,1)S(1)} %get-tuple-element.33), channel_id=1, source_target_pairs={{0,1},{1,0},{2,3},{3,2},{4,5},{5,4},{6,7},{7,6},{8,15},{9,10},{10,... | collective-permute-start | bytes 589832 | tf_op jit(solution)/shard_map/ppermute | solution.py:24
  37.6 0.0 collective-permute-done.6
  37.6 0.1 collective-permute-done.5
  37.7 1.6 %collective-permute-start.7 = (bf16[256,128]{1,0:T(8,128)(2,1)S(1)}, bf16[256,128]{1,0:T(8,128)(2,1)S(1)}, u32[]{:S(2)}, u32[]{:S(2)}) collective-permute-start(bf16[256,128]{1,0:T(8,128)(2,1)S(1)} %get-tuple-element.41), channel_id=1, source_target_pairs={{0,3},{1,6},{2,5},{3,0},{4,7},{5,2},{6,1},{7,4},{8,13},{9,12},{10,... | collective-permute-start | bytes 196616 | tf_op jit(solution)/shard_map/ppermute | solution.py:24
  39.3 1.5 %collective-permute-start.8 = (bf16[256,128]{1,0:T(8,128)(2,1)S(1)}, bf16[256,128]{1,0:T(8,128)(2,1)S(1)}, u32[]{:S(2)}, u32[]{:S(2)}) collective-permute-start(bf16[256,128]{1,0:T(8,128)(2,1)S(1)} %get-tuple-element.42), channel_id=1, source_target_pairs={{0,5},{1,4},{2,7},{3,6},{4,1},{5,0},{6,3},{7,2},{8,11},{9,14},{10,... | collective-permute-start | bytes 196616 | tf_op jit(solution)/shard_map/ppermute | solution.py:24
  40.8 0.0 collective-permute-done.10
  40.8 2.2 %collective-permute-done.9 = bf16[768,128]{1,0:T(8,128)(2,1)S(1)} collective-permute-done((bf16[768,128]{1,0:T(8,128)(2,1)S(1)}, bf16[768,128]{1,0:T(8,128)(2,1)S(1)}, u32[]{:S(2)}, u32[]{:S(2)}) %collective-permute-start.9) | collective-permute-done | bytes 196640 | tf_op jit(solution)/shard_map/ppermute | solution.py:24
  43.0 2.2 %collective-permute-start.11 = (bf16[256,128]{1,0:T(8,128)(2,1)S(1)}, bf16[256,128]{1,0:T(8,128)(2,1)S(1)}, u32[]{:S(2)}, u32[]{:S(2)}) collective-permute-start(bf16[256,128]{1,0:T(8,128)(2,1)S(1)} %get-tuple-element.39), channel_id=1, source_target_pairs={{0,3},{1,6},{2,5},{3,0},{4,7},{5,2},{6,1},{7,4},{8,13},{9,12},{10,... | collective-permute-start | bytes 196616 | tf_op jit(solution)/shard_map/ppermute | solution.py:24
  45.2 1.8 %collective-permute-start.12 = (bf16[256,128]{1,0:T(8,128)(2,1)S(1)}, bf16[256,128]{1,0:T(8,128)(2,1)S(1)}, u32[]{:S(2)}, u32[]{:S(2)}) collective-permute-start(bf16[256,128]{1,0:T(8,128)(2,1)S(1)} %get-tuple-element.40), channel_id=1, source_target_pairs={{0,5},{1,4},{2,7},{3,6},{4,1},{5,0},{6,3},{7,2},{8,11},{9,14},{10,... | collective-permute-start | bytes 196616 | tf_op jit(solution)/shard_map/ppermute | solution.py:24
  47.0 0.0 collective-permute-done.7
  47.0 0.0 collective-permute-done.8
  47.0 3.3 %collective-permute-done.11 = bf16[256,128]{1,0:T(8,128)(2,1)S(1)} collective-permute-done((bf16[256,128]{1,0:T(8,128)(2,1)S(1)}, bf16[256,128]{1,0:T(8,128)(2,1)S(1)}, u32[]{:S(2)}, u32[]{:S(2)}) %collective-permute-start.11) | collective-permute-done | bytes 65568 | tf_op jit(solution)/shard_map/ppermute | solution.py:24
  50.3 0.9 %collective-permute-done.12 = bf16[256,128]{1,0:T(8,128)(2,1)S(1)} collective-permute-done((bf16[256,128]{1,0:T(8,128)(2,1)S(1)}, bf16[256,128]{1,0:T(8,128)(2,1)S(1)}, u32[]{:S(2)}, u32[]{:S(2)}) %collective-permute-start.12) | collective-permute-done | bytes 65568 | tf_op jit(solution)/shard_map/ppermute | solution.py:24
  51.2 0.1 broadcast_select_fusion.1
  51.3 18.5 %all_to_all.5.m_ref = f32[32,16,128]{2,1,0:T(8,128)S(1)} all-to-all(f32[32,16,128]{2,1,0:T(8,128)S(1)} %bitcast.18), channel_id=1, replica_groups=mesh['pairs'=32,'zh'=2,'zl'=4] {'pairs'}, dimensions={0} | all-to-all | bytes 524288 | tf_op jit(solution)/shard_map/all_to_all | solution.py:305
  69.8 1.6 %shard_map.78 = f32[16,128,128]{2,1,0:T(8,128)} custom-call(f32[32,16,128]{2,1,0:T(8,128)S(1)} %all_to_all.5.m_ref, f32[64,128]{1,0:T(8,128)S(1)} %get-tuple-element.35.lam_ref, f32[64,128]{1,0:T(8,128)S(1)} %get-tuple-element.36.sig_ref), custom_call_target="tpu_custom_call" | custom-call | flops 268435456 | bytes 2097152 | tf_op jit(solution)/shard_map/pallas_call | solution.py:264
  (15 shorter events, 0.3 us)
Async XLA Ops:
  0.0 0.9 %copy-start = (bf16[1152,64]{0,1:T(8,128)(2,1)S(1)}, bf16[1152,64]{0,1:T(8,128)(2,1)}, u32[]{:S(2)}) copy-start(bf16[1152,64]{0,1:T(8,128)(2,1)} %param.11) | copy-start | bytes 442372
  1.7 12.1 %collective-permute-start.1 = (bf16[304,128]{1,0:T(8,128)(2,1)S(1)}, bf16[304,128]{1,0:T(8,128)(2,1)S(1)}, u32[]{:S(2)}, u32[]{:S(2)}) collective-permute-start(bf16[304,128]{1,0:T(8,128)(2,1)S(1)} %pad_maximum_fusion.2), channel_id=1, source_target_pairs={{0,5},{1,4},{2,7},{3,6},{4,1},{5,0},{6,3},{7,2},{8,11},{9,14},{10,... | collective-permute-start | bytes 233480 | tf_op jit(solution)/shard_map/ppermute | solution.py:24
  6.9 7.9 %collective-permute-start = (bf16[304,128]{1,0:T(8,128)(2,1)S(1)}, bf16[304,128]{1,0:T(8,128)(2,1)S(1)}, u32[]{:S(2)}, u32[]{:S(2)}) collective-permute-start(bf16[304,128]{1,0:T(8,128)(2,1)S(1)} %pad_maximum_fusion.2), channel_id=1, source_target_pairs={{0,3},{1,6},{2,5},{3,0},{4,7},{5,2},{6,1},{7,4},{8,13},{9,12},{10,... | collective-permute-start | bytes 233480 | tf_op jit(solution)/shard_map/ppermute | solution.py:24
  9.9 3.9 %copy-start.4 = (bf16[8,128]{1,0:T(8,128)(2,1)S(1)}, bf16[8,128]{1,0:T(8,128)(2,1)}, u32[]{:S(2)}) copy-start(bf16[8,128]{1,0:T(8,128)(2,1)} %param.13) | copy-start | bytes 6148
  9.9 7.6 %copy-start.3 = (bf16[8,128]{1,0:T(8,128)(2,1)S(1)}, bf16[8,128]{1,0:T(8,128)(2,1)}, u32[]{:S(2)}) copy-start(bf16[8,128]{1,0:T(8,128)(2,1)} %param.12) | copy-start | bytes 6148
  14.8 8.8 %collective-permute-start.2 = (bf16[912,128]{1,0:T(8,128)(2,1)S(1)}, bf16[912,128]{1,0:T(8,128)(2,1)S(1)}, u32[]{:S(2)}, u32[]{:S(2)}) collective-permute-start(bf16[912,128]{1,0:T(8,128)(2,1)S(1)} %get-tuple-element.43), channel_id=1, source_target_pairs={{0,1},{1,0},{2,3},{3,2},{4,5},{5,4},{6,7},{7,6},{8,15},{9,10},{10,... | collective-permute-start | bytes 700424 | tf_op jit(solution)/shard_map/ppermute | solution.py:24
  17.5 8.6 %copy-start.2 = (s32[1,8,2]{1,2,0:T(2,128)S(1)}, s32[1,8,2]{1,2,0:T(2,128)}, u32[]{:S(2)}) copy-start(s32[1,8,2]{1,2,0:T(2,128)} %param.8) | copy-start | bytes 196
  17.5 6.1 %collective-permute-start.3 = (bf16[608,128]{1,0:T(8,128)(2,1)S(1)}, bf16[608,128]{1,0:T(8,128)(2,1)S(1)}, u32[]{:S(2)}, u32[]{:S(2)}) collective-permute-start(bf16[608,128]{1,0:T(8,128)(2,1)S(1)} %pad_maximum_fusion.1), channel_id=1, source_target_pairs={{0,7},{1,2},{2,1},{3,4},{4,3},{5,6},{6,5},{7,0},{8,9},{9,8},{10,11... | collective-permute-start | bytes 466952 | tf_op jit(solution)/shard_map/ppermute | solution.py:24
  23.7 4.4 %collective-permute-start.4 = (bf16[2432,128]{1,0:T(8,128)(2,1)S(1)}, bf16[2432,128]{1,0:T(8,128)(2,1)S(1)}, u32[]{:S(2)}, u32[]{:S(2)}) collective-permute-start(bf16[2432,128]{1,0:T(8,128)(2,1)S(1)} %slice_dynamic-update-slice_fusion.1.mine_ref), channel_id=1, source_target_pairs={{0,8},{8,0},{16,24},{24,16},{32,40},{40,32},{48,56},{56,48},{64,72... | collective-permute-start | bytes 1867784 | tf_op jit(solution)/shard_map/ppermute | solution.py:292
  26.1 2.1 %copy-start.1 = (s32[144,144]{1,0:T(8,128)S(1)}, s32[144,144]{1,0:T(8,128)}, u32[]{:S(2)}) copy-start(s32[144,144]{1,0:T(8,128)} %screen_ref.1) | copy-start | bytes 248836
  30.4 7.2 %collective-permute-start.6 = (bf16[512,128]{1,0:T(8,128)(2,1)S(1)}, bf16[512,128]{1,0:T(8,128)(2,1)S(1)}, u32[]{:S(2)}, u32[]{:S(2)}) collective-permute-start(bf16[512,128]{1,0:T(8,128)(2,1)S(1)} %get-tuple-element.30), channel_id=1, source_target_pairs={{0,7},{1,2},{2,1},{3,4},{4,3},{5,6},{6,5},{7,0},{8,9},{9,8},{10,11... | collective-permute-start | bytes 393224 | tf_op jit(solution)/shard_map/ppermute | solution.py:24
  30.5 7.2 %collective-permute-start.5 = (bf16[768,128]{1,0:T(8,128)(2,1)S(1)}, bf16[768,128]{1,0:T(8,128)(2,1)S(1)}, u32[]{:S(2)}, u32[]{:S(2)}) collective-permute-start(bf16[768,128]{1,0:T(8,128)(2,1)S(1)} %get-tuple-element.29), channel_id=1, source_target_pairs={{0,1},{1,0},{2,3},{3,2},{4,5},{5,4},{6,7},{7,6},{8,15},{9,10},{10,... | collective-permute-start | bytes 589832 | tf_op jit(solution)/shard_map/ppermute | solution.py:24
  35.6 5.3 %collective-permute-start.10 = (bf16[512,128]{1,0:T(8,128)(2,1)S(1)}, bf16[512,128]{1,0:T(8,128)(2,1)S(1)}, u32[]{:S(2)}, u32[]{:S(2)}) collective-permute-start(bf16[512,128]{1,0:T(8,128)(2,1)S(1)} %get-tuple-element.34), channel_id=1, source_target_pairs={{0,7},{1,2},{2,1},{3,4},{4,3},{5,6},{6,5},{7,0},{8,9},{9,8},{10,11... | collective-permute-start | bytes 393224 | tf_op jit(solution)/shard_map/ppermute | solution.py:24
  35.9 7.1 %collective-permute-start.9 = (bf16[768,128]{1,0:T(8,128)(2,1)S(1)}, bf16[768,128]{1,0:T(8,128)(2,1)S(1)}, u32[]{:S(2)}, u32[]{:S(2)}) collective-permute-start(bf16[768,128]{1,0:T(8,128)(2,1)S(1)} %get-tuple-element.33), channel_id=1, source_target_pairs={{0,1},{1,0},{2,3},{3,2},{4,5},{5,4},{6,7},{7,6},{8,15},{9,10},{10,... | collective-permute-start | bytes 589832 | tf_op jit(solution)/shard_map/ppermute | solution.py:24
  37.7 9.3 %collective-permute-start.7 = (bf16[256,128]{1,0:T(8,128)(2,1)S(1)}, bf16[256,128]{1,0:T(8,128)(2,1)S(1)}, u32[]{:S(2)}, u32[]{:S(2)}) collective-permute-start(bf16[256,128]{1,0:T(8,128)(2,1)S(1)} %get-tuple-element.41), channel_id=1, source_target_pairs={{0,3},{1,6},{2,5},{3,0},{4,7},{5,2},{6,1},{7,4},{8,13},{9,12},{10,... | collective-permute-start | bytes 196616 | tf_op jit(solution)/shard_map/ppermute | solution.py:24
  39.3 7.7 %collective-permute-start.8 = (bf16[256,128]{1,0:T(8,128)(2,1)S(1)}, bf16[256,128]{1,0:T(8,128)(2,1)S(1)}, u32[]{:S(2)}, u32[]{:S(2)}) collective-permute-start(bf16[256,128]{1,0:T(8,128)(2,1)S(1)} %get-tuple-element.42), channel_id=1, source_target_pairs={{0,5},{1,4},{2,7},{3,6},{4,1},{5,0},{6,3},{7,2},{8,11},{9,14},{10,... | collective-permute-start | bytes 196616 | tf_op jit(solution)/shard_map/ppermute | solution.py:24
  43.0 7.3 %collective-permute-start.11 = (bf16[256,128]{1,0:T(8,128)(2,1)S(1)}, bf16[256,128]{1,0:T(8,128)(2,1)S(1)}, u32[]{:S(2)}, u32[]{:S(2)}) collective-permute-start(bf16[256,128]{1,0:T(8,128)(2,1)S(1)} %get-tuple-element.39), channel_id=1, source_target_pairs={{0,3},{1,6},{2,5},{3,0},{4,7},{5,2},{6,1},{7,4},{8,13},{9,12},{10,... | collective-permute-start | bytes 196616 | tf_op jit(solution)/shard_map/ppermute | solution.py:24
  45.2 6.0 %collective-permute-start.12 = (bf16[256,128]{1,0:T(8,128)(2,1)S(1)}, bf16[256,128]{1,0:T(8,128)(2,1)S(1)}, u32[]{:S(2)}, u32[]{:S(2)}) collective-permute-start(bf16[256,128]{1,0:T(8,128)(2,1)S(1)} %get-tuple-element.40), channel_id=1, source_target_pairs={{0,5},{1,4},{2,7},{3,6},{4,1},{5,0},{6,3},{7,2},{8,11},{9,14},{10,... | collective-permute-start | bytes 196616 | tf_op jit(solution)/shard_map/ppermute | solution.py:24
